TPU v7x, 32 devices: a whole 2x2x4 slice. The times are simulated.
32 devices in a mesh: gx: 8 (over y, x, core), gy: 4 (over z).
Axes of the slice: x: 2, y: 2, z: 4, core: 2. Of those that a mesh axis runs over, the one named last changes fastest.
Arguments:
- marker_comp: float32 [16384, 128], P(('gx', 'gy')), may hold values from 0 to 1
- marker_strain: float32 [16384, 128], P(('gx', 'gy')), may hold values from 0.01 to 10
- marker_live: int32 [16384, 128], P(('gx', 'gy')), may hold values 0 or 1
- marker_cell: int32 [16384, 128], P(('gx', 'gy')), may hold values from 0 to 65535, as said below
- block_dest: int32 [16384, 1], P(('gx', 'gy')), may hold values from 0 to 31; in each aligned block of 512 rows (0 to 511, 512 to 1023, ...) at most 32 rows name the same one
- old_logvisc: float32 [128, 128, 128], P('gx', 'gy'), may hold values from -1 to 1
- velocity: float32 [3, 128, 128, 128], P(None, 'gx', 'gy'), may hold values from -6 to 6
Outputs:
- logvisc: float32 [128, 128, 128], P('gx', 'gy')
- density: float32 [128, 128, 128], P('gx', 'gy')
- smoothed: float32 [3, 128, 128, 128], P(None, 'gx', 'gy')
Inputs may be any that keep to these rules, and one draw needn't show every extreme that they name: `block_dest`: in the rows of one device no owner is named by more than 32 rows. All markers of one block lie in one column of cells: their marker_cell // 128 are equal.
All inputs are finite; a program needn't handle non-finite values. No bound on the sum of `marker_live` on one device may be relied on, other than what follows from the above.
Results may differ from a plain program's by a relative error of at most 0.0003.
Values sent between devices are 32-bit elements; how exact they have to be, the bound alone decides.
No kernel may reach another device: no remote copies, remote signals or barrier semaphores. Data moves between devices by JAX's collectives and lax.ppermute only.
A program may use at most 64 MiB of HBM per device.

v0:
```python
import math

import jax
import jax.numpy as jnp
from jax import lax
from jax.sharding import PartitionSpec as P

SWEEPS = 2


LOG_HIGH = 1.5
LOG_LOW = -1.0
WEAKENING = 1.0
DENSITY_JUMP = 0.4
SOFTENING = 0.1
GRAVITY = 10.0
RELAX = 0.8
EXACT = lax.Precision.HIGHEST


def with_halo(cells, sides, width):
    for axis, dim in sides:
        count = lax.axis_size(axis)
        ends = count - 1
        head = lax.slice_in_dim(cells, 0, width, axis=dim)
        tail = lax.slice_in_dim(cells, cells.shape[dim] - width, cells.shape[dim], axis=dim)
        cells = jnp.concatenate(
            [
                lax.ppermute(tail, axis, [(i, (i + 1) % count) for i in range(ends)]),
                cells,
                lax.ppermute(head, axis, [((i + 1) % count, i) for i in range(ends)]),
            ],
            axis=dim,
        )
    return cells


def marker_terms(marker_comp, marker_strain, marker_live):
    soften = marker_strain / (1.0 + marker_strain)
    marker_logv = LOG_HIGH * marker_comp + LOG_LOW * (1.0 - marker_comp) - WEAKENING * soften
    marker_rho = 1.0 + DENSITY_JUMP * marker_comp - SOFTENING * soften
    weight = marker_live.astype(jnp.float32)
    return (marker_logv, marker_rho, weight)


def smooth(viscosity, force_z, velocity, widen_visc, widen_vel):
    padded_visc = widen_visc(viscosity)
    coeffs = [
        0.5 * (viscosity + padded_visc[2:, 1:-1, 1:-1]),
        0.5 * (viscosity + padded_visc[:-2, 1:-1, 1:-1]),
        0.5 * (viscosity + padded_visc[1:-1, 2:, 1:-1]),
        0.5 * (viscosity + padded_visc[1:-1, :-2, 1:-1]),
        0.5 * (viscosity + padded_visc[1:-1, 1:-1, 2:]),
        0.5 * (viscosity + padded_visc[1:-1, 1:-1, :-2]),
    ]
    diag = coeffs[0] + coeffs[1] + coeffs[2] + coeffs[3] + coeffs[4] + coeffs[5]
    zeros_field = jnp.zeros_like(force_z)
    force = jnp.stack([zeros_field, zeros_field, force_z])
    for sweep in range(SWEEPS):
        padded_vel = widen_vel(velocity)
        beside_all = (
            coeffs[0] * padded_vel[:, 2:, 1:-1, 1:-1] + coeffs[1] * padded_vel[:, :-2, 1:-1, 1:-1]
        )
        beside_all = (
            beside_all
            + coeffs[2] * padded_vel[:, 1:-1, 2:, 1:-1]
            + coeffs[3] * padded_vel[:, 1:-1, :-2, 1:-1]
        )
        beside_all = (
            beside_all
            + coeffs[4] * padded_vel[:, 1:-1, 1:-1, 2:]
            + coeffs[5] * padded_vel[:, 1:-1, 1:-1, :-2]
        )
        operator = diag * velocity - beside_all
        velocity = velocity + RELAX * (force - operator) / diag
    return velocity


def slab_visc(field):
    wider = with_halo(field, ((("gx", "gy"), 0),), 1)
    return jnp.pad(wider, ((0, 0), (1, 1), (1, 1)))


def slab_vel(field):
    wider = with_halo(field, ((("gx", "gy"), 1),), 1)
    return jnp.pad(wider, ((0, 0), (0, 0), (1, 1), (1, 1)))


def per_device(
    marker_comp, marker_strain, marker_live, marker_cell, block_dest, old_logvisc, velocity
):
    marker_logv, marker_rho, weight = marker_terms(marker_comp, marker_strain, marker_live)
    payload = jnp.stack(
        [weight * marker_logv, weight * marker_rho, weight, marker_cell.astype(jnp.float32)], axis=0
    )
    count_x = lax.axis_size("gx")
    count_y = lax.axis_size("gy")
    devices_all = count_x * count_y
    blocks = payload.shape[1]
    block_width = payload.shape[2]
    slots = 2 * blocks // devices_all
    total_slots = devices_all * slots
    target = block_dest[:, 0]
    owner_hot = (target[:, None] == jnp.arange(devices_all, dtype=jnp.int32)[None, :]).astype(
        jnp.float32
    )
    block_ids = jnp.arange(blocks, dtype=jnp.int32)
    lower = (block_ids[:, None] > block_ids[None, :]).astype(jnp.float32)
    before = jnp.dot(lower, owner_hot, precision=EXACT, preferred_element_type=jnp.float32)
    rank = jnp.sum(before * owner_hot, axis=1).astype(jnp.int32)
    place = target * slots + rank
    select = (place[:, None] == jnp.arange(total_slots, dtype=jnp.int32)[None, :]).astype(
        jnp.float32
    )
    outgoing = jnp.einsum(
        "bs,vbm->vsm", select, payload, precision=EXACT, preferred_element_type=jnp.float32
    )
    incoming = lax.all_to_all(outgoing, ("gx", "gy"), split_axis=1, concat_axis=1, tiled=True)
    brick_shape = old_logvisc.shape
    depth_cells = brick_shape[2]
    column_count = brick_shape[0] * brick_shape[1]
    cells = incoming[3].astype(jnp.int32)
    column_of = cells[:, 0] // depth_cells
    depth = cells % depth_cells
    group = math.gcd(total_slots, 128)
    group_count = total_slots // group
    values = incoming[:3].reshape(3, group_count, group, block_width).transpose(1, 0, 2, 3)
    depth_groups = depth.reshape(group_count, group, block_width)
    depth_ids = jnp.arange(depth_cells, dtype=jnp.int32)

    def column_sums(pieces):
        piece_values, piece_depth = pieces
        depth_hot = (piece_depth[:, :, None] == depth_ids[None, None, :]).astype(jnp.float32)
        return jnp.einsum(
            "vgm,gmz->vgz",
            piece_values,
            depth_hot,
            precision=EXACT,
            preferred_element_type=jnp.float32,
        )

    columns = lax.map(column_sums, (values, depth_groups))
    columns = columns.transpose(1, 0, 2, 3).reshape(3, total_slots, depth_cells)
    column_hot = (column_of[:, None] == jnp.arange(column_count, dtype=jnp.int32)[None, :]).astype(
        jnp.float32
    )
    totals = jnp.einsum(
        "sr,vsz->vrz", column_hot, columns, precision=EXACT, preferred_element_type=jnp.float32
    ).reshape(3, -1)
    denominator = totals[2] + 1.0
    logvisc = ((totals[0] + old_logvisc.reshape(-1)) / denominator).reshape(brick_shape)
    density = ((totals[1] + 1.0) / denominator).reshape(brick_shape)
    viscosity = jnp.exp(logvisc)
    force_z = GRAVITY * (1.0 - density)
    fields = jnp.concatenate([jnp.stack([viscosity, force_z]), velocity], axis=0)
    slabs = lax.all_to_all(fields, "gy", split_axis=1, concat_axis=2, tiled=True)
    slab_result = smooth(slabs[0], slabs[1], slabs[2:], slab_visc, slab_vel)
    smoothed = lax.all_to_all(slab_result, "gy", split_axis=2, concat_axis=1, tiled=True)
    return (logvisc, density, smoothed)


def solution(mesh):
    return jax.shard_map(
        per_device,
        mesh=mesh,
        in_specs=(
            P(("gx", "gy"), None),
            P(("gx", "gy"), None),
            P(("gx", "gy"), None),
            P(("gx", "gy"), None),
            P(("gx", "gy"), None),
            P("gx", "gy", None),
            P(None, "gx", "gy", None),
        ),
        out_specs=(P("gx", "gy", None), P("gx", "gy", None), P(None, "gx", "gy", None)),
        check_vma=False,
    )
```

profile of v0, /device:TPU:0, one launch (start us, length us, event | category | flops | bytes accessed | tf_op | source)
XLA Modules:
  0.0 223.1 jit_solution(10913902459270637245)
XLA Ops:
  0.6 1.0 fusion.27
  1.7 0.7 multiply_add_fusion
  2.4 1.1 copy.86
  3.4 1.1 copy.87
  4.5 1.1 copy.90
  5.6 1.1 copy.92
  6.8 0.1 multiply_bitcast_fusion.1
  6.9 2.1 fusion.18
  9.0 1.8 copy.93
  10.8 7.3 %all-to-all-start = ((f32[4,1024,128]{2,0,1:T(4,128)}), f32[4,1024,128]{2,0,1:T(4,128)S(1)}, u32[]{:S(2)}, u32[]{:S(2)}) async-start(f32[4,1024,128]{2,0,1:T(4,128)} %copy.93), calls=%async_computation | async-start | bytes 4194304 | tf_op jit(solution)/shard_map/all_to_all | solution.py:118
  18.1 47.5 %all-to-all-done = f32[4,1024,128]{2,0,1:T(4,128)S(1)} async-done(((f32[4,1024,128]{2,0,1:T(4,128)}), f32[4,1024,128]{2,0,1:T(4,128)S(1)}, u32[]{:S(2)}, u32[]{:S(2)}) %all-to-all-start) | async-done | bytes 2097184 | tf_op jit(solution)/shard_map/all_to_all | solution.py:118
  65.7 0.6 slice_convert_fusion
  66.2 0.4 fusion.64
  66.6 0.2 add_select_fusion.1
  66.8 51.6 %while.11 = (s32[]{:T(128)}, f32[8,3,128,128]{3,1,2,0:T(4,128)}, s32[8,128,128]{2,1,0:T(8,128)S(1)}, f32[8,3,128,128]{3,1,2,0:T(4,128)S(1)}, s32[]{:T(128)}) while((s32[]{:T(128)}, f32[8,3,128,128]{3,1,2,0:T(4,128)}, s32[8,128,128]{2,1,0:T(8,128)S(1)}, f32[8,3,128,128]{3,1,2,0:T(4,128)S(1)}, s32[]{:T(128)}) %tuple.45), condition=%wide.region_2.3_spmd.clone, body=%wide.region_1.2_spmd.clone.sunk | while | flops 77594624 | bytes 721993 | solution.py:142
  66.9 6.5 %fusion.90 = f32[8,3,128,128]{3,1,2,0:T(4,128)} fusion(f32[8,3,128,128]{3,1,2,0:T(4,128)} %get-tuple-element.106, s32[]{:T(128)S(6)} %copy.118, s32[128,128]{1,0:T(8,128)S(1)} %dynamic-slice_bitcast_fusion.2, f32[8,3,128,128]{3,1,2,0:T(4,128)S(1)} %get-tuple-element.113), kind=kOutput, calls=%fused_computation.5.clone.1 | convolution fusion | flops 77594624 | bytes 590848 | tf_op jit(solution)/shard_map/while/body/eval_jaxpr/vgm,gmz->vgz/dot_general | solution.py:134
  73.3 6.4 %fusion.90 = f32[8,3,128,128]{3,1,2,0:T(4,128)} fusion(f32[8,3,128,128]{3,1,2,0:T(4,128)} %get-tuple-element.106, s32[]{:T(128)S(6)} %copy.118, s32[128,128]{1,0:T(8,128)S(1)} %dynamic-slice_bitcast_fusion.2, f32[8,3,128,128]{3,1,2,0:T(4,128)S(1)} %get-tuple-element.113), kind=kOutput, calls=%fused_computation.5.clone.1 | convolution fusion | flops 77594624 | bytes 590848 | tf_op jit(solution)/shard_map/while/body/eval_jaxpr/vgm,gmz->vgz/dot_general | solution.py:134
  79.8 6.4 %fusion.90 = f32[8,3,128,128]{3,1,2,0:T(4,128)} fusion(f32[8,3,128,128]{3,1,2,0:T(4,128)} %get-tuple-element.106, s32[]{:T(128)S(6)} %copy.118, s32[128,128]{1,0:T(8,128)S(1)} %dynamic-slice_bitcast_fusion.2, f32[8,3,128,128]{3,1,2,0:T(4,128)S(1)} %get-tuple-element.113), kind=kOutput, calls=%fused_computation.5.clone.1 | convolution fusion | flops 77594624 | bytes 590848 | tf_op jit(solution)/shard_map/while/body/eval_jaxpr/vgm,gmz->vgz/dot_general | solution.py:134
  86.2 6.4 %fusion.90 = f32[8,3,128,128]{3,1,2,0:T(4,128)} fusion(f32[8,3,128,128]{3,1,2,0:T(4,128)} %get-tuple-element.106, s32[]{:T(128)S(6)} %copy.118, s32[128,128]{1,0:T(8,128)S(1)} %dynamic-slice_bitcast_fusion.2, f32[8,3,128,128]{3,1,2,0:T(4,128)S(1)} %get-tuple-element.113), kind=kOutput, calls=%fused_computation.5.clone.1 | convolution fusion | flops 77594624 | bytes 590848 | tf_op jit(solution)/shard_map/while/body/eval_jaxpr/vgm,gmz->vgz/dot_general | solution.py:134
  92.7 6.4 %fusion.90 = f32[8,3,128,128]{3,1,2,0:T(4,128)} fusion(f32[8,3,128,128]{3,1,2,0:T(4,128)} %get-tuple-element.106, s32[]{:T(128)S(6)} %copy.118, s32[128,128]{1,0:T(8,128)S(1)} %dynamic-slice_bitcast_fusion.2, f32[8,3,128,128]{3,1,2,0:T(4,128)S(1)} %get-tuple-element.113), kind=kOutput, calls=%fused_computation.5.clone.1 | convolution fusion | flops 77594624 | bytes 590848 | tf_op jit(solution)/shard_map/while/body/eval_jaxpr/vgm,gmz->vgz/dot_general | solution.py:134
  99.1 6.4 %fusion.90 = f32[8,3,128,128]{3,1,2,0:T(4,128)} fusion(f32[8,3,128,128]{3,1,2,0:T(4,128)} %get-tuple-element.106, s32[]{:T(128)S(6)} %copy.118, s32[128,128]{1,0:T(8,128)S(1)} %dynamic-slice_bitcast_fusion.2, f32[8,3,128,128]{3,1,2,0:T(4,128)S(1)} %get-tuple-element.113), kind=kOutput, calls=%fused_computation.5.clone.1 | convolution fusion | flops 77594624 | bytes 590848 | tf_op jit(solution)/shard_map/while/body/eval_jaxpr/vgm,gmz->vgz/dot_general | solution.py:134
  105.6 6.4 %fusion.90 = f32[8,3,128,128]{3,1,2,0:T(4,128)} fusion(f32[8,3,128,128]{3,1,2,0:T(4,128)} %get-tuple-element.106, s32[]{:T(128)S(6)} %copy.118, s32[128,128]{1,0:T(8,128)S(1)} %dynamic-slice_bitcast_fusion.2, f32[8,3,128,128]{3,1,2,0:T(4,128)S(1)} %get-tuple-element.113), kind=kOutput, calls=%fused_computation.5.clone.1 | convolution fusion | flops 77594624 | bytes 590848 | tf_op jit(solution)/shard_map/while/body/eval_jaxpr/vgm,gmz->vgz/dot_general | solution.py:134
  112.0 6.4 %fusion.90 = f32[8,3,128,128]{3,1,2,0:T(4,128)} fusion(f32[8,3,128,128]{3,1,2,0:T(4,128)} %get-tuple-element.106, s32[]{:T(128)S(6)} %copy.118, s32[128,128]{1,0:T(8,128)S(1)} %dynamic-slice_bitcast_fusion.2, f32[8,3,128,128]{3,1,2,0:T(4,128)S(1)} %get-tuple-element.113), kind=kOutput, calls=%fused_computation.5.clone.1 | convolution fusion | flops 77594624 | bytes 590848 | tf_op jit(solution)/shard_map/while/body/eval_jaxpr/vgm,gmz->vgz/dot_general | solution.py:134
  118.5 3.4 %fusion.22 = f32[3,512,128]{1,2,0:T(8,128)S(1)} fusion(f32[3,1024,128]{2,0,1:T(4,128)} %bitcast.97, s32[1024]{0:T(1024)S(1)} %fusion.64), kind=kOutput, calls=%fused_computation.30 | convolution fusion | flops 2416443392 | bytes 2363392 | tf_op jit(solution)/shard_map/sr,vsz->vrz/dot_general | solution.py:147
  121.9 0.0 copy-start.1
  121.9 0.0 copy-start
  121.9 0.1 subtract_multiply_fusion
  122.0 0.1 copy.98
  122.1 0.1 copy.97
  122.3 0.1 copy.96
  122.4 0.1 copy.95
  122.5 0.3 copy-done.1
  122.8 0.9 exponential_bitcast_fusion
  123.7 0.0 copy-done
  123.7 0.1 pad_maximum_fusion
  123.8 35.2 %all_to_all.38 = f32[5,16,32,128]{3,2,0,1:T(8,128)S(1)} all-to-all(f32[5,16,32,128]{3,2,0,1:T(8,128)S(1)} %pad_maximum_fusion), channel_id=1, replica_groups=mesh['gx'=8,'gy'=4] {'gy'}, dimensions={1} | all-to-all | bytes 2621440 | tf_op jit(solution)/shard_map/all_to_all | solution.py:156
  159.0 0.1 copy.102
  159.2 0.1 slice.172
  159.3 1.3 collective-permute-start
  160.6 4.5 %collective-permute-start.1 = (f32[1,128,128]{2,1,0:T(8,128)S(1)}, f32[1,128,128]{2,1,0:T(8,128)S(1)}, u32[]{:S(2)}, u32[]{:S(2)}) collective-permute-start(f32[1,128,128]{2,1,0:T(8,128)S(1)} %bitcast.92), channel_id=1, source_target_pairs={{0,1},{1,2},{2,3},{3,4},{4,5},{5,6},{6,7},{7,8},{8,9},{9,10},{10,1... | collective-permute-start | bytes 196616 | tf_op jit(solution)/shard_map/ppermute | solution.py:29
  165.2 0.1 copy.103
  165.3 2.1 collective-permute-start.3
  167.4 1.3 collective-permute-start.2
  168.7 0.0 collective-permute-done
  168.8 0.0 collective-permute-done.1
  168.8 0.3 select_maximum_fusion.4
  169.1 0.3 add_add_fusion
  169.4 2.0 collective-permute-done.3
  171.4 8.3 %collective-permute-done.2 = f32[3,1,128,128]{3,2,1,0:T(8,128)S(1)} collective-permute-done((f32[3,1,128,128]{3,2,1,0:T(8,128)S(1)}, f32[3,1,128,128]{3,2,1,0:T(8,128)S(1)}, u32[]{:S(2)}, u32[]{:S(2)}) %collective-permute-start.2) | collective-permute-done | bytes 196640 | tf_op jit(solution)/shard_map/ppermute | solution.py:31
  179.7 0.7 select_maximum_fusion.2
  180.4 0.8 fusion.42
  181.3 3.0 %collective-permute-start.5 = (f32[3,1,128,128]{3,2,1,0:T(8,128)S(1)}, f32[3,1,128,128]{3,2,1,0:T(8,128)S(1)}, u32[]{:S(2)}, u32[]{:S(2)}) collective-permute-start(f32[3,1,128,128]{3,2,1,0:T(8,128)S(1)} %get-tuple-element.62), channel_id=1, source_target_pairs={{0,1},{1,2},{2,3},{3,4},{4,5},{5,6},{6,7},{7,8},{8,9},{9,10},{10,1... | collective-permute-start | bytes 589832 | tf_op jit(solution)/shard_map/ppermute | solution.py:29
  184.3 1.3 collective-permute-start.4
  185.6 3.1 %collective-permute-done.5 = f32[3,1,128,128]{3,2,1,0:T(8,128)S(1)} collective-permute-done((f32[3,1,128,128]{3,2,1,0:T(8,128)S(1)}, f32[3,1,128,128]{3,2,1,0:T(8,128)S(1)}, u32[]{:S(2)}, u32[]{:S(2)}) %collective-permute-start.5) | collective-permute-done | bytes 196640 | tf_op jit(solution)/shard_map/ppermute | solution.py:29
  188.7 7.4 %collective-permute-done.4 = f32[3,1,128,128]{3,2,1,0:T(8,128)S(1)} collective-permute-done((f32[3,1,128,128]{3,2,1,0:T(8,128)S(1)}, f32[3,1,128,128]{3,2,1,0:T(8,128)S(1)}, u32[]{:S(2)}, u32[]{:S(2)}) %collective-permute-start.4) | collective-permute-done | bytes 196640 | tf_op jit(solution)/shard_map/ppermute | solution.py:31
  196.1 0.7 select_maximum_fusion
  196.8 0.8 fusion.45
  197.7 0.5 copy.106
  198.2 23.8 %all_to_all.39 = f32[3,4,128,128]{3,1,0,2:T(4,128)S(1)} all-to-all(f32[3,4,128,128]{3,1,0,2:T(4,128)S(1)} %copy.106), channel_id=1, replica_groups=mesh['gx'=8,'gy'=4] {'gy'}, dimensions={2} | all-to-all | bytes 1572864 | tf_op jit(solution)/shard_map/all_to_all | solution.py:158
  222.0 0.1 copy.107
  222.1 0.9 copy.108
  (17 shorter events, 0.2 us)
Async XLA Ops:
  10.8 54.8 %all-to-all-start = ((f32[4,1024,128]{2,0,1:T(4,128)}), f32[4,1024,128]{2,0,1:T(4,128)S(1)}, u32[]{:S(2)}, u32[]{:S(2)}) async-start(f32[4,1024,128]{2,0,1:T(4,128)} %copy.93), calls=%async_computation | async-start | bytes 4194304 | tf_op jit(solution)/shard_map/all_to_all | solution.py:118
  121.9 1.0 copy-start.1
  121.9 1.9 copy-start
  159.3 9.5 %collective-permute-start = (f32[1,128,128]{2,1,0:T(8,128)S(1)}, f32[1,128,128]{2,1,0:T(8,128)S(1)}, u32[]{:S(2)}, u32[]{:S(2)}) collective-permute-start(f32[1,128,128]{2,1,0:T(8,128)S(1)} %bitcast.93), channel_id=1, source_target_pairs={{1,0},{2,1},{3,2},{4,3},{5,4},{6,5},{7,6},{8,7},{9,8},{10,9},{11,1... | collective-permute-start | bytes 196616 | tf_op jit(solution)/shard_map/ppermute | solution.py:31
  160.6 8.2 %collective-permute-start.1 = (f32[1,128,128]{2,1,0:T(8,128)S(1)}, f32[1,128,128]{2,1,0:T(8,128)S(1)}, u32[]{:S(2)}, u32[]{:S(2)}) collective-permute-start(f32[1,128,128]{2,1,0:T(8,128)S(1)} %bitcast.92), channel_id=1, source_target_pairs={{0,1},{1,2},{2,3},{3,4},{4,5},{5,6},{6,7},{7,8},{8,9},{9,10},{10,1... | collective-permute-start | bytes 196616 | tf_op jit(solution)/shard_map/ppermute | solution.py:29
  165.3 6.1 %collective-permute-start.3 = (f32[3,1,128,128]{3,2,1,0:T(8,128)S(1)}, f32[3,1,128,128]{3,2,1,0:T(8,128)S(1)}, u32[]{:S(2)}, u32[]{:S(2)}) collective-permute-start(f32[3,1,128,128]{3,2,1,0:T(8,128)S(1)} %get-tuple-element.64), channel_id=1, source_target_pairs={{0,1},{1,2},{2,3},{3,4},{4,5},{5,6},{6,7},{7,8},{8,9},{9,10},{10,1... | collective-permute-start | bytes 589832 | tf_op jit(solution)/shard_map/ppermute | solution.py:29
  167.4 12.3 %collective-permute-start.2 = (f32[3,1,128,128]{3,2,1,0:T(8,128)S(1)}, f32[3,1,128,128]{3,2,1,0:T(8,128)S(1)}, u32[]{:S(2)}, u32[]{:S(2)}) collective-permute-start(f32[3,1,128,128]{3,2,1,0:T(8,128)S(1)} %get-tuple-element.65), channel_id=1, source_target_pairs={{1,0},{2,1},{3,2},{4,3},{5,4},{6,5},{7,6},{8,7},{9,8},{10,9},{11,1... | collective-permute-start | bytes 589832 | tf_op jit(solution)/shard_map/ppermute | solution.py:31
  181.3 7.3 %collective-permute-start.5 = (f32[3,1,128,128]{3,2,1,0:T(8,128)S(1)}, f32[3,1,128,128]{3,2,1,0:T(8,128)S(1)}, u32[]{:S(2)}, u32[]{:S(2)}) collective-permute-start(f32[3,1,128,128]{3,2,1,0:T(8,128)S(1)} %get-tuple-element.62), channel_id=1, source_target_pairs={{0,1},{1,2},{2,3},{3,4},{4,5},{5,6},{6,7},{7,8},{8,9},{9,10},{10,1... | collective-permute-start | bytes 589832 | tf_op jit(solution)/shard_map/ppermute | solution.py:29
  184.3 11.8 %collective-permute-start.4 = (f32[3,1,128,128]{3,2,1,0:T(8,128)S(1)}, f32[3,1,128,128]{3,2,1,0:T(8,128)S(1)}, u32[]{:S(2)}, u32[]{:S(2)}) collective-permute-start(f32[3,1,128,128]{3,2,1,0:T(8,128)S(1)} %get-tuple-element.63), channel_id=1, source_target_pairs={{1,0},{2,1},{3,2},{4,3},{5,4},{6,5},{7,6},{8,7},{9,8},{10,9},{11,1... | collective-permute-start | bytes 589832 | tf_op jit(solution)/shard_map/ppermute | solution.py:31
where the time goes:
time: 224 us; the launch traced here: 223 us
  waiting for transfers between devices  68.4 us (31%)
  blocking collectives  59 us (26%)
  matrix products  58.1 us (26%)
  starting transfers between devices  20.8 us (9%)
  local copies, waits for them, and re-layouts  8.87 us (4%)
  other arithmetic  6.88 us (3%)
    dot_general x8, matrix products, column_sums(): jnp.einsum('vgm,gmz->vgz', piece_values, depth_hot, precision=EXACT, pref...  51.6 us
    all_to_all x1, waiting for transfers between devices, per_device(): lax.all_to_all(outgoing, ('gx', 'gy'), split_axis=1, concat_axis=1, tiled...  47.5 us
    all_to_all x1, blocking collectives, per_device(): lax.all_to_all(fields, 'gy', split_axis=1, concat_axis=2, tiled=True)  35.2 us
    all_to_all x1, blocking collectives, per_device(): lax.all_to_all(slab_result, 'gy', split_axis=2, concat_axis=1, tiled=True)  23.8 us
    ppermute x3, waiting for transfers between devices, with_halo(): lax.ppermute(head, axis, [((i + 1) % count, i) for i in range(ends)])  15.8 us
    ppermute x3, starting transfers between devices, with_halo(): lax.ppermute(tail, axis, [(i, (i + 1) % count) for i in range(ends)])  9.65 us
    all_to_all x1, starting transfers between devices, per_device(): lax.all_to_all(outgoing, ('gx', 'gy'), split_axis=1, concat_axis=1, tiled...  7.3 us
    ppermute x3, waiting for transfers between devices, with_halo(): lax.ppermute(tail, axis, [(i, (i + 1) % count) for i in range(ends)])  5.07 us
  transfers between devices with their start and end apart: 7, of which 5 were waited for; matrix products, arithmetic and copies ran while one was open for 0% of the time, Pallas kernels for 0%

commit v1 on v0

v1 whole, which is shorter than its diff:
```python
import functools

import jax
import jax.numpy as jnp
from jax import lax
from jax.experimental import pallas as pl
from jax.experimental.pallas import tpu as pltpu
from jax.sharding import PartitionSpec as P

LOG_HIGH = 1.5
LOG_LOW = -1.0
WEAKENING = 1.0
DENSITY_JUMP = 0.4
SOFTENING = 0.1
GRAVITY = 10.0
RELAX = 0.8
BOTH = ("gx", "gy")
F32 = jnp.float32
BF16 = jnp.bfloat16
VMEM = pl.BlockSpec(memory_space=pltpu.VMEM)
SMEM = pl.BlockSpec(memory_space=pltpu.SMEM)
NEAR = 8
FAR = 32
LINE = 48


def split(values):
    high = values.astype(BF16).astype(F32)
    return high, values - high


def pack_kernel(
    slots, chunk, dest_ref, comp_ref, strain_ref, live_ref, cell_ref, out_ref, used_ref
):
    devices = used_ref.shape[0]
    blocks, marks = comp_ref.shape
    shift = marks.bit_length() - 1
    out_ref[...] = jnp.zeros_like(out_ref)
    for owner in range(devices):
        used_ref[owner] = 0
        out_ref[pl.ds(owner * chunk + 3 * slots, 1), :] = jnp.full((1, marks), -1.0, F32)
    depth_ids = lax.broadcasted_iota(jnp.int32, (marks, marks), 0).astype(F32).astype(BF16)
    row_ids = lax.broadcasted_iota(jnp.int32, (48, marks), 0) & 7
    lane_ids = lax.broadcasted_iota(jnp.int32, (1, marks), 1)

    def step(group, carry):
        rows = pl.ds(pl.multiple_of(group * 8, 8), 8)
        comp = comp_ref[rows, :]
        strain = strain_ref[rows, :]
        weight = live_ref[rows, :].astype(F32)
        cell = cell_ref[rows, :]
        soften = strain / (1.0 + strain)
        logv = weight * (LOG_HIGH * comp + LOG_LOW * (1.0 - comp) - WEAKENING * soften)
        rho = weight * (1.0 + DENSITY_JUMP * comp - SOFTENING * soften)
        pieces = [*split(logv), *split(rho), weight, jnp.zeros_like(weight)]
        values = jnp.concatenate(pieces, axis=0)
        depth = (cell & (marks - 1)).astype(F32)
        column = (cell >> shift).astype(F32)
        sums = jnp.zeros((48, marks), F32)
        for pair in range(4):
            left, right = [], []
            for k in (2 * pair, 2 * pair + 1):
                left.append(jnp.where(row_ids == k, values, 0.0).astype(BF16))
                line = jnp.broadcast_to(depth[k : k + 1, :], (16, marks)).astype(BF16)
                line = jnp.concatenate([line] * (marks // 16), axis=0)
                right.append(jnp.where(depth_ids == line, BF16(1.0), BF16(0.0)))
            sums = sums + lax.dot_general(
                jnp.concatenate(left, axis=1),
                jnp.concatenate(right, axis=1),
                (((1,), (1,)), ((), ())),
                preferred_element_type=F32,
            )
        sum_logv = sums[0:8] + sums[8:16]
        sum_rho = sums[16:24] + sums[24:32]
        count = sums[32:40]
        for k in range(8):
            owner = dest_ref[group * 8 + k]
            rank = used_ref[owner]
            used_ref[owner] = rank + 1
            base = owner * chunk
            out_ref[pl.ds(base + rank, 1), :] = sum_logv[k : k + 1]
            out_ref[pl.ds(base + slots + rank, 1), :] = sum_rho[k : k + 1]
            out_ref[pl.ds(base + 2 * slots + rank, 1), :] = count[k : k + 1]
            ids = pl.ds(base + 3 * slots, 1)
            out_ref[ids, :] = jnp.where(lane_ids == rank, column[k : k + 1], out_ref[ids, :])
        return carry

    lax.fori_loop(0, blocks // 8, step, 0)


def average_kernel(
    slots,
    chunk,
    bricks,
    recv_ref,
    old_ref,
    logvisc_ref,
    density_ref,
    visc_ref,
    force_ref,
    x_low_ref,
    x_high_ref,
    y_low_ref,
    y_high_ref,
    hot_ref,
    value_ref,
):
    size_x, size_y = bricks
    columns, depth = old_ref.shape
    total = hot_ref.shape[1]
    per = depth // slots
    lanes = lax.broadcasted_iota(jnp.int32, (1, depth), 1)
    column_ids = lax.broadcasted_iota(jnp.int32, (columns, depth), 0).astype(F32)
    for part in range(total // depth):
        span = slice(part * depth, (part + 1) * depth)
        ids = jnp.full((1, depth), -1.0, F32)
        for k in range(per):
            first = (part * per + k) * chunk
            line = recv_ref[first + 3 * slots : first + 3 * slots + 1, :]
            if k:
                line = pltpu.roll(line, k * slots, 1)
            ids = jnp.where((lanes >= k * slots) & (lanes < (k + 1) * slots), line, ids)
        hot_ref[:, span] = jnp.where(column_ids == ids, 1.0, 0.0).astype(BF16)
        for v in range(3):
            block = jnp.concatenate(
                [
                    recv_ref[pl.ds((part * per + k) * chunk + v * slots, slots), :]
                    for k in range(per)
                ],
                axis=0,
            )
            high, low = split(block)
            value_ref[span, pl.ds(2 * v * depth, depth)] = high.astype(BF16)
            if v < 2:
                value_ref[span, pl.ds((2 * v + 1) * depth, depth)] = low.astype(BF16)
    for tile in range(columns // depth):
        span = slice(tile * depth, (tile + 1) * depth)
        sums = jnp.dot(hot_ref[span, :], value_ref[...], preferred_element_type=F32)
        sum_logv = sums[:, 0:depth] + sums[:, depth : 2 * depth]
        sum_rho = sums[:, 2 * depth : 3 * depth] + sums[:, 3 * depth : 4 * depth]
        count = sums[:, 4 * depth : 5 * depth] + 1.0
        logvisc = (sum_logv + old_ref[span, :]) / count
        density = (sum_rho + 1.0) / count
        logvisc_ref[span, :] = logvisc
        density_ref[span, :] = density
        visc_ref[span, :] = jnp.exp(logvisc)
        force_ref[span, :] = GRAVITY * (1.0 - density)
    near = size_y
    x_low_ref[0 : 2 * near, :] = visc_ref[0 : 2 * near, :]
    x_low_ref[2 * near : 3 * near, :] = force_ref[0:near, :]
    x_high_ref[0 : 2 * near, :] = visc_ref[columns - 2 * near : columns, :]
    x_high_ref[2 * near : 3 * near, :] = force_ref[columns - near : columns, :]
    y_low_ref[...] = jnp.zeros_like(y_low_ref)
    y_high_ref[...] = jnp.zeros_like(y_high_ref)
    for ref, first, second in ((y_low_ref, 0, 1), (y_high_ref, size_y - 1, size_y - 2)):
        ref[NEAR : NEAR + size_x, :] = visc_ref[pl.ds(first, size_x, stride=size_y), :]
        ref[FAR : FAR + size_x, :] = visc_ref[pl.ds(second, size_x, stride=size_y), :]
        ref[LINE : LINE + size_x, :] = force_ref[pl.ds(first, size_x, stride=size_y), :]


def smooth_kernel(
    bricks,
    inside_ref,
    visc_ref,
    force_ref,
    vel_ref,
    vx_low_ref,
    vx_high_ref,
    vy_low_ref,
    vy_high_ref,
    x_low_ref,
    x_high_ref,
    y_low_ref,
    y_high_ref,
    out_ref,
    wide_visc,
    wide_vel,
    wide_next,
    coeff_ref,
):
    size_x, size_y = bricks
    cells, depth = visc_ref.shape
    pitch = size_y + 16
    lanes = lax.broadcasted_iota(jnp.int32, (1, depth), 1)

    def place(ref, offset, core, low, high, near_low, near_high):
        for plane in range(2):
            ref[pl.ds(offset + plane * pitch + 8, size_y), :] = low(plane)
            ref[pl.ds(offset + (size_x + 2 + plane) * pitch + 8, size_y), :] = high(plane)
        for plane in range(size_x):
            ref[pl.ds(offset + (plane + 2) * pitch + 8, size_y), :] = core(plane)
        planes = size_x + 2
        ref[pl.ds(offset + pitch + 7, planes, stride=pitch), :] = near_low
        ref[pl.ds(offset + pitch + 8 + size_y, planes, stride=pitch), :] = near_high

    def block(ref, first, count):
        return ref[pl.ds(first, count), :]

    place(
        wide_visc,
        0,
        lambda p: block(visc_ref, p * size_y, size_y),
        lambda p: block(x_low_ref, p * size_y, size_y),
        lambda p: block(x_high_ref, p * size_y, size_y),
        block(y_low_ref, NEAR - 1, size_x + 2),
        block(y_high_ref, NEAR - 1, size_x + 2),
    )
    field = (size_x + 4) * pitch
    field_next = (size_x + 2) * pitch
    for c in range(3):
        place(
            wide_vel,
            c * field,
            lambda p: block(vel_ref, c * cells + p * size_y, size_y),
            lambda p: block(vx_low_ref, (2 * c + p) * size_y, size_y),
            lambda p: block(vx_high_ref, (2 * c + p) * size_y, size_y),
            block(vy_low_ref, c * LINE + NEAR - 1, size_x + 2),
            block(vy_high_ref, c * LINE + NEAR - 1, size_x + 2),
        )

    def factors(visc, beside, force):
        up = jnp.where(lanes == depth - 1, 0.0, pltpu.roll(visc, depth - 1, 1))
        down = jnp.where(lanes == 0, 0.0, pltpu.roll(visc, 1, 1))
        faces = [visc + other for other in (*beside, up, down)]
        total = ((faces[0] + faces[1]) + (faces[2] + faces[3])) + (faces[4] + faces[5])
        scale = RELAX / total
        faces = [face * scale for face in faces]
        faces[4] = jnp.where(lanes == depth - 1, 0.0, faces[4])
        faces[5] = jnp.where(lanes == 0, 0.0, faces[5])
        return faces, 2.0 * force * scale

    def relax(faces, push, vel, beside):
        up = pltpu.roll(vel, depth - 1, 1)
        down = pltpu.roll(vel, 1, 1)
        terms = [face * other for face, other in zip(faces, (*beside, up, down))]
        result = ((terms[0] + terms[1]) + (terms[2] + terms[3])) + (terms[4] + terms[5])
        result = result + (1.0 - RELAX) * vel
        return result if push is None else result + push

    def around(ref, first):
        return (
            ref[pl.ds(first + pitch, size_y), :],
            ref[pl.ds(first - pitch, size_y), :],
            ref[pl.ds(first + 1, size_y), :],
            ref[pl.ds(first - 1, size_y), :],
        )

    def first_sweep(plane, force):
        at = (plane + 2) * pitch + 8
        faces, push = factors(wide_visc[pl.ds(at, size_y), :], around(wide_visc, at), force)
        results = []
        for c in range(3):
            vel = wide_vel[pl.ds(c * field + at, size_y), :]
            beside = around(wide_vel, c * field + at)
            results.append(relax(faces, push if c == 2 else None, vel, beside))
        return faces, push, results

    def put(plane, results):
        for c in range(3):
            at = c * field_next + (plane + 1) * pitch + 8
            wide_next[pl.ds(at, size_y), :] = results[c]

    for plane, ref, side in ((-1, x_low_ref, 0), (size_x, x_high_ref, 1)):
        _, _, results = first_sweep(plane, ref[pl.ds(2 * size_y, size_y), :])
        put(plane, [jnp.where(inside_ref[side] > 0, value, 0.0) for value in results])

    for row, near_row, visc_lines, vel_lines, side in (
        (7, 0, y_low_ref, vy_low_ref, 2),
        (8 + size_y, size_y - 1, y_high_ref, vy_high_ref, 3),
    ):

        def around_line(ref, first, inner):
            return (
                ref[pl.ds(first + NEAR + 1, size_x), :],
                ref[pl.ds(first + NEAR - 1, size_x), :],
                inner,
                ref[pl.ds(first + FAR, size_x), :],
            )

        inner = visc_ref[pl.ds(near_row, size_x, stride=size_y), :]
        faces, push = factors(
            visc_lines[pl.ds(NEAR, size_x), :],
            around_line(visc_lines, 0, inner),
            visc_lines[pl.ds(LINE, size_x), :],
        )
        for c in range(3):
            inner = vel_ref[pl.ds(c * cells + near_row, size_x, stride=size_y), :]
            value = relax(
                faces,
                push if c == 2 else None,
                vel_lines[pl.ds(c * LINE + NEAR, size_x), :],
                around_line(vel_lines, c * LINE, inner),
            )
            value = jnp.where(inside_ref[side] > 0, value, 0.0)
            at = c * field_next + pitch + row
            wide_next[pl.ds(at, size_x, stride=pitch), :] = value

    for plane in range(size_x):
        faces, push, results = first_sweep(plane, force_ref[pl.ds(plane * size_y, size_y), :])
        put(plane, results)
        for k, value in enumerate((*faces, push)):
            coeff_ref[pl.ds(k * cells + plane * size_y, size_y), :] = value

    for plane in range(size_x):
        faces = [coeff_ref[pl.ds(k * cells + plane * size_y, size_y), :] for k in range(6)]
        push = coeff_ref[pl.ds(6 * cells + plane * size_y, size_y), :]
        for c in range(3):
            at = c * field_next + (plane + 1) * pitch + 8
            vel = wide_next[pl.ds(at, size_y), :]
            value = relax(faces, push if c == 2 else None, vel, around(wide_next, at))
            out_ref[pl.ds(c * cells + plane * size_y, size_y), :] = value


def shifted(value, axis, step):
    count = lax.axis_size(axis)
    pairs = [(i, i + step) for i in range(count) if 0 <= i + step < count]
    return lax.ppermute(value, axis, pairs)


def per_device(
    marker_comp, marker_strain, marker_live, marker_cell, block_dest, old_logvisc, velocity
):
    count_x = lax.axis_size("gx")
    count_y = lax.axis_size("gy")
    devices = count_x * count_y
    blocks, marks = marker_comp.shape
    size_x, size_y, depth = old_logvisc.shape
    columns = size_x * size_y
    slots = 2 * blocks // devices
    chunk = -(-(3 * slots + 1) // 8) * 8
    total = devices * slots

    payload = pl.pallas_call(
        functools.partial(pack_kernel, slots, chunk),
        out_shape=jax.ShapeDtypeStruct((devices * chunk, marks), F32),
        in_specs=[SMEM, VMEM, VMEM, VMEM, VMEM],
        out_specs=VMEM,
        scratch_shapes=[pltpu.SMEM((devices,), jnp.int32)],
        name="pack",
    )(block_dest.reshape(blocks), marker_comp, marker_strain, marker_live, marker_cell)
    received = lax.all_to_all(payload, BOTH, split_axis=0, concat_axis=0, tiled=True)

    vx_low = shifted(velocity[:, size_x - 2 :], "gx", 1)
    vx_high = shifted(velocity[:, :2], "gx", -1)

    def vel_lines(near, far):
        blank = jnp.zeros((3, 7, depth), F32)
        parts = [blank, vx_low[:, 1, near][:, None], velocity[:, :, near]]
        parts += [vx_high[:, 0, near][:, None], blank, velocity[:, :, far]]
        return jnp.concatenate(parts, axis=1)

    vy_low = shifted(vel_lines(size_y - 1, size_y - 2), "gy", 1)
    vy_high = shifted(vel_lines(0, 1), "gy", -1)

    field = jax.ShapeDtypeStruct((columns, depth), F32)
    x_side = jax.ShapeDtypeStruct((3 * size_y, depth), F32)
    y_side = jax.ShapeDtypeStruct((LINE + size_x, depth), F32)
    logvisc, density, visc, force, x_first, x_last, y_first, y_last = pl.pallas_call(
        functools.partial(average_kernel, slots, chunk, (size_x, size_y)),
        out_shape=(field, field, field, field, x_side, x_side, y_side, y_side),
        in_specs=[VMEM, VMEM],
        out_specs=(VMEM,) * 8,
        scratch_shapes=[pltpu.VMEM((columns, total), BF16), pltpu.VMEM((total, 5 * depth), BF16)],
        name="average",
    )(received, old_logvisc.reshape(columns, depth))

    x_low = shifted(x_last, "gx", 1)
    x_high = shifted(x_first, "gx", -1)

    def with_corners(lines, near):
        parts = [lines[:7], x_low[size_y + near][None], lines[8 : 8 + size_x]]
        parts += [x_high[near][None], lines[9 + size_x :]]
        return jnp.concatenate(parts, axis=0)

    y_low = shifted(with_corners(y_last, size_y - 1), "gy", 1)
    y_high = shifted(with_corners(y_first, 0), "gy", -1)

    at_x = lax.axis_index("gx")
    at_y = lax.axis_index("gy")
    inside = jnp.stack([at_x > 0, at_x < count_x - 1, at_y > 0, at_y < count_y - 1])
    pitch = size_y + 16
    smoothed = pl.pallas_call(
        functools.partial(smooth_kernel, (size_x, size_y)),
        out_shape=jax.ShapeDtypeStruct((3 * columns, depth), F32),
        in_specs=[SMEM] + [VMEM] * 11,
        out_specs=VMEM,
        scratch_shapes=[
            pltpu.VMEM(((size_x + 4) * pitch, depth), F32),
            pltpu.VMEM((3 * (size_x + 4) * pitch, depth), F32),
            pltpu.VMEM((3 * (size_x + 2) * pitch, depth), F32),
            pltpu.VMEM((7 * columns, depth), F32),
        ],
        name="smooth",
    )(
        inside.astype(jnp.int32),
        visc,
        force,
        velocity.reshape(3 * columns, depth),
        vx_low.reshape(-1, depth),
        vx_high.reshape(-1, depth),
        vy_low.reshape(-1, depth),
        vy_high.reshape(-1, depth),
        x_low,
        x_high,
        y_low,
        y_high,
    )
    return (
        logvisc.reshape(old_logvisc.shape),
        density.reshape(old_logvisc.shape),
        smoothed.reshape(velocity.shape),
    )


def solution(mesh):
    return jax.shard_map(
        per_device,
        mesh=mesh,
        in_specs=(
            P(("gx", "gy"), None),
            P(("gx", "gy"), None),
            P(("gx", "gy"), None),
            P(("gx", "gy"), None),
            P(("gx", "gy"), None),
            P("gx", "gy", None),
            P(None, "gx", "gy", None),
        ),
        out_specs=(P("gx", "gy", None), P("gx", "gy", None), P(None, "gx", "gy", None)),
        check_vma=False,
    )
```

time: 224 us -> 101 us (0.45)
  the two profiles are of different devices: /device:TPU:0 before, /device:TPU:12 now
where the time goes in v1:
time: 101 us; the launch traced here: 100 us
  waiting for transfers between devices  36.5 us (36%)
  starting transfers between devices  27 us (27%)
  Pallas kernels  25 us (25%)
  local copies, waits for them, and re-layouts  10.3 us (10%)
    all_to_all x1, waiting for transfers between devices, per_device(): lax.all_to_all(payload, BOTH, split_axis=0, concat_axis=0, tiled=True)  28.1 us
    ppermute x8, starting transfers between devices, shifted(): return lax.ppermute(value, axis, pairs)  21 us
    pallas_call x1, Pallas kernels, per_device(): pl.pallas_call(functools.partial(pack_kernel, slots, chunk), out_shape=ja...  17.6 us
    ppermute x8, waiting for transfers between devices, shifted(): return lax.ppermute(value, axis, pairs)  8.44 us
    all_to_all x1, starting transfers between devices, per_device(): lax.all_to_all(payload, BOTH, split_axis=0, concat_axis=0, tiled=True)  5.99 us
    pallas_call x1, Pallas kernels, per_device(): pl.pallas_call(functools.partial(average_kernel, slots, chunk, (size_x, s...  3.71 us
    pallas_call x1, Pallas kernels, per_device(): pl.pallas_call(functools.partial(smooth_kernel, (size_x, size_y)), out_sh...  3.7 us
    slice x5, local copies, waits for them, and re-layouts, with_corners(): parts = [lines[:7], x_low[size_y + near][None], lines[8:8 + size_x]]  2.75 us
  transfers between devices with their start and end apart: 9, of which 3 were waited for; matrix products, arithmetic and copies ran while one was open for 9% of the time, Pallas kernels for 4%

profile of v1, /device:TPU:12, one launch (start us, length us, event | category | flops | bytes accessed | tf_op | source)
XLA Modules:
  0.0 100.2 jit_solution(13927221929775495059)
XLA Ops:
  0.6 17.6 %pack.1 = f32[3328,128]{1,0:T(8,128)} custom-call(s32[512]{0:T(512)} %bitcast.45, f32[512,128]{1,0:T(8,128)} %comp_ref.1, f32[512,128]{1,0:T(8,128)} %strain_ref.1, s32[512,128]{1,0:T(8,128)} %live_ref.1, s32[512,128]{1,0:T(8,128)} %cell_ref.1), custom_call_target="tpu_custom_call" | custom-call | tf_op jit(solution)/shard_map/pack/pallas_call | solution.py:333
  18.2 6.0 %all-to-all-start = ((f32[32,104,128]{2,1,0:T(8,128)}), f32[32,104,128]{2,1,0:T(8,128)S(1)}, u32[]{:S(2)}, u32[]{:S(2)}) async-start(f32[32,104,128]{2,1,0:T(8,128)} %bitcast.32), calls=%async_computation | async-start | bytes 3407872 | tf_op jit(solution)/shard_map/all_to_all | solution.py:341
  24.2 1.0 fusion.1
  25.2 0.1 copy.17
  25.3 3.1 %collective-permute-start.1 = (f32[3,2,32,128]{3,1,2,0:T(2,128)S(1)}, f32[3,2,32,128]{3,1,2,0:T(2,128)S(1)}, u32[]{:S(2)}, u32[]{:S(2)}) collective-permute-start(f32[3,2,32,128]{3,1,2,0:T(2,128)S(1)} %copy.17), channel_id=1, source_target_pairs={{4,0},{8,4},{12,8},{16,12},{20,16},{24,20},{28,24},{5,1},{9,5},{13... | collective-permute-start | bytes 294920 | tf_op jit(solution)/shard_map/ppermute | solution.py:317
  28.4 0.1 copy.16
  28.5 1.9 %collective-permute-start = (f32[3,2,32,128]{3,1,2,0:T(2,128)S(1)}, f32[3,2,32,128]{3,1,2,0:T(2,128)S(1)}, u32[]{:S(2)}, u32[]{:S(2)}) collective-permute-start(f32[3,2,32,128]{3,1,2,0:T(2,128)S(1)} %copy.16), channel_id=1, source_target_pairs={{0,4},{4,8},{8,12},{12,16},{16,20},{20,24},{24,28},{1,5},{5,9},{9,... | collective-permute-start | bytes 294920 | tf_op jit(solution)/shard_map/ppermute | solution.py:317
  30.4 1.3 %fusion = (f32[3,16,1,128]{3,2,1,0:T(1,128)S(1)}, f32[3,16,1,128]{3,2,1,0:T(1,128)S(1)}, f32[3,16,1,128]{3,2,1,0:T(1,128)S(1)}, f32[3,16,1,128]{3,2,1,0:T(1,128)S(1)}) fusion(f32[3,16,32,128]{3,2,1,0:T(8,128)} %param.13), kind=kLoop, calls=%fused_computation.5 | loop fusion | bytes 196608 | tf_op jit(solution)/shard_map/slice | solution.py:349
  31.7 3.9 %collective-permute-done.1 = f32[3,2,32,128]{3,1,2,0:T(2,128)S(1)} collective-permute-done((f32[3,2,32,128]{3,1,2,0:T(2,128)S(1)}, f32[3,2,32,128]{3,1,2,0:T(2,128)S(1)}, u32[]{:S(2)}, u32[]{:S(2)}) %collective-permute-start.1) | collective-permute-done | bytes 98336 | tf_op jit(solution)/shard_map/ppermute | solution.py:317
  35.6 28.1 %all-to-all-done = f32[32,104,128]{2,1,0:T(8,128)S(1)} async-done(((f32[32,104,128]{2,1,0:T(8,128)}), f32[32,104,128]{2,1,0:T(8,128)S(1)}, u32[]{:S(2)}, u32[]{:S(2)}) %all-to-all-start) | async-done | bytes 1703968 | tf_op jit(solution)/shard_map/all_to_all | solution.py:341
  63.7 0.0 copy-start
  63.7 1.2 %copy-done = f32[32,104,128]{2,1,0:T(8,128)} copy-done((f32[32,104,128]{2,1,0:T(8,128)}, f32[32,104,128]{2,1,0:T(8,128)S(1)}, u32[]{:S(2)}) %copy-start) | copy-done | bytes 1703960
  65.0 3.7 %average.1 = (f32[512,128]{1,0:T(8,128)}, f32[512,128]{1,0:T(8,128)}, f32[512,128]{1,0:T(8,128)}, f32[512,128]{1,0:T(8,128)}, f32[96,128]{1,0:T(8,128)}, /*index...) custom-call(f32[3328,128]{1,0:T(8,128)} %bitcast.33, f32[512,128]{1,0:T(8,128)} %bitcast.38), custom_call_target="tpu_custom_call" | custom-call | tf_op jit(solution)/shard_map/average/pallas_call | solution.py:358
  68.7 2.4 %collective-permute-start.5 = (f32[96,128]{1,0:T(8,128)}, f32[96,128]{1,0:T(8,128)S(1)}, u32[]{:S(2)}, u32[]{:S(2)}) collective-permute-start(f32[96,128]{1,0:T(8,128)} %get-tuple-element.16), channel_id=1, source_target_pairs={{4,0},{8,4},{12,8},{16,12},{20,16},{24,20},{28,24},{5,1},{9,5},{13... | collective-permute-start | bytes 147464 | tf_op jit(solution)/shard_map/ppermute | solution.py:317
  71.0 0.0 collective-permute-done
  71.1 3.4 %collective-permute-start.2 = (f32[3,48,128]{2,1,0:T(8,128)S(1)}, f32[3,48,128]{2,1,0:T(8,128)S(1)}, u32[]{:S(2)}, u32[]{:S(2)}) collective-permute-start(f32[3,48,128]{2,1,0:T(8,128)S(1)} %concatenate.12), channel_id=1, source_target_pairs={{0,1},{1,2},{2,3},{4,5},{5,6},{6,7},{8,9},{9,10},{10,11},{12,13},{... | collective-permute-start | bytes 221192 | tf_op jit(solution)/shard_map/ppermute | solution.py:317
  74.5 2.5 %collective-permute-start.3 = (f32[3,48,128]{2,1,0:T(8,128)S(1)}, f32[3,48,128]{2,1,0:T(8,128)S(1)}, u32[]{:S(2)}, u32[]{:S(2)}) collective-permute-start(f32[3,48,128]{2,1,0:T(8,128)S(1)} %concatenate.13), channel_id=1, source_target_pairs={{1,0},{2,1},{3,2},{5,4},{6,5},{7,6},{9,8},{10,9},{11,10},{13,12},{... | collective-permute-start | bytes 221192 | tf_op jit(solution)/shard_map/ppermute | solution.py:317
  77.0 0.7 slice.79
  77.7 0.7 slice.77
  78.4 0.7 slice.75
  79.1 0.7 slice.74
  79.8 0.7 slice.72
  80.5 0.7 slice.70
  81.2 1.9 %collective-permute-start.4 = (f32[96,128]{1,0:T(8,128)}, f32[96,128]{1,0:T(8,128)S(1)}, u32[]{:S(2)}, u32[]{:S(2)}) collective-permute-start(f32[96,128]{1,0:T(8,128)} %get-tuple-element.15), channel_id=1, source_target_pairs={{0,4},{4,8},{8,12},{12,16},{16,20},{20,24},{24,28},{1,5},{5,9},{9,... | collective-permute-start | bytes 147464 | tf_op jit(solution)/shard_map/ppermute | solution.py:317
  83.1 0.0 collective-permute-done.5.x_high_ref
  83.1 0.0 copy-start.3
  83.2 4.6 %collective-permute-done.4.x_low_ref = f32[96,128]{1,0:T(8,128)S(1)} collective-permute-done((f32[96,128]{1,0:T(8,128)}, f32[96,128]{1,0:T(8,128)S(1)}, u32[]{:S(2)}, u32[]{:S(2)}) %collective-permute-start.4) | collective-permute-done | bytes 49184 | tf_op jit(solution)/shard_map/ppermute | solution.py:317
  87.7 0.0 copy-start.4
  87.7 0.2 concatenate.15
  87.9 1.9 %collective-permute-start.7 = (f32[64,128]{1,0:T(8,128)S(1)}, f32[64,128]{1,0:T(8,128)S(1)}, u32[]{:S(2)}, u32[]{:S(2)}) collective-permute-start(f32[64,128]{1,0:T(8,128)S(1)} %concatenate.15), channel_id=1, source_target_pairs={{1,0},{2,1},{3,2},{5,4},{6,5},{7,6},{9,8},{10,9},{11,10},{13,12},{... | collective-permute-start | bytes 98312 | tf_op jit(solution)/shard_map/ppermute | solution.py:317
  89.9 0.2 concatenate.14
  90.0 3.9 %collective-permute-start.6 = (f32[64,128]{1,0:T(8,128)S(1)}, f32[64,128]{1,0:T(8,128)S(1)}, u32[]{:S(2)}, u32[]{:S(2)}) collective-permute-start(f32[64,128]{1,0:T(8,128)S(1)} %concatenate.14), channel_id=1, source_target_pairs={{0,1},{1,2},{2,3},{4,5},{5,6},{6,7},{8,9},{9,10},{10,11},{12,13},{... | collective-permute-start | bytes 98312 | tf_op jit(solution)/shard_map/ppermute | solution.py:317
  94.0 0.6 add_convert_fusion.inside_ref
  94.6 0.6 copy.11
  95.2 0.6 copy.13
  95.9 0.0 collective-permute-done.2
  95.9 0.0 copy-start.1
  95.9 0.0 collective-permute-done.3
  95.9 0.0 copy-start.2
  95.9 0.0 collective-permute-done.7.y_high_ref
  95.9 0.0 copy-start.5
  95.9 0.0 collective-permute-done.6.y_low_ref
  95.9 0.0 copy-start.6
  95.9 0.0 copy-done.3
  95.9 0.0 copy-done.4
  95.9 0.5 copy-done.1
  96.5 0.0 copy-done.2
  96.5 0.0 copy-done.5
  96.5 0.0 copy-done.6
  96.5 3.7 %smooth.1 = f32[1536,128]{1,0:T(8,128)} custom-call(s32[4]{0:T(128)} %add_convert_fusion.inside_ref, f32[512,128]{1,0:T(8,128)} %get-tuple-element.13.visc_ref, f32[512,128]{1,0:T(8,128)} %get-tuple-element.14.force_ref, f32[1536,128]{1,0:T(8,128)} %bitcast.34, f32[192,128]{1,0:T(8,128)} %bitcast.36, f32[192,128]{1,0:T(8,128)} %bitcast.37, ...), custom_call_target="tpu_custom_call" | custom-call | tf_op jit(solution)/shard_map/smooth/pallas_call | solution.py:382
  (7 shorter events, 0.1 us)
Async XLA Ops:
  18.2 45.5 %all-to-all-start = ((f32[32,104,128]{2,1,0:T(8,128)}), f32[32,104,128]{2,1,0:T(8,128)S(1)}, u32[]{:S(2)}, u32[]{:S(2)}) async-start(f32[32,104,128]{2,1,0:T(8,128)} %bitcast.32), calls=%async_computation | async-start | bytes 3407872 | tf_op jit(solution)/shard_map/all_to_all | solution.py:341
  25.3 10.3 %collective-permute-start.1 = (f32[3,2,32,128]{3,1,2,0:T(2,128)S(1)}, f32[3,2,32,128]{3,1,2,0:T(2,128)S(1)}, u32[]{:S(2)}, u32[]{:S(2)}) collective-permute-start(f32[3,2,32,128]{3,1,2,0:T(2,128)S(1)} %copy.17), channel_id=1, source_target_pairs={{4,0},{8,4},{12,8},{16,12},{20,16},{24,20},{28,24},{5,1},{9,5},{13... | collective-permute-start | bytes 294920 | tf_op jit(solution)/shard_map/ppermute | solution.py:317
  28.5 42.6 %collective-permute-start = (f32[3,2,32,128]{3,1,2,0:T(2,128)S(1)}, f32[3,2,32,128]{3,1,2,0:T(2,128)S(1)}, u32[]{:S(2)}, u32[]{:S(2)}) collective-permute-start(f32[3,2,32,128]{3,1,2,0:T(2,128)S(1)} %copy.16), channel_id=1, source_target_pairs={{0,4},{4,8},{8,12},{12,16},{16,20},{20,24},{24,28},{1,5},{5,9},{9,... | collective-permute-start | bytes 294920 | tf_op jit(solution)/shard_map/ppermute | solution.py:317
  63.7 1.2 %copy-start = (f32[32,104,128]{2,1,0:T(8,128)}, f32[32,104,128]{2,1,0:T(8,128)S(1)}, u32[]{:S(2)}) copy-start(f32[32,104,128]{2,1,0:T(8,128)S(1)} %all-to-all-done) | copy-start | bytes 5111812
  68.7 14.5 %collective-permute-start.5 = (f32[96,128]{1,0:T(8,128)}, f32[96,128]{1,0:T(8,128)S(1)}, u32[]{:S(2)}, u32[]{:S(2)}) collective-permute-start(f32[96,128]{1,0:T(8,128)} %get-tuple-element.16), channel_id=1, source_target_pairs={{4,0},{8,4},{12,8},{16,12},{20,16},{24,20},{28,24},{5,1},{9,5},{13... | collective-permute-start | bytes 147464 | tf_op jit(solution)/shard_map/ppermute | solution.py:317
  71.1 24.7 %collective-permute-start.2 = (f32[3,48,128]{2,1,0:T(8,128)S(1)}, f32[3,48,128]{2,1,0:T(8,128)S(1)}, u32[]{:S(2)}, u32[]{:S(2)}) collective-permute-start(f32[3,48,128]{2,1,0:T(8,128)S(1)} %concatenate.12), channel_id=1, source_target_pairs={{0,1},{1,2},{2,3},{4,5},{5,6},{6,7},{8,9},{9,10},{10,11},{12,13},{... | collective-permute-start | bytes 221192 | tf_op jit(solution)/shard_map/ppermute | solution.py:317
  74.5 21.3 %collective-permute-start.3 = (f32[3,48,128]{2,1,0:T(8,128)S(1)}, f32[3,48,128]{2,1,0:T(8,128)S(1)}, u32[]{:S(2)}, u32[]{:S(2)}) collective-permute-start(f32[3,48,128]{2,1,0:T(8,128)S(1)} %concatenate.13), channel_id=1, source_target_pairs={{1,0},{2,1},{3,2},{5,4},{6,5},{7,6},{9,8},{10,9},{11,10},{13,12},{... | collective-permute-start | bytes 221192 | tf_op jit(solution)/shard_map/ppermute | solution.py:317
  81.2 6.5 %collective-permute-start.4 = (f32[96,128]{1,0:T(8,128)}, f32[96,128]{1,0:T(8,128)S(1)}, u32[]{:S(2)}, u32[]{:S(2)}) collective-permute-start(f32[96,128]{1,0:T(8,128)} %get-tuple-element.15), channel_id=1, source_target_pairs={{0,4},{4,8},{8,12},{12,16},{16,20},{20,24},{24,28},{1,5},{5,9},{9,... | collective-permute-start | bytes 147464 | tf_op jit(solution)/shard_map/ppermute | solution.py:317
  83.1 12.8 %copy-start.3 = (f32[96,128]{1,0:T(8,128)}, f32[96,128]{1,0:T(8,128)S(1)}, u32[]{:S(2)}) copy-start(f32[96,128]{1,0:T(8,128)S(1)} %collective-permute-done.5.x_high_ref) | copy-start | bytes 147460
  87.7 8.2 %copy-start.4 = (f32[96,128]{1,0:T(8,128)}, f32[96,128]{1,0:T(8,128)S(1)}, u32[]{:S(2)}) copy-start(f32[96,128]{1,0:T(8,128)S(1)} %collective-permute-done.4.x_low_ref) | copy-start | bytes 147460
  87.9 8.0 %collective-permute-start.7 = (f32[64,128]{1,0:T(8,128)S(1)}, f32[64,128]{1,0:T(8,128)S(1)}, u32[]{:S(2)}, u32[]{:S(2)}) collective-permute-start(f32[64,128]{1,0:T(8,128)S(1)} %concatenate.15), channel_id=1, source_target_pairs={{1,0},{2,1},{3,2},{5,4},{6,5},{7,6},{9,8},{10,9},{11,10},{13,12},{... | collective-permute-start | bytes 98312 | tf_op jit(solution)/shard_map/ppermute | solution.py:317
  90.0 5.9 %collective-permute-start.6 = (f32[64,128]{1,0:T(8,128)S(1)}, f32[64,128]{1,0:T(8,128)S(1)}, u32[]{:S(2)}, u32[]{:S(2)}) collective-permute-start(f32[64,128]{1,0:T(8,128)S(1)} %concatenate.14), channel_id=1, source_target_pairs={{0,1},{1,2},{2,3},{4,5},{5,6},{6,7},{8,9},{9,10},{10,11},{12,13},{... | collective-permute-start | bytes 98312 | tf_op jit(solution)/shard_map/ppermute | solution.py:317
  95.9 0.6 copy-start.1
  95.9 0.6 copy-start.2
  95.9 0.6 copy-start.5
  95.9 0.6 copy-start.6

commit v2 on v1

--- a/solution.py
+++ b/solution.py
@@ -19,6 +19,10 @@
 BF16 = jnp.bfloat16
 VMEM = pl.BlockSpec(memory_space=pltpu.VMEM)
 SMEM = pl.BlockSpec(memory_space=pltpu.SMEM)
+HBM = pl.BlockSpec(memory_space=pltpu.HBM)
+BY_LANES = (((1,), (1,)), ((), ()))
+WAYS = 4
+BATCH = 32
 NEAR = 8
 FAR = 32
 LINE = 48
@@ -30,62 +34,158 @@
 
 
 def pack_kernel(
-    slots, chunk, dest_ref, comp_ref, strain_ref, live_ref, cell_ref, out_ref, used_ref
+    slots,
+    chunk,
+    dest_hbm,
+    comp_hbm,
+    strain_hbm,
+    live_hbm,
+    cell_hbm,
+    out_ref,
+    place_ref,
+    line_ref,
+    sums_ref,
+    place_sem,
+    dest_ref,
+    comp_ref,
+    strain_ref,
+    live_ref,
+    cell_ref,
+    load_sem,
 ):
-    devices = used_ref.shape[0]
     blocks, marks = comp_ref.shape
+    devices = out_ref.shape[0] // chunk
     shift = marks.bit_length() - 1
+    part = marks // WAYS
+    low_bits = part.bit_length() - 1
+    pairs = (
+        (dest_hbm, dest_ref),
+        (cell_hbm, cell_ref),
+        (comp_hbm, comp_ref),
+        (strain_hbm, strain_ref),
+        (live_hbm, live_ref),
+    )
+    loads = [pltpu.make_async_copy(*pair, load_sem.at[k]) for k, pair in enumerate(pairs)]
+    for load in loads:
+        load.start()
     out_ref[...] = jnp.zeros_like(out_ref)
+    loads[0].wait()
+    loads[1].wait()
+
+    owner_ids = lax.broadcasted_iota(jnp.int32, (devices, marks), 0)
+    rank_ids = lax.broadcasted_iota(jnp.int32, (slots, marks), 0)
+    square = (marks, marks)
+    before = lax.broadcasted_iota(jnp.int32, square, 0) < lax.broadcasted_iota(jnp.int32, square, 1)
+    before = jnp.where(before, 1.0, 0.0).astype(BF16)
+    seen = jnp.zeros((devices, 1), F32)
+    ids = jnp.zeros((devices, slots), F32)
+    for k in range(blocks // marks):
+        dest = dest_ref[k : k + 1, :]
+        mine = owner_ids == dest
+        hot = jnp.where(mine, 1.0, 0.0)
+        earlier = jnp.dot(hot.astype(BF16), before, preferred_element_type=F32) + seen
+        rank = jnp.sum(jnp.where(mine, earlier, 0.0), axis=0, keepdims=True).astype(jnp.int32)
+        seen = seen + jnp.sum(hot, axis=1, keepdims=True)
+        line_ref[k : k + 1, :] = dest * chunk + rank
+        column = (cell_ref[k * marks : (k + 1) * marks, :] >> shift).astype(F32).T[0:1] + 1.0
+        spot = jnp.where(rank_ids == rank, 1.0, 0.0).astype(BF16)
+        for piece in split(column):
+            weighted = jnp.where(mine, piece, 0.0).astype(BF16)
+            ids = ids + lax.dot_general(weighted, spot, BY_LANES, preferred_element_type=F32)
+    places = pltpu.make_async_copy(line_ref, place_ref, place_sem)
+    places.start()
+    ids = ids - 1.0
     for owner in range(devices):
-        used_ref[owner] = 0
-        out_ref[pl.ds(owner * chunk + 3 * slots, 1), :] = jnp.full((1, marks), -1.0, F32)
-    depth_ids = lax.broadcasted_iota(jnp.int32, (marks, marks), 0).astype(F32).astype(BF16)
-    row_ids = lax.broadcasted_iota(jnp.int32, (48, marks), 0) & 7
-    lane_ids = lax.broadcasted_iota(jnp.int32, (1, marks), 1)
-
-    def step(group, carry):
+        at = owner * chunk + 3 * slots
+        out_ref[at : at + 1, 0:slots] = ids[owner : owner + 1, :]
+    for load in loads[2:]:
+        load.wait()
+
+    fine_ids = lax.broadcasted_iota(jnp.int32, (part, marks), 0).astype(F32).astype(BF16)
+    row_ids = lax.broadcasted_iota(jnp.int32, (8, marks), 0)
+    lane_ids = lax.broadcasted_iota(jnp.int32, (8, marks), 1)
+    halves = [row_ids < 4, row_ids >= 4]
+    spans = [(lane_ids >> low_bits) == ((row_ids + w) & (WAYS - 1)) for w in range(WAYS)]
+
+    def depth_sums(group):
         rows = pl.ds(pl.multiple_of(group * 8, 8), 8)
         comp = comp_ref[rows, :]
         strain = strain_ref[rows, :]
         weight = live_ref[rows, :].astype(F32)
-        cell = cell_ref[rows, :]
         soften = strain / (1.0 + strain)
         logv = weight * (LOG_HIGH * comp + LOG_LOW * (1.0 - comp) - WEAKENING * soften)
         rho = weight * (1.0 + DENSITY_JUMP * comp - SOFTENING * soften)
-        pieces = [*split(logv), *split(rho), weight, jnp.zeros_like(weight)]
-        values = jnp.concatenate(pieces, axis=0)
-        depth = (cell & (marks - 1)).astype(F32)
-        column = (cell >> shift).astype(F32)
-        sums = jnp.zeros((48, marks), F32)
-        for pair in range(4):
-            left, right = [], []
-            for k in (2 * pair, 2 * pair + 1):
-                left.append(jnp.where(row_ids == k, values, 0.0).astype(BF16))
-                line = jnp.broadcast_to(depth[k : k + 1, :], (16, marks)).astype(BF16)
-                line = jnp.concatenate([line] * (marks // 16), axis=0)
-                right.append(jnp.where(depth_ids == line, BF16(1.0), BF16(0.0)))
-            sums = sums + lax.dot_general(
-                jnp.concatenate(left, axis=1),
-                jnp.concatenate(right, axis=1),
-                (((1,), (1,)), ((), ())),
-                preferred_element_type=F32,
-            )
-        sum_logv = sums[0:8] + sums[8:16]
-        sum_rho = sums[16:24] + sums[24:32]
-        count = sums[32:40]
-        for k in range(8):
-            owner = dest_ref[group * 8 + k]
-            rank = used_ref[owner]
-            used_ref[owner] = rank + 1
-            base = owner * chunk
-            out_ref[pl.ds(base + rank, 1), :] = sum_logv[k : k + 1]
-            out_ref[pl.ds(base + slots + rank, 1), :] = sum_rho[k : k + 1]
-            out_ref[pl.ds(base + 2 * slots + rank, 1), :] = count[k : k + 1]
-            ids = pl.ds(base + 3 * slots, 1)
-            out_ref[ids, :] = jnp.where(lane_ids == rank, column[k : k + 1], out_ref[ids, :])
+        pieces = [*split(logv), *split(rho), weight]
+        depth = cell_ref[rows, :] & (marks - 1)
+        coarse = ((depth >> low_bits) - row_ids) & (WAYS - 1)
+        fine = (depth & (part - 1)).astype(F32)
+        left, right = [], []
+        for half in halves:
+            lines = []
+            for w in range(WAYS):
+                mask = (coarse == w) & half
+                lines += [jnp.where(mask, piece, 0.0) for piece in pieces]
+            left.append(jnp.concatenate(lines, axis=0).astype(BF16))
+        for first in (0, 4):
+            lines = []
+            for b in range(first, first + 4):
+                line = jnp.broadcast_to(fine[b : b + 1, :], (16, marks)).astype(BF16)
+                line = jnp.concatenate([line] * (part // 16), axis=0)
+                lines.append(jnp.where(fine_ids == line, BF16(1.0), BF16(0.0)))
+            right.append(jnp.concatenate(lines, axis=0))
+        sums = lax.dot_general(
+            jnp.concatenate(left, axis=1),
+            jnp.concatenate(right, axis=1),
+            BY_LANES,
+            preferred_element_type=F32,
+        )
+
+        def piece_sum(w, p):
+            first = (w * len(pieces) + p) * 8
+            return sums[first : first + 8]
+
+        results = []
+        for numbers in ((0, 1), (2, 3), (4,)):
+            total = None
+            for w in range(WAYS):
+                value = piece_sum(w, numbers[0])
+                if len(numbers) > 1:
+                    value = value + piece_sum(w, numbers[1])
+                if w:
+                    value = pltpu.roll(value, part * w, 1)
+                total = value if total is None else jnp.where(spans[w], value, total)
+            results.append(total)
+        return results
+
+    def batch(step, g, f):
+        first = (step & 1) * (24 * BATCH) + g * 24 + f * 8
+        return pl.ds(pl.multiple_of(first, 8), 8)
+
+    def put(step):
+        for g in range(BATCH):
+            for f, value in enumerate(depth_sums(step * BATCH + g)):
+                sums_ref[batch(step, g, f), :] = value
+
+    def place(step):
+        for g in range(BATCH):
+            group = step * BATCH + g
+            values = [sums_ref[batch(step, g, f), :] for f in range(3)]
+            for k in range(8):
+                at = place_ref[group // 16, (group % 16) * 8 + k]
+                for f in range(3):
+                    out_ref[pl.ds(at + f * slots, 1), :] = values[f][k : k + 1]
+
+    steps = blocks // 8 // BATCH
+    put(0)
+    places.wait()
+
+    def step(i, carry):
+        place(i - 1)
+        put(i)
         return carry
 
-    lax.fori_loop(0, blocks // 8, step, 0)
+    lax.fori_loop(1, steps, step, 0)
+    place(steps - 1)
 
 
 def average_kernel(
@@ -160,7 +260,6 @@
 
 def smooth_kernel(
     bricks,
-    inside_ref,
     visc_ref,
     force_ref,
     vel_ref,
@@ -260,13 +359,14 @@
             at = c * field_next + (plane + 1) * pitch + 8
             wide_next[pl.ds(at, size_y), :] = results[c]
 
-    for plane, ref, side in ((-1, x_low_ref, 0), (size_x, x_high_ref, 1)):
+    for plane, ref in ((-1, x_low_ref), (size_x, x_high_ref)):
         _, _, results = first_sweep(plane, ref[pl.ds(2 * size_y, size_y), :])
-        put(plane, [jnp.where(inside_ref[side] > 0, value, 0.0) for value in results])
-
-    for row, near_row, visc_lines, vel_lines, side in (
-        (7, 0, y_low_ref, vy_low_ref, 2),
-        (8 + size_y, size_y - 1, y_high_ref, vy_high_ref, 3),
+        inside = wide_visc[pl.ds((plane + 2) * pitch + 8, size_y), :] > 0.0
+        put(plane, [jnp.where(inside, value, 0.0) for value in results])
+
+    for row, near_row, visc_lines, vel_lines in (
+        (7, 0, y_low_ref, vy_low_ref),
+        (8 + size_y, size_y - 1, y_high_ref, vy_high_ref),
     ):
 
         def around_line(ref, first, inner):
@@ -278,8 +378,9 @@
             )
 
         inner = visc_ref[pl.ds(near_row, size_x, stride=size_y), :]
+        visc = visc_lines[pl.ds(NEAR, size_x), :]
         faces, push = factors(
-            visc_lines[pl.ds(NEAR, size_x), :],
+            visc,
             around_line(visc_lines, 0, inner),
             visc_lines[pl.ds(LINE, size_x), :],
         )
@@ -291,7 +392,7 @@
                 vel_lines[pl.ds(c * LINE + NEAR, size_x), :],
                 around_line(vel_lines, c * LINE, inner),
             )
-            value = jnp.where(inside_ref[side] > 0, value, 0.0)
+            value = jnp.where(visc > 0.0, value, 0.0)
             at = c * field_next + pitch + row
             wide_next[pl.ds(at, size_x, stride=pitch), :] = value
 
@@ -309,6 +410,21 @@
             vel = wide_next[pl.ds(at, size_y), :]
             value = relax(faces, push if c == 2 else None, vel, around(wide_next, at))
             out_ref[pl.ds(c * cells + plane * size_y, size_y), :] = value
+
+
+def corner_kernel(bricks, first_in, last_in, x_low_ref, x_high_ref, first_ref, last_ref):
+    size_x, size_y = bricks
+    for ref, near in ((first_ref, 0), (last_ref, size_y - 1)):
+        ref[NEAR - 1 : NEAR, :] = x_low_ref[size_y + near : size_y + near + 1, :]
+        ref[NEAR + size_x : NEAR + size_x + 1, :] = x_high_ref[near : near + 1, :]
+
+
+def limit(mebibytes):
+    return pltpu.CompilerParams(vmem_limit_bytes=mebibytes << 20)
+
+
+def in_hbm(value):
+    return pltpu.with_memory_space_constraint(value, pltpu.HBM)
 
 
 def shifted(value, axis, step):
@@ -327,30 +443,58 @@
     size_x, size_y, depth = old_logvisc.shape
     columns = size_x * size_y
     slots = 2 * blocks // devices
-    chunk = -(-(3 * slots + 1) // 8) * 8
+    chunk = 3 * slots + 1
     total = devices * slots
+    lines = (blocks // marks, marks)
 
     payload = pl.pallas_call(
         functools.partial(pack_kernel, slots, chunk),
         out_shape=jax.ShapeDtypeStruct((devices * chunk, marks), F32),
-        in_specs=[SMEM, VMEM, VMEM, VMEM, VMEM],
+        in_specs=[HBM] * 5,
         out_specs=VMEM,
-        scratch_shapes=[pltpu.SMEM((devices,), jnp.int32)],
+        scratch_shapes=[
+            pltpu.SMEM(lines, jnp.int32),
+            pltpu.VMEM(lines, jnp.int32),
+            pltpu.VMEM((48 * BATCH, marks), F32),
+            pltpu.SemaphoreType.DMA,
+            pltpu.VMEM(lines, jnp.int32),
+            pltpu.VMEM((blocks, marks), F32),
+            pltpu.VMEM((blocks, marks), F32),
+            pltpu.VMEM((blocks, marks), jnp.int32),
+            pltpu.VMEM((blocks, marks), jnp.int32),
+            pltpu.SemaphoreType.DMA((5,)),
+        ],
+        compiler_params=limit(12),
         name="pack",
-    )(block_dest.reshape(blocks), marker_comp, marker_strain, marker_live, marker_cell)
+    )(
+        in_hbm(block_dest.reshape(lines)),
+        in_hbm(marker_comp),
+        in_hbm(marker_strain),
+        in_hbm(marker_live),
+        in_hbm(marker_cell),
+    )
+    payload = payload.reshape(devices * chunk, 1, marks)
     received = lax.all_to_all(payload, BOTH, split_axis=0, concat_axis=0, tiled=True)
-
-    vx_low = shifted(velocity[:, size_x - 2 :], "gx", 1)
-    vx_high = shifted(velocity[:, :2], "gx", -1)
+    received = received.reshape(devices * chunk, marks)
+
+    def x_planes(first):
+        return velocity[:, first : first + 2].reshape(6 * size_y, depth)
+
+    vx_low = shifted(x_planes(size_x - 2), "gx", 1)
+    vx_high = shifted(x_planes(0), "gx", -1)
 
     def vel_lines(near, far):
         blank = jnp.zeros((3, 7, depth), F32)
-        parts = [blank, vx_low[:, 1, near][:, None], velocity[:, :, near]]
-        parts += [vx_high[:, 0, near][:, None], blank, velocity[:, :, far]]
-        return jnp.concatenate(parts, axis=1)
+        low = vx_low.reshape(3, 2, size_y, depth)[:, 1, near][:, None]
+        high = vx_high.reshape(3, 2, size_y, depth)[:, 0, near][:, None]
+        parts = [blank, low, velocity[:, :, near], high, blank, velocity[:, :, far]]
+        return jnp.concatenate(parts, axis=1).reshape(3 * LINE, depth)
 
     vy_low = shifted(vel_lines(size_y - 1, size_y - 2), "gy", 1)
     vy_high = shifted(vel_lines(0, 1), "gy", -1)
+    received, vx_low, vx_high, vy_low, vy_high = lax.optimization_barrier(
+        (received, vx_low, vx_high, vy_low, vy_high)
+    )
 
     field = jax.ShapeDtypeStruct((columns, depth), F32)
     x_side = jax.ShapeDtypeStruct((3 * size_y, depth), F32)
@@ -361,28 +505,29 @@
         in_specs=[VMEM, VMEM],
         out_specs=(VMEM,) * 8,
         scratch_shapes=[pltpu.VMEM((columns, total), BF16), pltpu.VMEM((total, 5 * depth), BF16)],
+        compiler_params=limit(16),
         name="average",
     )(received, old_logvisc.reshape(columns, depth))
 
     x_low = shifted(x_last, "gx", 1)
     x_high = shifted(x_first, "gx", -1)
-
-    def with_corners(lines, near):
-        parts = [lines[:7], x_low[size_y + near][None], lines[8 : 8 + size_x]]
-        parts += [x_high[near][None], lines[9 + size_x :]]
-        return jnp.concatenate(parts, axis=0)
-
-    y_low = shifted(with_corners(y_last, size_y - 1), "gy", 1)
-    y_high = shifted(with_corners(y_first, 0), "gy", -1)
-
-    at_x = lax.axis_index("gx")
-    at_y = lax.axis_index("gy")
-    inside = jnp.stack([at_x > 0, at_x < count_x - 1, at_y > 0, at_y < count_y - 1])
+    y_first, y_last = pl.pallas_call(
+        functools.partial(corner_kernel, (size_x, size_y)),
+        out_shape=(y_side, y_side),
+        in_specs=[VMEM] * 4,
+        out_specs=(VMEM, VMEM),
+        input_output_aliases={0: 0, 1: 1},
+        compiler_params=limit(4),
+        name="corners",
+    )(y_first, y_last, x_low, x_high)
+    y_low = shifted(y_last, "gy", 1)
+    y_high = shifted(y_first, "gy", -1)
+
     pitch = size_y + 16
     smoothed = pl.pallas_call(
         functools.partial(smooth_kernel, (size_x, size_y)),
         out_shape=jax.ShapeDtypeStruct((3 * columns, depth), F32),
-        in_specs=[SMEM] + [VMEM] * 11,
+        in_specs=[VMEM] * 11,
         out_specs=VMEM,
         scratch_shapes=[
             pltpu.VMEM(((size_x + 4) * pitch, depth), F32),
@@ -390,16 +535,16 @@
             pltpu.VMEM((3 * (size_x + 2) * pitch, depth), F32),
             pltpu.VMEM((7 * columns, depth), F32),
         ],
+        compiler_params=limit(24),
         name="smooth",
     )(
-        inside.astype(jnp.int32),
         visc,
         force,
         velocity.reshape(3 * columns, depth),
-        vx_low.reshape(-1, depth),
-        vx_high.reshape(-1, depth),
-        vy_low.reshape(-1, depth),
-        vy_high.reshape(-1, depth),
+        vx_low,
+        vx_high,
+        vy_low,
+        vy_high,
         x_low,
         x_high,
         y_low,

time: 101 us -> 72 us (0.71)
  the two profiles are of different devices: /device:TPU:12 before, /device:TPU:3 now
where the time goes in v2:
time: 72 us; the launch traced here: 71.6 us
  waiting for transfers between devices  35.9 us (50%)
  starting transfers between devices  25.9 us (36%)
  Pallas kernels  8.89 us (12%)
  between operations  0.78 us (1%)
    ppermute x8, waiting for transfers between devices, shifted(): return lax.ppermute(value, axis, pairs)  25.6 us
    ppermute x8, starting transfers between devices, shifted(): return lax.ppermute(value, axis, pairs)  19.4 us
    all_to_all x1, waiting for transfers between devices, per_device(): lax.all_to_all(payload, BOTH, split_axis=0, concat_axis=0, tiled=True)  10.3 us
    all_to_all x1, starting transfers between devices, per_device(): lax.all_to_all(payload, BOTH, split_axis=0, concat_axis=0, tiled=True)  6.44 us
    pallas_call x1, Pallas kernels, per_device(): pl.pallas_call(functools.partial(pack_kernel, slots, chunk), out_shape=ja...  4.61 us
    pallas_call x1, Pallas kernels, per_device(): pl.pallas_call(functools.partial(smooth_kernel, (size_x, size_y)), out_sh...  2.27 us
    pallas_call x1, Pallas kernels, per_device(): pl.pallas_call(functools.partial(average_kernel, slots, chunk, (size_x, s...  2.01 us
  transfers between devices with their start and end apart: 9, of which 6 were waited for; matrix products, arithmetic and copies ran while one was open for 0% of the time, Pallas kernels for 0%

profile of v2, /device:TPU:3, one launch (start us, length us, event | category | flops | bytes accessed | tf_op | source)
XLA Modules:
  0.0 71.6 jit_solution(1259194961901742412)
XLA Ops:
  0.6 4.6 %pack.1 = f32[3104,128]{1,0:T(8,128)} custom-call(s32[4,128]{1,0:T(4,128)} %bitcast.54, f32[512,128]{1,0:T(8,128)} %comp_hbm.1, f32[512,128]{1,0:T(8,128)} %strain_hbm.1, s32[512,128]{1,0:T(8,128)} %live_hbm.1, s32[512,128]{1,0:T(8,128)} %cell_hbm.1), custom_call_target="tpu_custom_call" | custom-call | tf_op jit(solution)/shard_map/pack/pallas_call | solution.py:450
  5.3 0.0 copy-start
  5.3 0.0 copy-start.1
  5.3 6.4 %all-to-all-start = ((f32[3104,1,128]{2,1,0:T(1,128)}), f32[3104,1,128]{2,1,0:T(1,128)S(1)}, u32[]{:S(2)}, u32[]{:S(2)}) async-start(f32[3104,1,128]{2,1,0:T(1,128)} %bitcast.2), calls=%async_computation | async-start | bytes 3178496 | tf_op jit(solution)/shard_map/all_to_all | solution.py:477
  11.7 0.0 copy-done
  11.8 3.3 %collective-permute-start = (f32[192,128]{1,0:T(8,128)S(1)}, f32[192,128]{1,0:T(8,128)S(1)}, u32[]{:S(2)}, u32[]{:S(2)}) collective-permute-start(f32[192,128]{1,0:T(8,128)S(1)} %bitcast.51), channel_id=1, source_target_pairs={{0,4},{4,8},{8,12},{12,16},{16,20},{20,24},{24,28},{1,5},{5,9},{9,... | collective-permute-start | bytes 294920 | tf_op jit(solution)/shard_map/ppermute | solution.py:433
  15.1 1.9 %collective-permute-start.1 = (f32[192,128]{1,0:T(8,128)S(1)}, f32[192,128]{1,0:T(8,128)S(1)}, u32[]{:S(2)}, u32[]{:S(2)}) collective-permute-start(f32[192,128]{1,0:T(8,128)S(1)} %bitcast.50), channel_id=1, source_target_pairs={{4,0},{8,4},{12,8},{16,12},{20,16},{24,20},{28,24},{5,1},{9,5},{13... | collective-permute-start | bytes 294920 | tf_op jit(solution)/shard_map/ppermute | solution.py:433
  17.0 0.1 fusion
  17.1 5.7 %collective-permute-done.vx_low_ref = f32[192,128]{1,0:T(8,128)S(1)} collective-permute-done((f32[192,128]{1,0:T(8,128)S(1)}, f32[192,128]{1,0:T(8,128)S(1)}, u32[]{:S(2)}, u32[]{:S(2)}) %collective-permute-start) | collective-permute-done | bytes 98336 | tf_op jit(solution)/shard_map/ppermute | solution.py:433
  22.8 2.8 %collective-permute-done.1.vx_high_ref = f32[192,128]{1,0:T(8,128)S(1)} collective-permute-done((f32[192,128]{1,0:T(8,128)S(1)}, f32[192,128]{1,0:T(8,128)S(1)}, u32[]{:S(2)}, u32[]{:S(2)}) %collective-permute-start.1) | collective-permute-done | bytes 98336 | tf_op jit(solution)/shard_map/ppermute | solution.py:433
  25.6 2.1 %collective-permute-start.2 = (f32[144,128]{1,0:T(8,128)S(1)}, f32[144,128]{1,0:T(8,128)S(1)}, u32[]{:S(2)}, u32[]{:S(2)}) collective-permute-start(f32[144,128]{1,0:T(8,128)S(1)} %bitcast.52), channel_id=1, source_target_pairs={{0,1},{1,2},{2,3},{4,5},{5,6},{6,7},{8,9},{9,10},{10,11},{12,13},{... | collective-permute-start | bytes 221192 | tf_op jit(solution)/shard_map/ppermute | solution.py:433
  27.8 1.3 %collective-permute-start.3 = (f32[144,128]{1,0:T(8,128)S(1)}, f32[144,128]{1,0:T(8,128)S(1)}, u32[]{:S(2)}, u32[]{:S(2)}) collective-permute-start(f32[144,128]{1,0:T(8,128)S(1)} %bitcast.53), channel_id=1, source_target_pairs={{1,0},{2,1},{3,2},{5,4},{6,5},{7,6},{9,8},{10,9},{11,10},{13,12},{... | collective-permute-start | bytes 221192 | tf_op jit(solution)/shard_map/ppermute | solution.py:433
  29.1 9.9 %collective-permute-done.2.vy_low_ref = f32[144,128]{1,0:T(8,128)S(1)} collective-permute-done((f32[144,128]{1,0:T(8,128)S(1)}, f32[144,128]{1,0:T(8,128)S(1)}, u32[]{:S(2)}, u32[]{:S(2)}) %collective-permute-start.2) | collective-permute-done | bytes 73760 | tf_op jit(solution)/shard_map/ppermute | solution.py:433
  39.0 0.0 collective-permute-done.3.vy_high_ref
  39.0 10.3 %all-to-all-done = f32[3104,1,128]{2,1,0:T(1,128)S(1)} async-done(((f32[3104,1,128]{2,1,0:T(1,128)}), f32[3104,1,128]{2,1,0:T(1,128)S(1)}, u32[]{:S(2)}, u32[]{:S(2)}) %all-to-all-start) | async-done | bytes 1589280 | tf_op jit(solution)/shard_map/all_to_all | solution.py:477
  49.2 0.0 copy-done.1
  49.2 2.0 %average.1 = (f32[512,128]{1,0:T(8,128)}, f32[512,128]{1,0:T(8,128)}, f32[512,128]{1,0:T(8,128)S(1)}, f32[512,128]{1,0:T(8,128)S(1)}, f32[96,128]{1,0:T(8,128)S(...) custom-call(f32[3104,128]{1,0:T(8,128)S(1)} %bitcast.40, f32[512,128]{1,0:T(8,128)S(1)} %bitcast.42), custom_call_target="tpu_custom_call" | custom-call | tf_op jit(solution)/shard_map/average/pallas_call | solution.py:502
  51.2 1.9 %collective-permute-start.4 = (f32[96,128]{1,0:T(8,128)S(1)}, f32[96,128]{1,0:T(8,128)S(1)}, u32[]{:S(2)}, u32[]{:S(2)}) collective-permute-start(f32[96,128]{1,0:T(8,128)S(1)} %get-tuple-element.27), channel_id=1, source_target_pairs={{0,4},{4,8},{8,12},{12,16},{16,20},{20,24},{24,28},{1,5},{5,9},{9,... | collective-permute-start | bytes 147464 | tf_op jit(solution)/shard_map/ppermute | solution.py:433
  53.2 2.4 %collective-permute-start.5 = (f32[96,128]{1,0:T(8,128)S(1)}, f32[96,128]{1,0:T(8,128)S(1)}, u32[]{:S(2)}, u32[]{:S(2)}) collective-permute-start(f32[96,128]{1,0:T(8,128)S(1)} %get-tuple-element.28), channel_id=1, source_target_pairs={{4,0},{8,4},{12,8},{16,12},{20,16},{24,20},{28,24},{5,1},{9,5},{13... | collective-permute-start | bytes 147464 | tf_op jit(solution)/shard_map/ppermute | solution.py:433
  55.6 0.0 collective-permute-done.4.x_low_ref
  55.6 3.9 %collective-permute-done.5.x_high_ref = f32[96,128]{1,0:T(8,128)S(1)} collective-permute-done((f32[96,128]{1,0:T(8,128)S(1)}, f32[96,128]{1,0:T(8,128)S(1)}, u32[]{:S(2)}, u32[]{:S(2)}) %collective-permute-start.5) | collective-permute-done | bytes 49184 | tf_op jit(solution)/shard_map/ppermute | solution.py:433
  59.5 5.2 %collective-permute-start.6 = (f32[64,128]{1,0:T(8,128)S(1)}, f32[64,128]{1,0:T(8,128)S(1)}, u32[]{:S(2)}, u32[]{:S(2)}) collective-permute-start(f32[64,128]{1,0:T(8,128)S(1)} %get-tuple-element.31), channel_id=1, source_target_pairs={{0,1},{1,2},{2,3},{4,5},{5,6},{6,7},{8,9},{9,10},{10,11},{12,13},{... | collective-permute-start | bytes 98312 | tf_op jit(solution)/shard_map/ppermute | solution.py:433
  64.7 1.3 %collective-permute-start.7 = (f32[64,128]{1,0:T(8,128)S(1)}, f32[64,128]{1,0:T(8,128)S(1)}, u32[]{:S(2)}, u32[]{:S(2)}) collective-permute-start(f32[64,128]{1,0:T(8,128)S(1)} %get-tuple-element.32), channel_id=1, source_target_pairs={{1,0},{2,1},{3,2},{5,4},{6,5},{7,6},{9,8},{10,9},{11,10},{13,12},{... | collective-permute-start | bytes 98312 | tf_op jit(solution)/shard_map/ppermute | solution.py:433
  66.0 0.0 collective-permute-done.6.y_low_ref
  66.0 3.3 %collective-permute-done.7.y_high_ref = f32[64,128]{1,0:T(8,128)S(1)} collective-permute-done((f32[64,128]{1,0:T(8,128)S(1)}, f32[64,128]{1,0:T(8,128)S(1)}, u32[]{:S(2)}, u32[]{:S(2)}) %collective-permute-start.7) | collective-permute-done | bytes 32800 | tf_op jit(solution)/shard_map/ppermute | solution.py:433
  69.3 2.3 %smooth.1 = f32[1536,128]{1,0:T(8,128)} custom-call(f32[512,128]{1,0:T(8,128)S(1)} %get-tuple-element.21.visc_ref, f32[512,128]{1,0:T(8,128)S(1)} %get-tuple-element.22.force_ref, f32[1536,128]{1,0:T(8,128)S(1)} %bitcast.41, f32[192,128]{1,0:T(8,128)S(1)} %collective-permute-done.vx_low_ref, f32[192,128]{1,0:T(8,128)S(1)} %collective-permute-done.1.vx_high_ref, ...), custom_call_target="tpu_custom_call" | custom-call | tf_op jit(solution)/shard_map/smooth/pallas_call | solution.py:527
  (7 shorter events, 0.1 us)
Async XLA Ops:
  5.3 6.5 %copy-start = (f32[3,16,32,128]{3,2,1,0:T(8,128)S(1)}, f32[3,16,32,128]{3,2,1,0:T(8,128)}, u32[]{:S(2)}) copy-start(f32[3,16,32,128]{3,2,1,0:T(8,128)} %param.13) | copy-start | bytes 2359300
  5.3 44.0 %copy-start.1 = (f32[16,32,128]{2,1,0:T(8,128)S(1)}, f32[16,32,128]{2,1,0:T(8,128)}, u32[]{:S(2)}) copy-start(f32[16,32,128]{2,1,0:T(8,128)} %param.12) | copy-start | bytes 786436
  5.3 44.0 %all-to-all-start = ((f32[3104,1,128]{2,1,0:T(1,128)}), f32[3104,1,128]{2,1,0:T(1,128)S(1)}, u32[]{:S(2)}, u32[]{:S(2)}) async-start(f32[3104,1,128]{2,1,0:T(1,128)} %bitcast.2), calls=%async_computation | async-start | bytes 3178496 | tf_op jit(solution)/shard_map/all_to_all | solution.py:477
  11.8 11.1 %collective-permute-start = (f32[192,128]{1,0:T(8,128)S(1)}, f32[192,128]{1,0:T(8,128)S(1)}, u32[]{:S(2)}, u32[]{:S(2)}) collective-permute-start(f32[192,128]{1,0:T(8,128)S(1)} %bitcast.51), channel_id=1, source_target_pairs={{0,4},{4,8},{8,12},{12,16},{16,20},{20,24},{24,28},{1,5},{5,9},{9,... | collective-permute-start | bytes 294920 | tf_op jit(solution)/shard_map/ppermute | solution.py:433
  15.1 10.5 %collective-permute-start.1 = (f32[192,128]{1,0:T(8,128)S(1)}, f32[192,128]{1,0:T(8,128)S(1)}, u32[]{:S(2)}, u32[]{:S(2)}) collective-permute-start(f32[192,128]{1,0:T(8,128)S(1)} %bitcast.50), channel_id=1, source_target_pairs={{4,0},{8,4},{12,8},{16,12},{20,16},{24,20},{28,24},{5,1},{9,5},{13... | collective-permute-start | bytes 294920 | tf_op jit(solution)/shard_map/ppermute | solution.py:433
  25.6 13.3 %collective-permute-start.2 = (f32[144,128]{1,0:T(8,128)S(1)}, f32[144,128]{1,0:T(8,128)S(1)}, u32[]{:S(2)}, u32[]{:S(2)}) collective-permute-start(f32[144,128]{1,0:T(8,128)S(1)} %bitcast.52), channel_id=1, source_target_pairs={{0,1},{1,2},{2,3},{4,5},{5,6},{6,7},{8,9},{9,10},{10,11},{12,13},{... | collective-permute-start | bytes 221192 | tf_op jit(solution)/shard_map/ppermute | solution.py:433
  27.8 11.2 %collective-permute-start.3 = (f32[144,128]{1,0:T(8,128)S(1)}, f32[144,128]{1,0:T(8,128)S(1)}, u32[]{:S(2)}, u32[]{:S(2)}) collective-permute-start(f32[144,128]{1,0:T(8,128)S(1)} %bitcast.53), channel_id=1, source_target_pairs={{1,0},{2,1},{3,2},{5,4},{6,5},{7,6},{9,8},{10,9},{11,10},{13,12},{... | collective-permute-start | bytes 221192 | tf_op jit(solution)/shard_map/ppermute | solution.py:433
  51.2 4.3 %collective-permute-start.4 = (f32[96,128]{1,0:T(8,128)S(1)}, f32[96,128]{1,0:T(8,128)S(1)}, u32[]{:S(2)}, u32[]{:S(2)}) collective-permute-start(f32[96,128]{1,0:T(8,128)S(1)} %get-tuple-element.27), channel_id=1, source_target_pairs={{0,4},{4,8},{8,12},{12,16},{16,20},{20,24},{24,28},{1,5},{5,9},{9,... | collective-permute-start | bytes 147464 | tf_op jit(solution)/shard_map/ppermute | solution.py:433
  53.2 6.3 %collective-permute-start.5 = (f32[96,128]{1,0:T(8,128)S(1)}, f32[96,128]{1,0:T(8,128)S(1)}, u32[]{:S(2)}, u32[]{:S(2)}) collective-permute-start(f32[96,128]{1,0:T(8,128)S(1)} %get-tuple-element.28), channel_id=1, source_target_pairs={{4,0},{8,4},{12,8},{16,12},{20,16},{24,20},{28,24},{5,1},{9,5},{13... | collective-permute-start | bytes 147464 | tf_op jit(solution)/shard_map/ppermute | solution.py:433
  59.5 6.5 %collective-permute-start.6 = (f32[64,128]{1,0:T(8,128)S(1)}, f32[64,128]{1,0:T(8,128)S(1)}, u32[]{:S(2)}, u32[]{:S(2)}) collective-permute-start(f32[64,128]{1,0:T(8,128)S(1)} %get-tuple-element.31), channel_id=1, source_target_pairs={{0,1},{1,2},{2,3},{4,5},{5,6},{6,7},{8,9},{9,10},{10,11},{12,13},{... | collective-permute-start | bytes 98312 | tf_op jit(solution)/shard_map/ppermute | solution.py:433
  64.7 4.7 %collective-permute-start.7 = (f32[64,128]{1,0:T(8,128)S(1)}, f32[64,128]{1,0:T(8,128)S(1)}, u32[]{:S(2)}, u32[]{:S(2)}) collective-permute-start(f32[64,128]{1,0:T(8,128)S(1)} %get-tuple-element.32), channel_id=1, source_target_pairs={{1,0},{2,1},{3,2},{5,4},{6,5},{7,6},{9,8},{10,9},{11,10},{13,12},{... | collective-permute-start | bytes 98312 | tf_op jit(solution)/shard_map/ppermute | solution.py:433

commit v3 on v2

--- a/solution.py
+++ b/solution.py
@@ -188,6 +188,10 @@
     place(steps - 1)
 
 
+def parities():
+    return lax.axis_index("gx") & 1, lax.axis_index("gy") & 1
+
+
 def average_kernel(
     slots,
     chunk,
@@ -198,10 +202,10 @@
     density_ref,
     visc_ref,
     force_ref,
-    x_low_ref,
-    x_high_ref,
-    y_low_ref,
-    y_high_ref,
+    x_even_ref,
+    x_odd_ref,
+    y_even_ref,
+    y_odd_ref,
     hot_ref,
     value_ref,
 ):
@@ -245,17 +249,19 @@
         density_ref[span, :] = density
         visc_ref[span, :] = jnp.exp(logvisc)
         force_ref[span, :] = GRAVITY * (1.0 - density)
-    near = size_y
-    x_low_ref[0 : 2 * near, :] = visc_ref[0 : 2 * near, :]
-    x_low_ref[2 * near : 3 * near, :] = force_ref[0:near, :]
-    x_high_ref[0 : 2 * near, :] = visc_ref[columns - 2 * near : columns, :]
-    x_high_ref[2 * near : 3 * near, :] = force_ref[columns - near : columns, :]
-    y_low_ref[...] = jnp.zeros_like(y_low_ref)
-    y_high_ref[...] = jnp.zeros_like(y_high_ref)
-    for ref, first, second in ((y_low_ref, 0, 1), (y_high_ref, size_y - 1, size_y - 2)):
-        ref[NEAR : NEAR + size_x, :] = visc_ref[pl.ds(first, size_x, stride=size_y), :]
-        ref[FAR : FAR + size_x, :] = visc_ref[pl.ds(second, size_x, stride=size_y), :]
-        ref[LINE : LINE + size_x, :] = force_ref[pl.ds(first, size_x, stride=size_y), :]
+    odd_x, odd_y = parities()
+    for ref, first in ((x_even_ref, odd_x == 1), (x_odd_ref, odd_x == 0)):
+        start = jnp.where(first, 0, columns - 2 * size_y)
+        ref[0 : 2 * size_y, :] = visc_ref[pl.ds(pl.multiple_of(start, 8), 2 * size_y), :]
+        start = jnp.where(first, 0, columns - size_y)
+        ref[2 * size_y :, :] = force_ref[pl.ds(pl.multiple_of(start, 8), size_y), :]
+    for ref, first in ((y_even_ref, odd_y == 1), (y_odd_ref, odd_y == 0)):
+        near = jnp.where(first, 0, size_y - 1)
+        far = jnp.where(first, 1, size_y - 2)
+        ref[...] = jnp.zeros_like(ref)
+        ref[NEAR : NEAR + size_x, :] = visc_ref[pl.ds(near, size_x, stride=size_y), :]
+        ref[FAR : FAR + size_x, :] = visc_ref[pl.ds(far, size_x, stride=size_y), :]
+        ref[LINE : LINE + size_x, :] = force_ref[pl.ds(near, size_x, stride=size_y), :]
 
 
 def smooth_kernel(
@@ -267,10 +273,10 @@
     vx_high_ref,
     vy_low_ref,
     vy_high_ref,
-    x_low_ref,
-    x_high_ref,
-    y_low_ref,
-    y_high_ref,
+    x_even_ref,
+    x_odd_ref,
+    y_even_ref,
+    y_odd_ref,
     out_ref,
     wide_visc,
     wide_vel,
@@ -282,40 +288,42 @@
     pitch = size_y + 16
     lanes = lax.broadcasted_iota(jnp.int32, (1, depth), 1)
 
-    def place(ref, offset, core, low, high, near_low, near_high):
-        for plane in range(2):
-            ref[pl.ds(offset + plane * pitch + 8, size_y), :] = low(plane)
-            ref[pl.ds(offset + (size_x + 2 + plane) * pitch + 8, size_y), :] = high(plane)
-        for plane in range(size_x):
-            ref[pl.ds(offset + (plane + 2) * pitch + 8, size_y), :] = core(plane)
-        planes = size_x + 2
-        ref[pl.ds(offset + pitch + 7, planes, stride=pitch), :] = near_low
-        ref[pl.ds(offset + pitch + 8 + size_y, planes, stride=pitch), :] = near_high
-
-    def block(ref, first, count):
-        return ref[pl.ds(first, count), :]
-
-    place(
-        wide_visc,
-        0,
-        lambda p: block(visc_ref, p * size_y, size_y),
-        lambda p: block(x_low_ref, p * size_y, size_y),
-        lambda p: block(x_high_ref, p * size_y, size_y),
-        block(y_low_ref, NEAR - 1, size_x + 2),
-        block(y_high_ref, NEAR - 1, size_x + 2),
-    )
     field = (size_x + 4) * pitch
     field_next = (size_x + 2) * pitch
+    odd_x, odd_y = parities()
+
+    def x_side(is_low):
+        return jnp.where(is_low, -1, size_x)
+
+    def y_row(is_low):
+        return jnp.where(is_low, 7, 8 + size_y)
+
+    def place(ref, offset, source, first):
+        for plane in range(size_x):
+            at = offset + (plane + 2) * pitch + 8
+            ref[pl.ds(at, size_y), :] = source[pl.ds(first + plane * size_y, size_y), :]
+
+    def place_x(ref, offset, source, first, is_low):
+        base = offset + jnp.where(is_low, 0, (size_x + 2) * pitch) + 8
+        for plane in range(2):
+            at = pl.multiple_of(base + plane * pitch, 8)
+            ref[pl.ds(at, size_y), :] = source[pl.ds(first + plane * size_y, size_y), :]
+
+    def place_y(ref, offset, source, first, row):
+        span = pl.ds(offset + pitch + row, size_x + 2, stride=pitch)
+        ref[span, :] = source[pl.ds(first + NEAR - 1, size_x + 2), :]
+
+    place(wide_visc, 0, visc_ref, 0)
+    place_x(wide_visc, 0, x_even_ref, 0, odd_x == 1)
+    place_x(wide_visc, 0, x_odd_ref, 0, odd_x == 0)
+    place_y(wide_visc, 0, y_even_ref, 0, y_row(odd_y == 1))
+    place_y(wide_visc, 0, y_odd_ref, 0, y_row(odd_y == 0))
     for c in range(3):
-        place(
-            wide_vel,
-            c * field,
-            lambda p: block(vel_ref, c * cells + p * size_y, size_y),
-            lambda p: block(vx_low_ref, (2 * c + p) * size_y, size_y),
-            lambda p: block(vx_high_ref, (2 * c + p) * size_y, size_y),
-            block(vy_low_ref, c * LINE + NEAR - 1, size_x + 2),
-            block(vy_high_ref, c * LINE + NEAR - 1, size_x + 2),
-        )
+        place(wide_vel, c * field, vel_ref, c * cells)
+        place_x(wide_vel, c * field, vx_low_ref, 2 * c * size_y, True)
+        place_x(wide_vel, c * field, vx_high_ref, 2 * c * size_y, False)
+        place_y(wide_vel, c * field, vy_low_ref, c * LINE, 7)
+        place_y(wide_vel, c * field, vy_high_ref, c * LINE, 8 + size_y)
 
     def factors(visc, beside, force):
         up = jnp.where(lanes == depth - 1, 0.0, pltpu.roll(visc, depth - 1, 1))
@@ -345,7 +353,7 @@
         )
 
     def first_sweep(plane, force):
-        at = (plane + 2) * pitch + 8
+        at = pl.multiple_of((plane + 2) * pitch + 8, 8)
         faces, push = factors(wide_visc[pl.ds(at, size_y), :], around(wide_visc, at), force)
         results = []
         for c in range(3):
@@ -356,41 +364,52 @@
 
     def put(plane, results):
         for c in range(3):
-            at = c * field_next + (plane + 1) * pitch + 8
+            at = pl.multiple_of(c * field_next + (plane + 1) * pitch + 8, 8)
             wide_next[pl.ds(at, size_y), :] = results[c]
 
-    for plane, ref in ((-1, x_low_ref), (size_x, x_high_ref)):
+    for plane, ref in ((x_side(odd_x == 1), x_even_ref), (x_side(odd_x == 0), x_odd_ref)):
         _, _, results = first_sweep(plane, ref[pl.ds(2 * size_y, size_y), :])
-        inside = wide_visc[pl.ds((plane + 2) * pitch + 8, size_y), :] > 0.0
+        inside = ref[pl.ds(jnp.where(plane < 0, size_y, 0), size_y), :] > 0.0
         put(plane, [jnp.where(inside, value, 0.0) for value in results])
 
-    for row, near_row, visc_lines, vel_lines in (
-        (7, 0, y_low_ref, vy_low_ref),
-        (8 + size_y, size_y - 1, y_high_ref, vy_high_ref),
+    def y_lines(is_low, ref):
+        near = jnp.where(is_low, 0, size_y - 1)
+        return y_row(is_low), near, is_low, ref
+
+    for row, near_row, is_low, visc_lines in (
+        y_lines(odd_y == 1, y_even_ref),
+        y_lines(odd_y == 0, y_odd_ref),
     ):
 
-        def around_line(ref, first, inner):
+        def vel_line(first, count):
+            span = pl.ds(first, count)
+            return jnp.where(is_low, vy_low_ref[span, :], vy_high_ref[span, :])
+
+        def visc_line(first, count):
+            return visc_lines[pl.ds(first, count), :]
+
+        def around_line(line, first, inner):
             return (
-                ref[pl.ds(first + NEAR + 1, size_x), :],
-                ref[pl.ds(first + NEAR - 1, size_x), :],
+                line(first + NEAR + 1, size_x),
+                line(first + NEAR - 1, size_x),
                 inner,
-                ref[pl.ds(first + FAR, size_x), :],
+                line(first + FAR, size_x),
             )
 
         inner = visc_ref[pl.ds(near_row, size_x, stride=size_y), :]
-        visc = visc_lines[pl.ds(NEAR, size_x), :]
+        visc = visc_line(NEAR, size_x)
         faces, push = factors(
             visc,
-            around_line(visc_lines, 0, inner),
-            visc_lines[pl.ds(LINE, size_x), :],
+            around_line(visc_line, 0, inner),
+            visc_line(LINE, size_x),
         )
         for c in range(3):
             inner = vel_ref[pl.ds(c * cells + near_row, size_x, stride=size_y), :]
             value = relax(
                 faces,
                 push if c == 2 else None,
-                vel_lines[pl.ds(c * LINE + NEAR, size_x), :],
-                around_line(vel_lines, c * LINE, inner),
+                vel_line(c * LINE + NEAR, size_x),
+                around_line(vel_line, c * LINE, inner),
             )
             value = jnp.where(visc > 0.0, value, 0.0)
             at = c * field_next + pitch + row
@@ -412,11 +431,18 @@
             out_ref[pl.ds(c * cells + plane * size_y, size_y), :] = value
 
 
-def corner_kernel(bricks, first_in, last_in, x_low_ref, x_high_ref, first_ref, last_ref):
+def corner_kernel(
+    bricks, even_in, odd_in, x_even_ref, x_odd_ref, y_even_ref, y_odd_ref
+):
     size_x, size_y = bricks
-    for ref, near in ((first_ref, 0), (last_ref, size_y - 1)):
-        ref[NEAR - 1 : NEAR, :] = x_low_ref[size_y + near : size_y + near + 1, :]
-        ref[NEAR + size_x : NEAR + size_x + 1, :] = x_high_ref[near : near + 1, :]
+    odd_x, odd_y = parities()
+    swapped = odd_x == 1
+    for ref, first in ((y_even_ref, odd_y == 1), (y_odd_ref, odd_y == 0)):
+        near = jnp.where(first, 0, size_y - 1)
+        low, high = pl.ds(size_y + near, 1), pl.ds(near, 1)
+        ref[NEAR - 1 : NEAR, :] = jnp.where(swapped, x_even_ref[low, :], x_odd_ref[low, :])
+        high = jnp.where(swapped, x_odd_ref[high, :], x_even_ref[high, :])
+        ref[NEAR + size_x : NEAR + size_x + 1, :] = high
 
 
 def limit(mebibytes):
@@ -431,6 +457,12 @@
     count = lax.axis_size(axis)
     pairs = [(i, i + step) for i in range(count) if 0 <= i + step < count]
     return lax.ppermute(value, axis, pairs)
+
+
+def swapped(value, axis, first):
+    count = lax.axis_size(axis)
+    pairs = [(i, i + 1) for i in range(first, count - 1, 2)]
+    return lax.ppermute(value, axis, pairs + [(b, a) for a, b in pairs])
 
 
 def per_device(
@@ -499,7 +531,7 @@
     field = jax.ShapeDtypeStruct((columns, depth), F32)
     x_side = jax.ShapeDtypeStruct((3 * size_y, depth), F32)
     y_side = jax.ShapeDtypeStruct((LINE + size_x, depth), F32)
-    logvisc, density, visc, force, x_first, x_last, y_first, y_last = pl.pallas_call(
+    logvisc, density, visc, force, x_even, x_odd, y_even, y_odd = pl.pallas_call(
         functools.partial(average_kernel, slots, chunk, (size_x, size_y)),
         out_shape=(field, field, field, field, x_side, x_side, y_side, y_side),
         in_specs=[VMEM, VMEM],
@@ -509,9 +541,9 @@
         name="average",
     )(received, old_logvisc.reshape(columns, depth))
 
-    x_low = shifted(x_last, "gx", 1)
-    x_high = shifted(x_first, "gx", -1)
-    y_first, y_last = pl.pallas_call(
+    x_even = swapped(x_even, "gx", 0)
+    x_odd = swapped(x_odd, "gx", 1)
+    y_even, y_odd = pl.pallas_call(
         functools.partial(corner_kernel, (size_x, size_y)),
         out_shape=(y_side, y_side),
         in_specs=[VMEM] * 4,
@@ -519,9 +551,9 @@
         input_output_aliases={0: 0, 1: 1},
         compiler_params=limit(4),
         name="corners",
-    )(y_first, y_last, x_low, x_high)
-    y_low = shifted(y_last, "gy", 1)
-    y_high = shifted(y_first, "gy", -1)
+    )(y_even, y_odd, x_even, x_odd)
+    y_even = swapped(y_even, "gy", 0)
+    y_odd = swapped(y_odd, "gy", 1)
 
     pitch = size_y + 16
     smoothed = pl.pallas_call(
@@ -545,10 +577,10 @@
         vx_high,
         vy_low,
         vy_high,
-        x_low,
-        x_high,
-        y_low,
-        y_high,
+        x_even,
+        x_odd,
+        y_even,
+        y_odd,
     )
     return (
         logvisc.reshape(old_logvisc.shape),

time: 72 us -> 66.5 us (0.924)
  the two profiles are of different devices: /device:TPU:3 before, /device:TPU:12 now
where the time goes in v3:
time: 66.5 us; the launch traced here: 66.2 us
  waiting for transfers between devices  32 us (48%)
  starting transfers between devices  24.4 us (37%)
  Pallas kernels  8.93 us (13%)
  between operations  0.78 us (1%)
    ppermute x4, waiting for transfers between devices, shifted(): return lax.ppermute(value, axis, pairs)  25.7 us
    ppermute x4, starting transfers between devices, shifted(): return lax.ppermute(value, axis, pairs)  12.3 us
    ppermute x4, waiting for transfers between devices, swapped(): return lax.ppermute(value, axis, pairs + [(b, a) for a, b in pairs])  6.31 us
    ppermute x4, starting transfers between devices, swapped(): return lax.ppermute(value, axis, pairs + [(b, a) for a, b in pairs])  6.08 us
    all_to_all x1, starting transfers between devices, per_device(): lax.all_to_all(payload, BOTH, split_axis=0, concat_axis=0, tiled=True)  6 us
    pallas_call x1, Pallas kernels, per_device(): pl.pallas_call(functools.partial(pack_kernel, slots, chunk), out_shape=ja...  4.61 us
    pallas_call x1, Pallas kernels, per_device(): pl.pallas_call(functools.partial(smooth_kernel, (size_x, size_y)), out_sh...  2.29 us
    pallas_call x1, Pallas kernels, per_device(): pl.pallas_call(functools.partial(average_kernel, slots, chunk, (size_x, s...  2.03 us
  transfers between devices with their start and end apart: 9, of which 6 were waited for; matrix products, arithmetic and copies ran while one was open for 0% of the time, Pallas kernels for 0%

profile of v3, /device:TPU:12, one launch (start us, length us, event | category | flops | bytes accessed | tf_op | source)
XLA Modules:
  0.0 66.2 jit_solution(4165432202762979546)
XLA Ops:
  0.6 4.6 %pack.1 = f32[3104,128]{1,0:T(8,128)} custom-call(s32[4,128]{1,0:T(4,128)} %bitcast.54, f32[512,128]{1,0:T(8,128)} %comp_hbm.1, f32[512,128]{1,0:T(8,128)} %strain_hbm.1, s32[512,128]{1,0:T(8,128)} %live_hbm.1, s32[512,128]{1,0:T(8,128)} %cell_hbm.1), custom_call_target="tpu_custom_call" | custom-call | tf_op jit(solution)/shard_map/pack/pallas_call | solution.py:482
  5.2 0.0 copy-start
  5.3 0.0 copy-start.1
  5.3 6.0 %all-to-all-start = ((f32[3104,1,128]{2,1,0:T(1,128)}), f32[3104,1,128]{2,1,0:T(1,128)S(1)}, u32[]{:S(2)}, u32[]{:S(2)}) async-start(f32[3104,1,128]{2,1,0:T(1,128)} %bitcast.2), calls=%async_computation | async-start | bytes 3178496 | tf_op jit(solution)/shard_map/all_to_all | solution.py:509
  11.3 0.0 copy-done
  11.3 2.1 %collective-permute-start = (f32[192,128]{1,0:T(8,128)S(1)}, f32[192,128]{1,0:T(8,128)S(1)}, u32[]{:S(2)}, u32[]{:S(2)}) collective-permute-start(f32[192,128]{1,0:T(8,128)S(1)} %bitcast.51), channel_id=1, source_target_pairs={{0,4},{4,8},{8,12},{12,16},{16,20},{20,24},{24,28},{1,5},{5,9},{9,... | collective-permute-start | bytes 294920 | tf_op jit(solution)/shard_map/ppermute | solution.py:459
  13.4 4.4 %collective-permute-start.1 = (f32[192,128]{1,0:T(8,128)S(1)}, f32[192,128]{1,0:T(8,128)S(1)}, u32[]{:S(2)}, u32[]{:S(2)}) collective-permute-start(f32[192,128]{1,0:T(8,128)S(1)} %bitcast.50), channel_id=1, source_target_pairs={{4,0},{8,4},{12,8},{16,12},{20,16},{24,20},{28,24},{5,1},{9,5},{13... | collective-permute-start | bytes 294920 | tf_op jit(solution)/shard_map/ppermute | solution.py:459
  17.8 0.1 fusion
  17.9 7.2 %collective-permute-done.vx_low_ref = f32[192,128]{1,0:T(8,128)S(1)} collective-permute-done((f32[192,128]{1,0:T(8,128)S(1)}, f32[192,128]{1,0:T(8,128)S(1)}, u32[]{:S(2)}, u32[]{:S(2)}) %collective-permute-start) | collective-permute-done | bytes 98336 | tf_op jit(solution)/shard_map/ppermute | solution.py:459
  25.0 0.0 collective-permute-done.1.vx_high_ref
  25.1 1.9 %collective-permute-start.2 = (f32[144,128]{1,0:T(8,128)S(1)}, f32[144,128]{1,0:T(8,128)S(1)}, u32[]{:S(2)}, u32[]{:S(2)}) collective-permute-start(f32[144,128]{1,0:T(8,128)S(1)} %bitcast.52), channel_id=1, source_target_pairs={{0,1},{1,2},{2,3},{4,5},{5,6},{6,7},{8,9},{9,10},{10,11},{12,13},{... | collective-permute-start | bytes 221192 | tf_op jit(solution)/shard_map/ppermute | solution.py:459
  27.1 3.9 %collective-permute-start.3 = (f32[144,128]{1,0:T(8,128)S(1)}, f32[144,128]{1,0:T(8,128)S(1)}, u32[]{:S(2)}, u32[]{:S(2)}) collective-permute-start(f32[144,128]{1,0:T(8,128)S(1)} %bitcast.53), channel_id=1, source_target_pairs={{1,0},{2,1},{3,2},{5,4},{6,5},{7,6},{9,8},{10,9},{11,10},{13,12},{... | collective-permute-start | bytes 221192 | tf_op jit(solution)/shard_map/ppermute | solution.py:459
  31.0 16.6 %collective-permute-done.2.vy_low_ref = f32[144,128]{1,0:T(8,128)S(1)} collective-permute-done((f32[144,128]{1,0:T(8,128)S(1)}, f32[144,128]{1,0:T(8,128)S(1)}, u32[]{:S(2)}, u32[]{:S(2)}) %collective-permute-start.2) | collective-permute-done | bytes 73760 | tf_op jit(solution)/shard_map/ppermute | solution.py:459
  47.6 1.9 %collective-permute-done.3.vy_high_ref = f32[144,128]{1,0:T(8,128)S(1)} collective-permute-done((f32[144,128]{1,0:T(8,128)S(1)}, f32[144,128]{1,0:T(8,128)S(1)}, u32[]{:S(2)}, u32[]{:S(2)}) %collective-permute-start.3) | collective-permute-done | bytes 73760 | tf_op jit(solution)/shard_map/ppermute | solution.py:459
  49.5 0.0 all-to-all-done
  49.5 0.0 copy-done.1
  49.5 2.0 %average.1 = (f32[512,128]{1,0:T(8,128)}, f32[512,128]{1,0:T(8,128)}, f32[512,128]{1,0:T(8,128)S(1)}, f32[512,128]{1,0:T(8,128)S(1)}, f32[96,128]{1,0:T(8,128)S(...) custom-call(f32[3104,128]{1,0:T(8,128)S(1)} %bitcast.40, f32[512,128]{1,0:T(8,128)S(1)} %bitcast.42), custom_call_target="tpu_custom_call" | custom-call | tf_op jit(solution)/shard_map/average/pallas_call | solution.py:534
  51.5 0.0 collective-permute-start.4
  51.5 3.5 %collective-permute-start.5 = (f32[96,128]{1,0:T(8,128)S(1)}, f32[96,128]{1,0:T(8,128)S(1)}, u32[]{:S(2)}, u32[]{:S(2)}) collective-permute-start(f32[96,128]{1,0:T(8,128)S(1)} %get-tuple-element.28), channel_id=1, source_target_pairs={{4,8},{12,16},{20,24},{8,4},{16,12},{24,20},{5,9},{13,17},{21,25},... | collective-permute-start | bytes 147464 | tf_op jit(solution)/shard_map/ppermute | solution.py:465
  55.0 0.0 collective-permute-done.4.x_even_ref
  55.0 3.1 %collective-permute-done.5.x_odd_ref = f32[96,128]{1,0:T(8,128)S(1)} collective-permute-done((f32[96,128]{1,0:T(8,128)S(1)}, f32[96,128]{1,0:T(8,128)S(1)}, u32[]{:S(2)}, u32[]{:S(2)}) %collective-permute-start.5) | collective-permute-done | bytes 49184 | tf_op jit(solution)/shard_map/ppermute | solution.py:465
  58.1 0.0 collective-permute-start.6
  58.1 2.6 %collective-permute-start.7 = (f32[64,128]{1,0:T(8,128)S(1)}, f32[64,128]{1,0:T(8,128)S(1)}, u32[]{:S(2)}, u32[]{:S(2)}) collective-permute-start(f32[64,128]{1,0:T(8,128)S(1)} %get-tuple-element.32), channel_id=1, source_target_pairs={{1,2},{2,1},{5,6},{6,5},{9,10},{10,9},{13,14},{14,13},{17,18},{18,... | collective-permute-start | bytes 98312 | tf_op jit(solution)/shard_map/ppermute | solution.py:465
  60.8 1.3 %collective-permute-done.6.y_even_ref = f32[64,128]{1,0:T(8,128)S(1)} collective-permute-done((f32[64,128]{1,0:T(8,128)S(1)}, f32[64,128]{1,0:T(8,128)S(1)}, u32[]{:S(2)}, u32[]{:S(2)}) %collective-permute-start.6) | collective-permute-done | bytes 32800 | tf_op jit(solution)/shard_map/ppermute | solution.py:465
  62.0 1.9 %collective-permute-done.7.y_odd_ref = f32[64,128]{1,0:T(8,128)S(1)} collective-permute-done((f32[64,128]{1,0:T(8,128)S(1)}, f32[64,128]{1,0:T(8,128)S(1)}, u32[]{:S(2)}, u32[]{:S(2)}) %collective-permute-start.7) | collective-permute-done | bytes 32800 | tf_op jit(solution)/shard_map/ppermute | solution.py:465
  63.9 2.3 %smooth.1 = f32[1536,128]{1,0:T(8,128)} custom-call(f32[512,128]{1,0:T(8,128)S(1)} %get-tuple-element.21.visc_ref, f32[512,128]{1,0:T(8,128)S(1)} %get-tuple-element.22.force_ref, f32[1536,128]{1,0:T(8,128)S(1)} %bitcast.41, f32[192,128]{1,0:T(8,128)S(1)} %collective-permute-done.vx_low_ref, f32[192,128]{1,0:T(8,128)S(1)} %collective-permute-done.1.vx_high_ref, ...), custom_call_target="tpu_custom_call" | custom-call | tf_op jit(solution)/shard_map/smooth/pallas_call | solution.py:559
  (7 shorter events, 0.1 us)
Async XLA Ops:
  5.2 6.0 %copy-start = (f32[3,16,32,128]{3,2,1,0:T(8,128)S(1)}, f32[3,16,32,128]{3,2,1,0:T(8,128)}, u32[]{:S(2)}) copy-start(f32[3,16,32,128]{3,2,1,0:T(8,128)} %param.13) | copy-start | bytes 2359300
  5.3 44.2 %copy-start.1 = (f32[16,32,128]{2,1,0:T(8,128)S(1)}, f32[16,32,128]{2,1,0:T(8,128)}, u32[]{:S(2)}) copy-start(f32[16,32,128]{2,1,0:T(8,128)} %param.12) | copy-start | bytes 786436
  5.3 44.2 %all-to-all-start = ((f32[3104,1,128]{2,1,0:T(1,128)}), f32[3104,1,128]{2,1,0:T(1,128)S(1)}, u32[]{:S(2)}, u32[]{:S(2)}) async-start(f32[3104,1,128]{2,1,0:T(1,128)} %bitcast.2), calls=%async_computation | async-start | bytes 3178496 | tf_op jit(solution)/shard_map/all_to_all | solution.py:509
  11.3 13.7 %collective-permute-start = (f32[192,128]{1,0:T(8,128)S(1)}, f32[192,128]{1,0:T(8,128)S(1)}, u32[]{:S(2)}, u32[]{:S(2)}) collective-permute-start(f32[192,128]{1,0:T(8,128)S(1)} %bitcast.51), channel_id=1, source_target_pairs={{0,4},{4,8},{8,12},{12,16},{16,20},{20,24},{24,28},{1,5},{5,9},{9,... | collective-permute-start | bytes 294920 | tf_op jit(solution)/shard_map/ppermute | solution.py:459
  13.4 11.7 %collective-permute-start.1 = (f32[192,128]{1,0:T(8,128)S(1)}, f32[192,128]{1,0:T(8,128)S(1)}, u32[]{:S(2)}, u32[]{:S(2)}) collective-permute-start(f32[192,128]{1,0:T(8,128)S(1)} %bitcast.50), channel_id=1, source_target_pairs={{4,0},{8,4},{12,8},{16,12},{20,16},{24,20},{28,24},{5,1},{9,5},{13... | collective-permute-start | bytes 294920 | tf_op jit(solution)/shard_map/ppermute | solution.py:459
  25.1 22.4 %collective-permute-start.2 = (f32[144,128]{1,0:T(8,128)S(1)}, f32[144,128]{1,0:T(8,128)S(1)}, u32[]{:S(2)}, u32[]{:S(2)}) collective-permute-start(f32[144,128]{1,0:T(8,128)S(1)} %bitcast.52), channel_id=1, source_target_pairs={{0,1},{1,2},{2,3},{4,5},{5,6},{6,7},{8,9},{9,10},{10,11},{12,13},{... | collective-permute-start | bytes 221192 | tf_op jit(solution)/shard_map/ppermute | solution.py:459
  27.1 22.4 %collective-permute-start.3 = (f32[144,128]{1,0:T(8,128)S(1)}, f32[144,128]{1,0:T(8,128)S(1)}, u32[]{:S(2)}, u32[]{:S(2)}) collective-permute-start(f32[144,128]{1,0:T(8,128)S(1)} %bitcast.53), channel_id=1, source_target_pairs={{1,0},{2,1},{3,2},{5,4},{6,5},{7,6},{9,8},{10,9},{11,10},{13,12},{... | collective-permute-start | bytes 221192 | tf_op jit(solution)/shard_map/ppermute | solution.py:459
  51.5 3.5 %collective-permute-start.4 = (f32[96,128]{1,0:T(8,128)S(1)}, f32[96,128]{1,0:T(8,128)S(1)}, u32[]{:S(2)}, u32[]{:S(2)}) collective-permute-start(f32[96,128]{1,0:T(8,128)S(1)} %get-tuple-element.27), channel_id=1, source_target_pairs={{0,4},{8,12},{16,20},{24,28},{4,0},{12,8},{20,16},{28,24},{1,5},{9... | collective-permute-start | bytes 147464 | tf_op jit(solution)/shard_map/ppermute | solution.py:465
  51.5 6.6 %collective-permute-start.5 = (f32[96,128]{1,0:T(8,128)S(1)}, f32[96,128]{1,0:T(8,128)S(1)}, u32[]{:S(2)}, u32[]{:S(2)}) collective-permute-start(f32[96,128]{1,0:T(8,128)S(1)} %get-tuple-element.28), channel_id=1, source_target_pairs={{4,8},{12,16},{20,24},{8,4},{16,12},{24,20},{5,9},{13,17},{21,25},... | collective-permute-start | bytes 147464 | tf_op jit(solution)/shard_map/ppermute | solution.py:465
  58.1 3.9 %collective-permute-start.6 = (f32[64,128]{1,0:T(8,128)S(1)}, f32[64,128]{1,0:T(8,128)S(1)}, u32[]{:S(2)}, u32[]{:S(2)}) collective-permute-start(f32[64,128]{1,0:T(8,128)S(1)} %get-tuple-element.31), channel_id=1, source_target_pairs={{0,1},{2,3},{1,0},{3,2},{4,5},{6,7},{5,4},{7,6},{8,9},{10,11},{9,8... | collective-permute-start | bytes 98312 | tf_op jit(solution)/shard_map/ppermute | solution.py:465
  58.1 5.8 %collective-permute-start.7 = (f32[64,128]{1,0:T(8,128)S(1)}, f32[64,128]{1,0:T(8,128)S(1)}, u32[]{:S(2)}, u32[]{:S(2)}) collective-permute-start(f32[64,128]{1,0:T(8,128)S(1)} %get-tuple-element.32), channel_id=1, source_target_pairs={{1,2},{2,1},{5,6},{6,5},{9,10},{10,9},{13,14},{14,13},{17,18},{18,... | collective-permute-start | bytes 98312 | tf_op jit(solution)/shard_map/ppermute | solution.py:465

commit v4 on v3

v4 whole, which is shorter than its diff:
```python
import functools

import jax
import jax.numpy as jnp
from jax import lax
from jax.experimental import pallas as pl
from jax.experimental.pallas import tpu as pltpu
from jax.sharding import PartitionSpec as P

LOG_HIGH = 1.5
LOG_LOW = -1.0
WEAKENING = 1.0
DENSITY_JUMP = 0.4
SOFTENING = 0.1
GRAVITY = 10.0
RELAX = 0.8
BOTH = ("gx", "gy")
F32 = jnp.float32
BF16 = jnp.bfloat16
VMEM = pl.BlockSpec(memory_space=pltpu.VMEM)
SMEM = pl.BlockSpec(memory_space=pltpu.SMEM)
HBM = pl.BlockSpec(memory_space=pltpu.HBM)
BY_LANES = (((1,), (1,)), ((), ()))
WAYS = 4
BATCH = 32
CORNERS = 8


def split(values):
    high = values.astype(BF16).astype(F32)
    return high, values - high


def pack_kernel(
    slots,
    chunk,
    dest_hbm,
    comp_hbm,
    strain_hbm,
    live_hbm,
    cell_hbm,
    out_ref,
    place_ref,
    line_ref,
    sums_ref,
    place_sem,
    dest_ref,
    comp_ref,
    strain_ref,
    live_ref,
    cell_ref,
    load_sem,
):
    blocks, marks = comp_ref.shape
    devices = out_ref.shape[0] // chunk
    shift = marks.bit_length() - 1
    part = marks // WAYS
    low_bits = part.bit_length() - 1
    pairs = (
        (dest_hbm, dest_ref),
        (cell_hbm, cell_ref),
        (comp_hbm, comp_ref),
        (strain_hbm, strain_ref),
        (live_hbm, live_ref),
    )
    loads = [pltpu.make_async_copy(*pair, load_sem.at[k]) for k, pair in enumerate(pairs)]
    for load in loads:
        load.start()
    out_ref[...] = jnp.zeros_like(out_ref)
    loads[0].wait()
    loads[1].wait()

    owner_ids = lax.broadcasted_iota(jnp.int32, (devices, marks), 0)
    rank_ids = lax.broadcasted_iota(jnp.int32, (slots, marks), 0)
    square = (marks, marks)
    before = lax.broadcasted_iota(jnp.int32, square, 0) < lax.broadcasted_iota(jnp.int32, square, 1)
    before = jnp.where(before, 1.0, 0.0).astype(BF16)
    seen = jnp.zeros((devices, 1), F32)
    ids = jnp.zeros((devices, slots), F32)
    for k in range(blocks // marks):
        dest = dest_ref[k : k + 1, :]
        mine = owner_ids == dest
        hot = jnp.where(mine, 1.0, 0.0)
        earlier = jnp.dot(hot.astype(BF16), before, preferred_element_type=F32) + seen
        rank = jnp.sum(jnp.where(mine, earlier, 0.0), axis=0, keepdims=True).astype(jnp.int32)
        seen = seen + jnp.sum(hot, axis=1, keepdims=True)
        line_ref[k : k + 1, :] = dest * chunk + rank
        column = (cell_ref[k * marks : (k + 1) * marks, :] >> shift).astype(F32).T[0:1] + 1.0
        spot = jnp.where(rank_ids == rank, 1.0, 0.0).astype(BF16)
        for piece in split(column):
            weighted = jnp.where(mine, piece, 0.0).astype(BF16)
            ids = ids + lax.dot_general(weighted, spot, BY_LANES, preferred_element_type=F32)
    places = pltpu.make_async_copy(line_ref, place_ref, place_sem)
    places.start()
    ids = ids - 1.0
    for owner in range(devices):
        at = owner * chunk + 3 * slots
        out_ref[at : at + 1, 0:slots] = ids[owner : owner + 1, :]
    for load in loads[2:]:
        load.wait()

    fine_ids = lax.broadcasted_iota(jnp.int32, (part, marks), 0).astype(F32).astype(BF16)
    row_ids = lax.broadcasted_iota(jnp.int32, (8, marks), 0)
    lane_ids = lax.broadcasted_iota(jnp.int32, (8, marks), 1)
    halves = [row_ids < 4, row_ids >= 4]
    spans = [(lane_ids >> low_bits) == ((row_ids + w) & (WAYS - 1)) for w in range(WAYS)]

    def depth_sums(group):
        rows = pl.ds(pl.multiple_of(group * 8, 8), 8)
        comp = comp_ref[rows, :]
        strain = strain_ref[rows, :]
        weight = live_ref[rows, :].astype(F32)
        soften = strain / (1.0 + strain)
        logv = weight * (LOG_HIGH * comp + LOG_LOW * (1.0 - comp) - WEAKENING * soften)
        rho = weight * (1.0 + DENSITY_JUMP * comp - SOFTENING * soften)
        pieces = [*split(logv), *split(rho), weight]
        depth = cell_ref[rows, :] & (marks - 1)
        coarse = ((depth >> low_bits) - row_ids) & (WAYS - 1)
        fine = (depth & (part - 1)).astype(F32)
        left, right = [], []
        for half in halves:
            lines = []
            for w in range(WAYS):
                mask = (coarse == w) & half
                lines += [jnp.where(mask, piece, 0.0) for piece in pieces]
            left.append(jnp.concatenate(lines, axis=0).astype(BF16))
        for first in (0, 4):
            lines = []
            for b in range(first, first + 4):
                line = jnp.broadcast_to(fine[b : b + 1, :], (16, marks)).astype(BF16)
                line = jnp.concatenate([line] * (part // 16), axis=0)
                lines.append(jnp.where(fine_ids == line, BF16(1.0), BF16(0.0)))
            right.append(jnp.concatenate(lines, axis=0))
        sums = lax.dot_general(
            jnp.concatenate(left, axis=1),
            jnp.concatenate(right, axis=1),
            BY_LANES,
            preferred_element_type=F32,
        )

        def piece_sum(w, p):
            first = (w * len(pieces) + p) * 8
            return sums[first : first + 8]

        results = []
        for numbers in ((0, 1), (2, 3), (4,)):
            total = None
            for w in range(WAYS):
                value = piece_sum(w, numbers[0])
                if len(numbers) > 1:
                    value = value + piece_sum(w, numbers[1])
                if w:
                    value = pltpu.roll(value, part * w, 1)
                total = value if total is None else jnp.where(spans[w], value, total)
            results.append(total)
        return results

    def batch(step, g, f):
        first = (step & 1) * (24 * BATCH) + g * 24 + f * 8
        return pl.ds(pl.multiple_of(first, 8), 8)

    def put(step):
        for g in range(BATCH):
            for f, value in enumerate(depth_sums(step * BATCH + g)):
                sums_ref[batch(step, g, f), :] = value

    def place(step):
        for g in range(BATCH):
            group = step * BATCH + g
            values = [sums_ref[batch(step, g, f), :] for f in range(3)]
            for k in range(8):
                at = place_ref[group // 16, (group % 16) * 8 + k]
                for f in range(3):
                    out_ref[pl.ds(at + f * slots, 1), :] = values[f][k : k + 1]

    steps = blocks // 8 // BATCH
    put(0)
    places.wait()

    def step(i, carry):
        place(i - 1)
        put(i)
        return carry

    lax.fori_loop(1, steps, step, 0)
    place(steps - 1)


def parities():
    return lax.axis_index("gx") & 1, lax.axis_index("gy") & 1


def at_end(axis):
    place, last = lax.axis_index(axis), lax.axis_size(axis) - 1
    return (place == 0) | (place == last) if last % 2 else place == 0


def boundary_columns(size_x, size_y):
    return (
        (0, 2 * size_y, 1),
        ((size_x - 2) * size_y, 2 * size_y, 1),
        (0, size_x, size_y),
        (1, size_x, size_y),
        (size_y - 1, size_x, size_y),
        (size_y - 2, size_x, size_y),
    )


def averages(sums, depth, old):
    sum_logv = sums[:, 0:depth] + sums[:, depth : 2 * depth]
    sum_rho = sums[:, 2 * depth : 3 * depth] + sums[:, 3 * depth : 4 * depth]
    count = sums[:, 4 * depth : 5 * depth] + 1.0
    return (sum_logv + old) / count, (sum_rho + 1.0) / count


def edge_kernel(
    slots,
    chunk,
    bricks,
    recv_ref,
    old_ref,
    vy_low_ref,
    vy_high_ref,
    wide_in,
    x_even_ref,
    x_odd_ref,
    y_even_ref,
    y_odd_ref,
    value_ref,
    ids_ref,
    wide_ref,
    hot_ref,
    visc_ref,
    force_ref,
):
    size_x, size_y = bricks
    depth = old_ref.shape[1]
    total = value_ref.shape[0]
    per = depth // slots
    lanes = lax.broadcasted_iota(jnp.int32, (1, depth), 1)
    runs = boundary_columns(size_x, size_y)
    wide = Wide(bricks)
    for c in range(3):
        for ref, near, far in ((vy_low_ref, -1, -2), (vy_high_ref, size_y, size_y + 1)):
            for k, row in enumerate((near, far)):
                wide_ref[wide.line(c, row), :] = ref[pl.ds((2 * c + k) * size_x, size_x), :]
    names = []
    for first, count, stride in runs:
        names.append(lax.broadcasted_iota(jnp.int32, (count, depth), 0) * stride + first)
    names = jnp.concatenate(names, axis=0).astype(F32)
    for part in range(total // depth):
        span = slice(part * depth, (part + 1) * depth)
        ids = jnp.full((1, depth), -1.0, F32)
        for k in range(per):
            first = (part * per + k) * chunk
            line = recv_ref[first + 3 * slots : first + 3 * slots + 1, :]
            if k:
                line = pltpu.roll(line, k * slots, 1)
            ids = jnp.where((lanes >= k * slots) & (lanes < (k + 1) * slots), line, ids)
        ids_ref[part : part + 1, :] = ids
        hot_ref[:, span] = jnp.where(names == ids, 1.0, 0.0).astype(BF16)
        for v in range(3):
            lines = []
            for k in range(per):
                lines.append(recv_ref[pl.ds((part * per + k) * chunk + v * slots, slots), :])
            high, low = split(jnp.concatenate(lines, axis=0))
            value_ref[span, pl.ds(2 * v * depth, depth)] = high.astype(BF16)
            if v < 2:
                value_ref[span, pl.ds((2 * v + 1) * depth, depth)] = low.astype(BF16)
    sums = jnp.dot(hot_ref[...], value_ref[...], preferred_element_type=F32)
    old = []
    for first, count, stride in runs:
        old.append(old_ref[pl.ds(first, count, stride=stride) if stride > 1 else pl.ds(first, count), :])
    logvisc, density = averages(sums, depth, jnp.concatenate(old, axis=0))
    visc_ref[...] = jnp.exp(logvisc)
    force_ref[...] = GRAVITY * (1.0 - density)
    odd_x, odd_y = parities()
    for ref, is_first in ((y_even_ref, odd_y == 1), (y_odd_ref, odd_y == 0)):
        start = pl.multiple_of(jnp.where(is_first, 4 * size_y, 4 * size_y + 2 * size_x), 8)
        ref[0 : 2 * size_x, :] = visc_ref[pl.ds(start, 2 * size_x), :]
        ref[2 * size_x :, :] = force_ref[pl.ds(start, size_x), :]
    for ref, is_first in ((x_even_ref, odd_x == 1), (x_odd_ref, odd_x == 0)):
        start = pl.multiple_of(jnp.where(is_first, 0, 2 * size_y), 8)
        ref[0 : 2 * size_y, :] = visc_ref[pl.ds(start, 2 * size_y), :]
        start = pl.multiple_of(jnp.where(is_first, 0, 3 * size_y), 8)
        ref[2 * size_y : 3 * size_y, :] = force_ref[pl.ds(start, size_y), :]
        ref[3 * size_y :, :] = jnp.zeros((CORNERS, depth), F32)

    @pl.when(at_end("gx"))
    def _():
        x_odd_ref[...] = jnp.zeros_like(x_odd_ref)

    @pl.when(at_end("gy"))
    def _():
        y_odd_ref[...] = jnp.zeros_like(y_odd_ref)


def factors(visc, beside, force):
    depth = visc.shape[1]
    lanes = lax.broadcasted_iota(jnp.int32, (1, depth), 1)
    up = jnp.where(lanes == depth - 1, 0.0, pltpu.roll(visc, depth - 1, 1))
    down = jnp.where(lanes == 0, 0.0, pltpu.roll(visc, 1, 1))
    faces = [visc + other for other in (*beside, up, down)]
    total = ((faces[0] + faces[1]) + (faces[2] + faces[3])) + (faces[4] + faces[5])
    scale = RELAX / total
    faces = [face * scale for face in faces]
    faces[4] = jnp.where(lanes == depth - 1, 0.0, faces[4])
    faces[5] = jnp.where(lanes == 0, 0.0, faces[5])
    return faces, 2.0 * force * scale


def relax(faces, push, vel, beside):
    depth = vel.shape[1]
    up = pltpu.roll(vel, depth - 1, 1)
    down = pltpu.roll(vel, 1, 1)
    terms = [face * other for face, other in zip(faces, (*beside, up, down))]
    result = ((terms[0] + terms[1]) + (terms[2] + terms[3])) + (terms[4] + terms[5])
    result = result + (1.0 - RELAX) * vel
    return result if push is None else result + push


class Wide:
    def __init__(self, bricks):
        self.size_x, self.size_y = bricks
        self.pitch = self.size_y + 16
        self.cells = self.size_x * self.size_y
        self.field = (self.size_x + 4) * self.pitch

    def plane(self, field, plane, dx=0, dy=0, row=0, rows=None):
        at = field * self.field + (plane + 2 + dx) * self.pitch + 8 + row
        if dy == 0 and row == 0 and not isinstance(at, int):
            at = pl.multiple_of(at, 8)
        return pl.ds(at + dy, rows or self.size_y)

    def cell(self, field, plane, row):
        return pl.ds(field * self.field + (plane + 2) * self.pitch + 8 + row, 1)

    def line(self, field, row, dx=0):
        at = field * self.field + (2 + dx) * self.pitch + 8 + row
        return pl.ds(at, self.size_x, stride=self.pitch)

    def around(self, ref, field, plane, **tile):
        steps = ((1, 0), (-1, 0), (0, 1), (0, -1))
        return tuple(ref[self.plane(field, plane, dx=dx, dy=dy, **tile), :] for dx, dy in steps)

    def core(self, plane, field=0, row=0, rows=None):
        return pl.ds(field * self.cells + plane * self.size_y + row, rows or self.size_y)

    def first_sweep(self, visc_ref, vel_ref, plane, force, **tile):
        visc = visc_ref[self.plane(0, plane, **tile), :]
        faces, push = factors(visc, self.around(visc_ref, 0, plane, **tile), force)
        results = []
        for c in range(3):
            vel = vel_ref[self.plane(c, plane, **tile), :]
            beside = self.around(vel_ref, c, plane, **tile)
            results.append(relax(faces, push if c == 2 else None, vel, beside))
        return faces, push, results

    def around_line(self, ref, field, row):
        places = (
            self.line(field, row, dx=1),
            self.line(field, row, dx=-1),
            self.line(field, row + 1),
            self.line(field, row - 1),
        )
        return tuple(ref[place, :] for place in places)

    def first_ring(self, visc_ref, vel_ref, next_ref, plane, force, **tile):
        _, _, results = self.first_sweep(visc_ref, vel_ref, plane, force, **tile)
        inside = visc_ref[self.plane(0, plane, **tile), :] > 0.0
        for c in range(3):
            next_ref[self.plane(c, plane, **tile), :] = jnp.where(inside, results[c], 0.0)

    def first_core(self, visc_ref, vel_ref, force_ref, next_ref, coeff_ref, plane, **tile):
        force = force_ref[self.core(plane, **tile), :]
        faces, push, results = self.first_sweep(visc_ref, vel_ref, plane, force, **tile)
        for c in range(3):
            next_ref[self.plane(c, plane, **tile), :] = results[c]
        for k, value in enumerate((*faces, push)):
            coeff_ref[self.core(plane, k, **tile), :] = value

    def second_sweep(self, coeff_ref, next_ref, last_ref, plane, **tile):
        faces = [coeff_ref[self.core(plane, k, **tile), :] for k in range(6)]
        push = coeff_ref[self.core(plane, 6, **tile), :]
        for c in range(3):
            beside = self.around(next_ref, c, plane, **tile)
            vel = next_ref[self.plane(c, plane, **tile), :]
            value = relax(faces, push if c == 2 else None, vel, beside)
            last_ref[self.core(plane, c, **tile), :] = value


def widen_kernel(bricks, vel_ref, vx_low_ref, vx_high_ref, wide_ref):
    size_x = bricks[0]
    wide = Wide(bricks)
    for c in range(3):
        for plane in range(size_x):
            wide_ref[wide.plane(c, plane), :] = vel_ref[wide.core(plane, c), :]
        for plane in range(2):
            wide_ref[wide.plane(c, plane - 2), :] = vx_low_ref[wide.core(2 * c + plane), :]
            wide_ref[wide.plane(c, size_x + plane), :] = vx_high_ref[wide.core(2 * c + plane), :]


def interior_kernel(
    bricks,
    value_ref,
    ids_ref,
    old_ref,
    logvisc_ref,
    density_ref,
    force_ref,
    visc_ref,
    hot_ref,
):
    size_y = bricks[1]
    wide = Wide(bricks)
    columns, depth = old_ref.shape
    names = lax.broadcasted_iota(jnp.int32, (columns, depth), 0).astype(F32)
    for part in range(value_ref.shape[0] // depth):
        hot = jnp.where(names == ids_ref[part : part + 1, :], 1.0, 0.0)
        hot_ref[:, part * depth : (part + 1) * depth] = hot.astype(BF16)
    for tile in range(columns // depth):
        span = slice(tile * depth, (tile + 1) * depth)
        sums = jnp.dot(hot_ref[span, :], value_ref[...], preferred_element_type=F32)
        logvisc, density = averages(sums, depth, old_ref[span, :])
        visc = jnp.exp(logvisc)
        logvisc_ref[span, :] = logvisc
        density_ref[span, :] = density
        force_ref[span, :] = GRAVITY * (1.0 - density)
        for k in range(depth // size_y):
            plane = tile * (depth // size_y) + k
            visc_ref[wide.plane(0, plane), :] = visc[k * size_y : (k + 1) * size_y]


def sweep_kernel(
    bricks,
    visc_in,
    force_ref,
    wide_ref,
    y_even_ref,
    y_odd_ref,
    visc_ref,
    next_ref,
    coeff_ref,
    last_ref,
):
    size_x, size_y = bricks
    wide = Wide(bricks)
    odd_y = parities()[1]
    rows = ((odd_y == 1, y_even_ref), (odd_y == 0, y_odd_ref))
    for is_low, ref in rows:
        row = jnp.where(is_low, -1, size_y)
        visc_ref[wide.line(0, row), :] = ref[pl.ds(0, size_x), :]
        outer = jnp.where(is_low, -2, size_y + 1)
        visc_ref[wide.line(0, outer), :] = ref[pl.ds(size_x, size_x), :]
    for is_low, ref in rows:
        row = jnp.where(is_low, -1, size_y)
        visc = ref[pl.ds(0, size_x), :]
        force = ref[pl.ds(2 * size_x, size_x), :]
        faces, push = factors(visc, wide.around_line(visc_ref, 0, row), force)
        for c in range(3):
            vel = wide_ref[wide.line(c, row), :]
            beside = wide.around_line(wide_ref, c, row)
            value = relax(faces, push if c == 2 else None, vel, beside)
            next_ref[wide.line(c, row), :] = jnp.where(visc > 0.0, value, 0.0)
    for plane in range(1, size_x - 1):
        wide.first_core(visc_ref, wide_ref, force_ref, next_ref, coeff_ref, plane)
    for plane in range(2, size_x - 2):
        wide.second_sweep(coeff_ref, next_ref, last_ref, plane)


def finish_kernel(
    bricks,
    visc_in,
    next_in,
    coeff_in,
    last_in,
    wide_in,
    force_ref,
    x_even_ref,
    x_odd_ref,
    y_even_ref,
    y_odd_ref,
    out_ref,
    visc_ref,
    next_ref,
    coeff_ref,
    last_ref,
    wide_ref,
    sems,
):
    size_x, size_y = bricks
    wide = Wide(bricks)
    odd_x, odd_y = parities()
    whole = last_ref.reshape(3, size_x, size_y, last_ref.shape[1])
    copies = []
    for k, (first, stop) in enumerate(((2, size_x - 2), (0, 2), (size_x - 2, size_x))):
        at = (slice(None), slice(first, stop))
        copies.append(pltpu.make_async_copy(whole.at[at], out_ref.at[at], sems.at[k]))
    copies[0].start()

    sides = ((odd_x == 1, x_even_ref), (odd_x == 0, x_odd_ref))
    for is_low, ref in sides:
        first = jnp.where(is_low, -2, size_x)
        for k in range(2):
            visc_ref[wide.plane(0, first + k), :] = ref[pl.ds(k * size_y, size_y), :]
        plane = jnp.where(is_low, -1, size_x)
        for k, row in enumerate((-1, size_y)):
            at = 3 * size_y + 4 * k
            visc_ref[wide.cell(0, plane, row), :] = ref[at : at + 1, :]
            for c in range(3):
                wide_ref[wide.cell(c, plane, row), :] = ref[at + 1 + c : at + 2 + c, :]

    for plane in (0, size_x - 1):
        wide.first_core(visc_ref, wide_ref, force_ref, next_ref, coeff_ref, plane)
        at = slice(2 * size_x + plane, 2 * size_x + plane + 1)
        forces = (y_even_ref[at, :], y_odd_ref[at, :])
        for row, is_even in ((-1, odd_y == 1), (size_y, odd_y == 0)):
            force = jnp.where(is_even, *forces)
            wide.first_ring(visc_ref, wide_ref, next_ref, plane, force, row=row, rows=1)
    for is_low, ref in sides:
        plane = jnp.where(is_low, -1, size_x)
        force = ref[pl.ds(2 * size_y, size_y), :]
        wide.first_ring(visc_ref, wide_ref, next_ref, plane, force)

    for plane in (0, 1, size_x - 2, size_x - 1):
        wide.second_sweep(coeff_ref, next_ref, last_ref, plane)
        if plane == 1:
            copies[1].start()
    copies[2].start()
    for copy in copies:
        copy.wait()


def corner_kernel(
    bricks, even_in, odd_in, y_even_ref, y_odd_ref, wide_ref, x_even_ref, x_odd_ref
):
    size_x, size_y = bricks
    wide = Wide(bricks)
    odd_x, odd_y = parities()
    for ref, is_first in ((x_even_ref, odd_x == 1), (x_odd_ref, odd_x == 0)):
        near = jnp.where(is_first, 0, size_x - 1)
        pair = (y_even_ref[pl.ds(near, 1), :], y_odd_ref[pl.ds(near, 1), :])
        for k, row in enumerate((-1, size_y)):
            at = 3 * size_y + 4 * k
            ref[at : at + 1, :] = jnp.where(odd_y == 1 - k, *pair)
            for c in range(3):
                ref[at + 1 + c : at + 2 + c, :] = wide_ref[wide.cell(c, near, row), :]

    @pl.when(at_end("gx"))
    def _():
        x_odd_ref[3 * size_y :, :] = jnp.zeros((CORNERS, x_odd_ref.shape[1]), F32)


def limit(mebibytes):
    return pltpu.CompilerParams(vmem_limit_bytes=mebibytes << 20)


def in_hbm(value):
    return pltpu.with_memory_space_constraint(value, pltpu.HBM)


def shifted(value, axis, step):
    count = lax.axis_size(axis)
    pairs = [(i, i + step) for i in range(count) if 0 <= i + step < count]
    return lax.ppermute(value, axis, pairs)


def swapped(value, axis, first):
    counts = {name: lax.axis_size(name) for name in BOTH}
    other = BOTH[1 - BOTH.index(axis)]
    pairs = []
    for i in range(counts[axis]):
        for j in range(counts[other]):
            partner, beside = i + 1 - 2 * ((i + first) % 2), j
            if not 0 <= partner < counts[axis]:
                partner, beside = i, j ^ 1
                if first == 0 or beside >= counts[other]:
                    continue
            ends = ((i, j), (partner, beside))
            if axis == BOTH[1]:
                ends = tuple(end[::-1] for end in ends)
            pairs.append(tuple(x * counts["gy"] + y for x, y in ends))
    return lax.ppermute(value, BOTH, pairs)


def per_device(
    marker_comp, marker_strain, marker_live, marker_cell, block_dest, old_logvisc, velocity
):
    count_x = lax.axis_size("gx")
    count_y = lax.axis_size("gy")
    devices = count_x * count_y
    blocks, marks = marker_comp.shape
    size_x, size_y, depth = old_logvisc.shape
    columns = size_x * size_y
    slots = 2 * blocks // devices
    chunk = 3 * slots + 1
    total = devices * slots
    lines = (blocks // marks, marks)

    payload = pl.pallas_call(
        functools.partial(pack_kernel, slots, chunk),
        out_shape=jax.ShapeDtypeStruct((devices * chunk, marks), F32),
        in_specs=[HBM] * 5,
        out_specs=VMEM,
        scratch_shapes=[
            pltpu.SMEM(lines, jnp.int32),
            pltpu.VMEM(lines, jnp.int32),
            pltpu.VMEM((48 * BATCH, marks), F32),
            pltpu.SemaphoreType.DMA,
            pltpu.VMEM(lines, jnp.int32),
            pltpu.VMEM((blocks, marks), F32),
            pltpu.VMEM((blocks, marks), F32),
            pltpu.VMEM((blocks, marks), jnp.int32),
            pltpu.VMEM((blocks, marks), jnp.int32),
            pltpu.SemaphoreType.DMA((5,)),
        ],
        compiler_params=limit(12),
        name="pack",
    )(
        in_hbm(block_dest.reshape(lines)),
        in_hbm(marker_comp),
        in_hbm(marker_strain),
        in_hbm(marker_live),
        in_hbm(marker_cell),
    )
    payload = payload.reshape(devices * chunk, 1, marks)
    received = lax.all_to_all(payload, BOTH, split_axis=0, concat_axis=0, tiled=True)
    received = received.reshape(devices * chunk, marks)

    def y_lines(near, far):
        pair = jnp.concatenate([velocity[:, :, near], velocity[:, :, far]], axis=1)
        return pair.reshape(6 * size_x, depth)

    def x_planes(first):
        return velocity[:, first : first + 2].reshape(6 * size_y, depth)

    vy_low = shifted(y_lines(size_y - 1, size_y - 2), "gy", 1)
    vy_high = shifted(y_lines(0, 1), "gy", -1)
    vx_low = shifted(x_planes(size_x - 2), "gx", 1)
    vx_high = shifted(x_planes(0), "gx", -1)

    bricks = (size_x, size_y)
    wide = Wide(bricks)

    def shape(rows, width=depth, kind=F32):
        return jax.ShapeDtypeStruct((rows, width), kind)

    wide_vel = pl.pallas_call(
        functools.partial(widen_kernel, bricks),
        out_shape=shape(3 * wide.field),
        in_specs=[VMEM] * 3,
        out_specs=VMEM,
        compiler_params=limit(8),
        name="widen",
    )(velocity.reshape(3 * columns, depth), vx_low, vx_high)
    received, wide_vel = lax.optimization_barrier((received, wide_vel))

    edge = 4 * (size_x + size_y)
    x_side, y_side = shape(3 * size_y + CORNERS), shape(3 * size_x)
    old = old_logvisc.reshape(columns, depth)
    x_even, x_odd, y_even, y_odd, values, ids, wide_vel = pl.pallas_call(
        functools.partial(edge_kernel, slots, chunk, bricks),
        out_shape=(
            *(x_side, x_side, y_side, y_side),
            shape(total, 5 * depth, BF16),
            shape(total // depth),
            shape(3 * wide.field),
        ),
        in_specs=[VMEM] * 5,
        out_specs=(VMEM,) * 7,
        input_output_aliases={4: 6},
        scratch_shapes=[
            pltpu.VMEM((edge, total), BF16),
            pltpu.VMEM((edge, depth), F32),
            pltpu.VMEM((edge, depth), F32),
        ],
        compiler_params=limit(16),
        name="edge",
    )(received, old, vy_low, vy_high, wide_vel)
    logvisc, density, force, visc = pl.pallas_call(
        functools.partial(interior_kernel, bricks),
        out_shape=(*(shape(columns),) * 3, shape(wide.field)),
        in_specs=[VMEM] * 3,
        out_specs=(VMEM,) * 4,
        scratch_shapes=[pltpu.VMEM((columns, total), BF16)],
        compiler_params=limit(16),
        name="interior",
    )(values, ids, old)
    y_even = swapped(y_even, "gy", 0)
    y_odd = swapped(y_odd, "gy", 1)
    y_even, y_odd, visc, force = lax.optimization_barrier((y_even, y_odd, visc, force))
    x_even, x_odd = pl.pallas_call(
        functools.partial(corner_kernel, bricks),
        out_shape=(x_side, x_side),
        in_specs=[VMEM] * 5,
        out_specs=(VMEM, VMEM),
        input_output_aliases={0: 0, 1: 1},
        compiler_params=limit(4),
        name="corners",
    )(x_even, x_odd, y_even, y_odd, wide_vel)
    visc, wide_next, coeff, last = pl.pallas_call(
        functools.partial(sweep_kernel, bricks),
        out_shape=(
            shape(wide.field),
            shape(3 * wide.field),
            shape(7 * columns),
            shape(3 * columns),
        ),
        in_specs=[VMEM] * 5,
        out_specs=(VMEM,) * 4,
        input_output_aliases={0: 0},
        compiler_params=limit(12),
        name="sweep",
    )(visc, force, wide_vel, y_even, y_odd)
    x_even = swapped(x_even, "gx", 0)
    x_odd = swapped(x_odd, "gx", 1)
    smoothed = pl.pallas_call(
        functools.partial(finish_kernel, bricks),
        out_shape=(
            jax.ShapeDtypeStruct(velocity.shape, F32),
            shape(wide.field),
            shape(3 * wide.field),
            shape(7 * columns),
            shape(3 * columns),
            shape(3 * wide.field),
        ),
        in_specs=[VMEM] * 10,
        out_specs=(HBM, *(VMEM,) * 5),
        scratch_shapes=[pltpu.SemaphoreType.DMA((3,))],
        input_output_aliases={0: 1, 1: 2, 2: 3, 3: 4, 4: 5},
        compiler_params=limit(12),
        name="finish",
    )(
        visc,
        wide_next,
        coeff,
        last,
        wide_vel,
        force,
        x_even,
        x_odd,
        y_even,
        y_odd,
    )[0]
    return (
        logvisc.reshape(old_logvisc.shape),
        density.reshape(old_logvisc.shape),
        smoothed,
    )


def solution(mesh):
    return jax.shard_map(
        per_device,
        mesh=mesh,
        in_specs=(
            P(("gx", "gy"), None),
            P(("gx", "gy"), None),
            P(("gx", "gy"), None),
            P(("gx", "gy"), None),
            P(("gx", "gy"), None),
            P("gx", "gy", None),
            P(None, "gx", "gy", None),
        ),
        out_specs=(P("gx", "gy", None), P("gx", "gy", None), P(None, "gx", "gy", None)),
        check_vma=False,
    )
```

time: 66.5 us -> 61.2 us (0.920); the launches traced: 66.2 us -> 59.9 us
  waiting for transfers between devices: 32 us -> 24.9 us
  local copies, waits for them, and re-layouts: 0.2 us -> 3.41 us
  starting transfers between devices: 24.4 us -> 21.4 us
    ppermute x4, waiting for transfers between devices: 25.7 us -> 0.65 us  [shifted(): return lax.ppermute(value, axis, pairs)]
    all_to_all x1, waiting for transfers between devices: 0.01 us -> 21 us  [per_device(): lax.all_to_all(payload, BOTH, split_axis=0, concat_axis=0, tiled=True)]
    ppermute x4, starting transfers between devices: 6.08 us -> 2.95 us  [swapped(): return lax.ppermute(value, BOTH, pairs)]
    ppermute x4, waiting for transfers between devices: 6.31 us -> 3.24 us  [swapped(): return lax.ppermute(value, BOTH, pairs)]
    slice x1, local copies, waits for them, and re-layouts: 0.07 us -> 1.31 us  [y_lines(): pair = jnp.concatenate([velocity[:, :, near], velocity[:, :, far]], axis=1)]
    unnamed x4, local copies, waits for them, and re-layouts: 0.01 us -> 1.13 us
    slice x1, local copies, waits for them, and re-layouts: 0.02 us -> 0.96 us  [x_planes(): return velocity[:, first:first + 2].reshape(6 * size_y, depth)]
    pallas_call x3 -> x6, Pallas kernels: 4.32 us -> 4.83 us  [the longest x1 1.79 us: per_device(): pl.pallas_call(functools.partial(interior_kernel, bricks), out_shape=(*(s...]
  transfers between devices with their start and end apart: 9 -> 9, of which waited for: 6 -> 5; matrix products, arithmetic and copies ran while one was open for 0% -> 4% of each run, Pallas kernels for 0% -> 5%
where the time goes in v4:
time: 61.2 us; the launch traced here: 59.9 us
  waiting for transfers between devices  24.9 us (41%)
  starting transfers between devices  21.4 us (35%)
  Pallas kernels  9.45 us (15%)
  local copies, waits for them, and re-layouts  3.41 us (6%)
  between operations  0.78 us (1%)
    all_to_all x1, waiting for transfers between devices, per_device(): lax.all_to_all(payload, BOTH, split_axis=0, concat_axis=0, tiled=True)  21 us
    ppermute x4, starting transfers between devices, shifted(): return lax.ppermute(value, axis, pairs)  12.4 us
    all_to_all x1, starting transfers between devices, per_device(): lax.all_to_all(payload, BOTH, split_axis=0, concat_axis=0, tiled=True)  5.99 us
    pallas_call x1, Pallas kernels, per_device(): pl.pallas_call(functools.partial(pack_kernel, slots, chunk), out_shape=ja...  4.62 us
    ppermute x4, waiting for transfers between devices, swapped(): return lax.ppermute(value, BOTH, pairs)  3.24 us
    ppermute x4, starting transfers between devices, swapped(): return lax.ppermute(value, BOTH, pairs)  2.95 us
    pallas_call x1, Pallas kernels, per_device(): pl.pallas_call(functools.partial(interior_kernel, bricks), out_shape=(*(s...  1.79 us
    slice x1, local copies, waits for them, and re-layouts, y_lines(): pair = jnp.concatenate([velocity[:, :, near], velocity[:, :, far]], axis=1)  1.31 us
  transfers between devices with their start and end apart: 9, of which 5 were waited for; matrix products, arithmetic and copies ran while one was open for 4% of the time, Pallas kernels for 5%

profile of v4, /device:TPU:12, one launch (start us, length us, event | category | flops | bytes accessed | tf_op | source)
XLA Modules:
  0.0 59.9 jit_solution(8089424393617933385)
XLA Ops:
  0.6 4.6 %pack.1 = f32[3104,128]{1,0:T(8,128)} custom-call(s32[4,128]{1,0:T(4,128)} %bitcast.33, f32[512,128]{1,0:T(8,128)} %comp_hbm.1, f32[512,128]{1,0:T(8,128)} %strain_hbm.1, s32[512,128]{1,0:T(8,128)} %live_hbm.1, s32[512,128]{1,0:T(8,128)} %cell_hbm.1), custom_call_target="tpu_custom_call" | custom-call | tf_op jit(solution)/shard_map/pack/pallas_call | solution.py:600
  5.3 6.0 %all-to-all-start = ((f32[3104,1,128]{2,1,0:T(1,128)}), f32[3104,1,128]{2,1,0:T(1,128)S(1)}, u32[]{:S(2)}, u32[]{:S(2)}) async-start(f32[3104,1,128]{2,1,0:T(1,128)} %bitcast.2), calls=%async_computation | async-start | bytes 3178496 | tf_op jit(solution)/shard_map/all_to_all | solution.py:627
  11.3 1.3 %fusion = (f32[3,16,1,128]{3,2,1,0:T(1,128)S(1)}, f32[3,16,1,128]{3,2,1,0:T(1,128)S(1)}, f32[3,16,1,128]{3,2,1,0:T(1,128)S(1)}, f32[3,16,1,128]{3,2,1,0:T(1,128)S(1)}) fusion(f32[3,16,32,128]{3,2,1,0:T(8,128)} %param.13), kind=kLoop, calls=%fused_computation.2 | loop fusion | bytes 196608 | tf_op jit(solution)/shard_map/slice | solution.py:631
  12.6 0.0 copy-start.1
  12.6 3.5 %collective-permute-start.2 = (f32[96,128]{1,0:T(8,128)S(1)}, f32[96,128]{1,0:T(8,128)S(1)}, u32[]{:S(2)}, u32[]{:S(2)}) collective-permute-start(f32[96,128]{1,0:T(8,128)S(1)} %bitcast.31), channel_id=1, source_target_pairs={{0,1},{1,2},{2,3},{4,5},{5,6},{6,7},{8,9},{9,10},{10,11},{12,13},{... | collective-permute-start | bytes 147464 | tf_op jit(solution)/shard_map/ppermute | solution.py:565
  16.1 1.0 %fusion.1 = (f32[3,2,32,128]{3,2,1,0:T(8,128)S(1)}, f32[3,2,32,128]{3,2,1,0:T(8,128)S(1)}) fusion(f32[3,16,32,128]{3,2,1,0:T(8,128)} %param.13), kind=kLoop, calls=%fused_computation.3 | loop fusion | bytes 393216 | tf_op jit(solution)/shard_map/slice | solution.py:635
  17.1 1.9 %collective-permute-start = (f32[192,128]{1,0:T(8,128)S(1)}, f32[192,128]{1,0:T(8,128)S(1)}, u32[]{:S(2)}, u32[]{:S(2)}) collective-permute-start(f32[192,128]{1,0:T(8,128)S(1)} %bitcast.30), channel_id=1, source_target_pairs={{0,4},{4,8},{8,12},{12,16},{16,20},{20,24},{24,28},{1,5},{5,9},{9,... | collective-permute-start | bytes 294920 | tf_op jit(solution)/shard_map/ppermute | solution.py:565
  19.0 4.5 %collective-permute-start.1 = (f32[192,128]{1,0:T(8,128)S(1)}, f32[192,128]{1,0:T(8,128)S(1)}, u32[]{:S(2)}, u32[]{:S(2)}) collective-permute-start(f32[192,128]{1,0:T(8,128)S(1)} %bitcast.29), channel_id=1, source_target_pairs={{4,0},{8,4},{12,8},{16,12},{20,16},{24,20},{28,24},{5,1},{9,5},{13... | collective-permute-start | bytes 294920 | tf_op jit(solution)/shard_map/ppermute | solution.py:565
  23.6 2.5 %collective-permute-start.3 = (f32[96,128]{1,0:T(8,128)S(1)}, f32[96,128]{1,0:T(8,128)S(1)}, u32[]{:S(2)}, u32[]{:S(2)}) collective-permute-start(f32[96,128]{1,0:T(8,128)S(1)} %bitcast.32), channel_id=1, source_target_pairs={{1,0},{2,1},{3,2},{5,4},{6,5},{7,6},{9,8},{10,9},{11,10},{13,12},{... | collective-permute-start | bytes 147464 | tf_op jit(solution)/shard_map/ppermute | solution.py:565
  26.0 0.0 collective-permute-done.vx_low_ref
  26.1 0.0 collective-permute-done.1.vx_high_ref
  26.1 0.0 copy-start
  26.1 1.1 %copy-done = f32[3,16,32,128]{3,2,1,0:T(8,128)S(1)} copy-done((f32[3,16,32,128]{3,2,1,0:T(8,128)S(1)}, f32[3,16,32,128]{3,2,1,0:T(8,128)}, u32[]{:S(2)}) %copy-start) | copy-done | bytes 786456
  27.2 0.1 widen.1.wide_in
  27.3 21.0 %all-to-all-done = f32[3104,1,128]{2,1,0:T(1,128)S(1)} async-done(((f32[3104,1,128]{2,1,0:T(1,128)}), f32[3104,1,128]{2,1,0:T(1,128)S(1)}, u32[]{:S(2)}, u32[]{:S(2)}) %all-to-all-start) | async-done | bytes 1589280 | tf_op jit(solution)/shard_map/all_to_all | solution.py:627
  48.3 0.0 collective-permute-done.2.vy_low_ref
  48.3 0.6 %collective-permute-done.3.vy_high_ref = f32[96,128]{1,0:T(8,128)S(1)} collective-permute-done((f32[96,128]{1,0:T(8,128)S(1)}, f32[96,128]{1,0:T(8,128)S(1)}, u32[]{:S(2)}, u32[]{:S(2)}) %collective-permute-start.3) | collective-permute-done | bytes 49184 | tf_op jit(solution)/shard_map/ppermute | solution.py:565
  48.9 0.0 copy-done.1
  48.9 0.7 %edge.1 = (f32[104,128]{1,0:T(8,128)S(1)}, f32[104,128]{1,0:T(8,128)S(1)}, f32[48,128]{1,0:T(8,128)S(1)}, f32[48,128]{1,0:T(8,128)S(1)}, bf16[1024,640]{1,0:T(8,...) custom-call(f32[3104,128]{1,0:T(8,128)S(1)} %bitcast.21, ...), custom_call_target="tpu_custom_call", output_to_operand_aliasing={{6}: (4, {})} | custom-call | tf_op jit(solution)/shard_map/edge/pallas_call | solution.py:661
  49.7 0.1 collective-permute-start.4
  49.8 1.3 %collective-permute-start.5 = (f32[48,128]{1,0:T(8,128)S(1)}, f32[48,128]{1,0:T(8,128)S(1)}, u32[]{:S(2)}, u32[]{:S(2)}) collective-permute-start(f32[48,128]{1,0:T(8,128)S(1)} %get-tuple-element.34), channel_id=1, source_target_pairs={{0,4},{4,0},{8,12},{12,8},{16,20},{20,16},{24,28},{28,24},{1,2},{5... | collective-permute-start | bytes 73736 | tf_op jit(solution)/shard_map/ppermute | solution.py:583
  51.0 1.8 %interior.1 = (f32[512,128]{1,0:T(8,128)}, f32[512,128]{1,0:T(8,128)}, f32[512,128]{1,0:T(8,128)S(1)}, f32[960,128]{1,0:T(8,128)S(1)}) custom-call(bf16[1024,640]{1,0:T(8,128)(2,1)S(1)} %get-tuple-element.29.value_ref, f32[8,128]{1,0:T(8,128)S(1)} %get-tuple-element.30.ids_ref, f32[512,128]{1,0:T(8,128)S(1)} %bitcast.24), custom_call_target="tpu_custom_call" | custom-call | tf_op jit(solution)/shard_map/interior/pallas_call | solution.py:680
  52.8 0.8 %collective-permute-done.4.y_even_ref = f32[48,128]{1,0:T(8,128)S(1)} collective-permute-done((f32[48,128]{1,0:T(8,128)S(1)}, f32[48,128]{1,0:T(8,128)S(1)}, u32[]{:S(2)}, u32[]{:S(2)}) %collective-permute-start.4) | collective-permute-done | bytes 24608 | tf_op jit(solution)/shard_map/ppermute | solution.py:583
  53.6 0.1 collective-permute-done.5.y_odd_ref
  53.7 0.1 collective-permute-start.6
  53.7 1.6 %collective-permute-start.7 = (f32[104,128]{1,0:T(8,128)S(1)}, f32[104,128]{1,0:T(8,128)S(1)}, u32[]{:S(2)}, u32[]{:S(2)}) collective-permute-start(f32[104,128]{1,0:T(8,128)S(1)} %get-tuple-element.49), channel_id=1, source_target_pairs={{0,1},{1,0},{2,3},{3,2},{4,8},{5,9},{6,10},{7,11},{8,4},{9,5},{10,... | collective-permute-start | bytes 159752 | tf_op jit(solution)/shard_map/ppermute | solution.py:583
  55.3 1.1 %sweep.1 = (f32[960,128]{1,0:T(8,128)S(1)}, f32[2880,128]{1,0:T(8,128)S(1)}, f32[3584,128]{1,0:T(8,128)S(1)}, f32[1536,128]{1,0:T(8,128)S(1)}) custom-call(f32[960,128]{1,0:T(8,128)S(1)} %get-tuple-element.37.visc_in, f32[512,128]{1,0:T(8,128)S(1)} %get-tuple-element.38.force_ref, ...), custom_call_target="tpu_custom_call", output_to_operand_aliasing={{0}: (0, {})} | custom-call | tf_op jit(solution)/shard_map/sweep/pallas_call | solution.py:701
  56.4 0.0 collective-permute-done.6.x_even_ref
  56.4 2.4 %collective-permute-done.7.x_odd_ref = f32[104,128]{1,0:T(8,128)S(1)} collective-permute-done((f32[104,128]{1,0:T(8,128)S(1)}, f32[104,128]{1,0:T(8,128)S(1)}, u32[]{:S(2)}, u32[]{:S(2)}) %collective-permute-start.7) | collective-permute-done | bytes 53280 | tf_op jit(solution)/shard_map/ppermute | solution.py:583
  58.8 1.1 %finish.1 = (f32[3,16,32,128]{3,2,1,0:T(8,128)}, f32[960,128]{1,0:T(8,128)S(1)}, f32[2880,128]{1,0:T(8,128)S(1)}, f32[3584,128]{1,0:T(8,128)S(1)}, f32[1536,128]{1,0:T(8,128)S(1)}, /*index=5*/f32[2880,128]{1,0:T(8,128)S(1)}) custom-call(f32[960,128]{1,0:T(8,128)S(1)} %get-tuple-element.42.vis, ...), custom_call_target="tpu_custom_call", output_to_operand_aliasing={{1}: (0, {}), {2}: (1, {}), {3}: (2, {}), {4}: (3, {}), {5}... | custom-call | tf_op jit(solution)/shard_map/finish/pallas_call | solution.py:717
  (3 shorter events, 0.0 us)
Async XLA Ops:
  5.3 43.0 %all-to-all-start = ((f32[3104,1,128]{2,1,0:T(1,128)}), f32[3104,1,128]{2,1,0:T(1,128)S(1)}, u32[]{:S(2)}, u32[]{:S(2)}) async-start(f32[3104,1,128]{2,1,0:T(1,128)} %bitcast.2), calls=%async_computation | async-start | bytes 3178496 | tf_op jit(solution)/shard_map/all_to_all | solution.py:627
  12.6 36.4 %copy-start.1 = (f32[16,32,128]{2,1,0:T(8,128)S(1)}, f32[16,32,128]{2,1,0:T(8,128)}, u32[]{:S(2)}) copy-start(f32[16,32,128]{2,1,0:T(8,128)} %param.12) | copy-start | bytes 786436
  12.6 35.7 %collective-permute-start.2 = (f32[96,128]{1,0:T(8,128)S(1)}, f32[96,128]{1,0:T(8,128)S(1)}, u32[]{:S(2)}, u32[]{:S(2)}) collective-permute-start(f32[96,128]{1,0:T(8,128)S(1)} %bitcast.31), channel_id=1, source_target_pairs={{0,1},{1,2},{2,3},{4,5},{5,6},{6,7},{8,9},{9,10},{10,11},{12,13},{... | collective-permute-start | bytes 147464 | tf_op jit(solution)/shard_map/ppermute | solution.py:565
  17.1 9.0 %collective-permute-start = (f32[192,128]{1,0:T(8,128)S(1)}, f32[192,128]{1,0:T(8,128)S(1)}, u32[]{:S(2)}, u32[]{:S(2)}) collective-permute-start(f32[192,128]{1,0:T(8,128)S(1)} %bitcast.30), channel_id=1, source_target_pairs={{0,4},{4,8},{8,12},{12,16},{16,20},{20,24},{24,28},{1,5},{5,9},{9,... | collective-permute-start | bytes 294920 | tf_op jit(solution)/shard_map/ppermute | solution.py:565
  19.0 7.0 %collective-permute-start.1 = (f32[192,128]{1,0:T(8,128)S(1)}, f32[192,128]{1,0:T(8,128)S(1)}, u32[]{:S(2)}, u32[]{:S(2)}) collective-permute-start(f32[192,128]{1,0:T(8,128)S(1)} %bitcast.29), channel_id=1, source_target_pairs={{4,0},{8,4},{12,8},{16,12},{20,16},{24,20},{28,24},{5,1},{9,5},{13... | collective-permute-start | bytes 294920 | tf_op jit(solution)/shard_map/ppermute | solution.py:565
  23.6 25.4 %collective-permute-start.3 = (f32[96,128]{1,0:T(8,128)S(1)}, f32[96,128]{1,0:T(8,128)S(1)}, u32[]{:S(2)}, u32[]{:S(2)}) collective-permute-start(f32[96,128]{1,0:T(8,128)S(1)} %bitcast.32), channel_id=1, source_target_pairs={{1,0},{2,1},{3,2},{5,4},{6,5},{7,6},{9,8},{10,9},{11,10},{13,12},{... | collective-permute-start | bytes 147464 | tf_op jit(solution)/shard_map/ppermute | solution.py:565
  26.1 1.1 %copy-start = (f32[3,16,32,128]{3,2,1,0:T(8,128)S(1)}, f32[3,16,32,128]{3,2,1,0:T(8,128)}, u32[]{:S(2)}) copy-start(f32[3,16,32,128]{3,2,1,0:T(8,128)} %param.13) | copy-start | bytes 2359300
  49.7 3.9 %collective-permute-start.4 = (f32[48,128]{1,0:T(8,128)S(1)}, f32[48,128]{1,0:T(8,128)S(1)}, u32[]{:S(2)}, u32[]{:S(2)}) collective-permute-start(f32[48,128]{1,0:T(8,128)S(1)} %get-tuple-element.33), channel_id=1, source_target_pairs={{0,1},{4,5},{8,9},{12,13},{16,17},{20,21},{24,25},{28,29},{1,0},{5... | collective-permute-start | bytes 73736 | tf_op jit(solution)/shard_map/ppermute | solution.py:583
  49.8 3.9 %collective-permute-start.5 = (f32[48,128]{1,0:T(8,128)S(1)}, f32[48,128]{1,0:T(8,128)S(1)}, u32[]{:S(2)}, u32[]{:S(2)}) collective-permute-start(f32[48,128]{1,0:T(8,128)S(1)} %get-tuple-element.34), channel_id=1, source_target_pairs={{0,4},{4,0},{8,12},{12,8},{16,20},{20,16},{24,28},{28,24},{1,2},{5... | collective-permute-start | bytes 73736 | tf_op jit(solution)/shard_map/ppermute | solution.py:583
  53.7 2.8 %collective-permute-start.6 = (f32[104,128]{1,0:T(8,128)S(1)}, f32[104,128]{1,0:T(8,128)S(1)}, u32[]{:S(2)}, u32[]{:S(2)}) collective-permute-start(f32[104,128]{1,0:T(8,128)S(1)} %get-tuple-element.48), channel_id=1, source_target_pairs={{0,4},{1,5},{2,6},{3,7},{4,0},{5,1},{6,2},{7,3},{8,12},{9,13},{10,... | collective-permute-start | bytes 159752 | tf_op jit(solution)/shard_map/ppermute | solution.py:583
  53.7 5.1 %collective-permute-start.7 = (f32[104,128]{1,0:T(8,128)S(1)}, f32[104,128]{1,0:T(8,128)S(1)}, u32[]{:S(2)}, u32[]{:S(2)}) collective-permute-start(f32[104,128]{1,0:T(8,128)S(1)} %get-tuple-element.49), channel_id=1, source_target_pairs={{0,1},{1,0},{2,3},{3,2},{4,8},{5,9},{6,10},{7,11},{8,4},{9,5},{10,... | collective-permute-start | bytes 159752 | tf_op jit(solution)/shard_map/ppermute | solution.py:583

commit v5 on v4

--- a/solution.py
+++ b/solution.py
@@ -31,94 +31,29 @@
     return high, values - high
 
 
-def pack_kernel(
-    slots,
-    chunk,
-    dest_hbm,
-    comp_hbm,
-    strain_hbm,
-    live_hbm,
-    cell_hbm,
-    out_ref,
-    place_ref,
-    line_ref,
-    sums_ref,
-    place_sem,
-    dest_ref,
-    comp_ref,
-    strain_ref,
-    live_ref,
-    cell_ref,
-    load_sem,
-):
-    blocks, marks = comp_ref.shape
-    devices = out_ref.shape[0] // chunk
-    shift = marks.bit_length() - 1
-    part = marks // WAYS
-    low_bits = part.bit_length() - 1
-    pairs = (
-        (dest_hbm, dest_ref),
-        (cell_hbm, cell_ref),
-        (comp_hbm, comp_ref),
-        (strain_hbm, strain_ref),
-        (live_hbm, live_ref),
-    )
-    loads = [pltpu.make_async_copy(*pair, load_sem.at[k]) for k, pair in enumerate(pairs)]
-    for load in loads:
-        load.start()
-    out_ref[...] = jnp.zeros_like(out_ref)
-    loads[0].wait()
-    loads[1].wait()
-
-    owner_ids = lax.broadcasted_iota(jnp.int32, (devices, marks), 0)
-    rank_ids = lax.broadcasted_iota(jnp.int32, (slots, marks), 0)
-    square = (marks, marks)
-    before = lax.broadcasted_iota(jnp.int32, square, 0) < lax.broadcasted_iota(jnp.int32, square, 1)
-    before = jnp.where(before, 1.0, 0.0).astype(BF16)
-    seen = jnp.zeros((devices, 1), F32)
-    ids = jnp.zeros((devices, slots), F32)
-    for k in range(blocks // marks):
-        dest = dest_ref[k : k + 1, :]
-        mine = owner_ids == dest
-        hot = jnp.where(mine, 1.0, 0.0)
-        earlier = jnp.dot(hot.astype(BF16), before, preferred_element_type=F32) + seen
-        rank = jnp.sum(jnp.where(mine, earlier, 0.0), axis=0, keepdims=True).astype(jnp.int32)
-        seen = seen + jnp.sum(hot, axis=1, keepdims=True)
-        line_ref[k : k + 1, :] = dest * chunk + rank
-        column = (cell_ref[k * marks : (k + 1) * marks, :] >> shift).astype(F32).T[0:1] + 1.0
-        spot = jnp.where(rank_ids == rank, 1.0, 0.0).astype(BF16)
-        for piece in split(column):
-            weighted = jnp.where(mine, piece, 0.0).astype(BF16)
-            ids = ids + lax.dot_general(weighted, spot, BY_LANES, preferred_element_type=F32)
-    places = pltpu.make_async_copy(line_ref, place_ref, place_sem)
-    places.start()
-    ids = ids - 1.0
-    for owner in range(devices):
-        at = owner * chunk + 3 * slots
-        out_ref[at : at + 1, 0:slots] = ids[owner : owner + 1, :]
-    for load in loads[2:]:
-        load.wait()
-
-    fine_ids = lax.broadcasted_iota(jnp.int32, (part, marks), 0).astype(F32).astype(BF16)
-    row_ids = lax.broadcasted_iota(jnp.int32, (8, marks), 0)
-    lane_ids = lax.broadcasted_iota(jnp.int32, (8, marks), 1)
-    halves = [row_ids < 4, row_ids >= 4]
-    spans = [(lane_ids >> low_bits) == ((row_ids + w) & (WAYS - 1)) for w in range(WAYS)]
-
-    def depth_sums(group):
-        rows = pl.ds(pl.multiple_of(group * 8, 8), 8)
-        comp = comp_ref[rows, :]
-        strain = strain_ref[rows, :]
-        weight = live_ref[rows, :].astype(F32)
-        soften = strain / (1.0 + strain)
-        logv = weight * (LOG_HIGH * comp + LOG_LOW * (1.0 - comp) - WEAKENING * soften)
-        rho = weight * (1.0 + DENSITY_JUMP * comp - SOFTENING * soften)
-        pieces = [*split(logv), *split(rho), weight]
-        depth = cell_ref[rows, :] & (marks - 1)
-        coarse = ((depth >> low_bits) - row_ids) & (WAYS - 1)
+class Depth:
+    def __init__(self, marks):
+        self.marks = marks
+        self.shift = marks.bit_length() - 1
+        self.part = marks // WAYS
+        self.low_bits = self.part.bit_length() - 1
+        ids = lax.broadcasted_iota(jnp.int32, (self.part, marks), 0)
+        self.fine_ids = ids.astype(F32).astype(BF16)
+        self.row_ids = lax.broadcasted_iota(jnp.int32, (8, marks), 0)
+        lane_ids = lax.broadcasted_iota(jnp.int32, (8, marks), 1)
+        self.halves = [self.row_ids < 4, self.row_ids >= 4]
+        self.spans = [
+            (lane_ids >> self.low_bits) == ((self.row_ids + w) & (WAYS - 1)) for w in range(WAYS)
+        ]
+
+    def sums(self, fields, cell):
+        marks, part = self.marks, self.part
+        pieces = [piece for field in fields for piece in field]
+        depth = cell & (marks - 1)
+        coarse = ((depth >> self.low_bits) - self.row_ids) & (WAYS - 1)
         fine = (depth & (part - 1)).astype(F32)
         left, right = [], []
-        for half in halves:
+        for half in self.halves:
             lines = []
             for w in range(WAYS):
                 mask = (coarse == w) & half
@@ -129,7 +64,7 @@
             for b in range(first, first + 4):
                 line = jnp.broadcast_to(fine[b : b + 1, :], (16, marks)).astype(BF16)
                 line = jnp.concatenate([line] * (part // 16), axis=0)
-                lines.append(jnp.where(fine_ids == line, BF16(1.0), BF16(0.0)))
+                lines.append(jnp.where(self.fine_ids == line, BF16(1.0), BF16(0.0)))
             right.append(jnp.concatenate(lines, axis=0))
         sums = lax.dot_general(
             jnp.concatenate(left, axis=1),
@@ -137,43 +72,42 @@
             BY_LANES,
             preferred_element_type=F32,
         )
-
-        def piece_sum(w, p):
-            first = (w * len(pieces) + p) * 8
-            return sums[first : first + 8]
-
-        results = []
-        for numbers in ((0, 1), (2, 3), (4,)):
+        results, number = [], 0
+        for field in fields:
             total = None
             for w in range(WAYS):
-                value = piece_sum(w, numbers[0])
-                if len(numbers) > 1:
-                    value = value + piece_sum(w, numbers[1])
+                rows = [(w * len(pieces) + number + p) * 8 for p in range(len(field))]
+                value = sums[rows[0] : rows[0] + 8]
+                for row in rows[1:]:
+                    value = value + sums[row : row + 8]
                 if w:
                     value = pltpu.roll(value, part * w, 1)
-                total = value if total is None else jnp.where(spans[w], value, total)
+                total = value if total is None else jnp.where(self.spans[w], value, total)
             results.append(total)
+            number += len(field)
         return results
 
+
+def placed(blocks, count, compute, places, place_ref, sums_ref, out_ref, slots):
     def batch(step, g, f):
-        first = (step & 1) * (24 * BATCH) + g * 24 + f * 8
+        first = ((step & 1) * BATCH + g) * (8 * count) + f * 8
         return pl.ds(pl.multiple_of(first, 8), 8)
 
     def put(step):
         for g in range(BATCH):
-            for f, value in enumerate(depth_sums(step * BATCH + g)):
+            rows = pl.ds(pl.multiple_of((step * BATCH + g) * 8, 8), 8)
+            for f, value in enumerate(compute(rows)):
                 sums_ref[batch(step, g, f), :] = value
 
     def place(step):
         for g in range(BATCH):
             group = step * BATCH + g
-            values = [sums_ref[batch(step, g, f), :] for f in range(3)]
+            values = [sums_ref[batch(step, g, f), :] for f in range(count)]
             for k in range(8):
                 at = place_ref[group // 16, (group % 16) * 8 + k]
-                for f in range(3):
+                for f in range(count):
                     out_ref[pl.ds(at + f * slots, 1), :] = values[f][k : k + 1]
 
-    steps = blocks // 8 // BATCH
     put(0)
     places.wait()
 
@@ -182,8 +116,151 @@
         put(i)
         return carry
 
+    steps = blocks // 8 // BATCH
     lax.fori_loop(1, steps, step, 0)
     place(steps - 1)
+
+
+def count_kernel(slots, chunk, counts, dest_hbm, live_hbm, cell_hbm, *refs):
+    size_x, size_y = counts
+    plane_refs = refs[:size_y]
+    (
+        line_ref,
+        ids_ref,
+        rows_ref,
+        place_ref,
+        spot_ref,
+        sums_ref,
+        place_sem,
+        dest_ref,
+        live_ref,
+        cell_ref,
+        load_sem,
+    ) = refs[size_y:]
+    blocks, marks = live_ref.shape
+    devices = size_x * size_y
+    depth = Depth(marks)
+    pairs = ((dest_hbm, dest_ref), (cell_hbm, cell_ref), (live_hbm, live_ref))
+    loads = [pltpu.make_async_copy(*pair, load_sem.at[k]) for k, pair in enumerate(pairs)]
+    for load in loads:
+        load.start()
+    rows_ref[...] = jnp.zeros_like(rows_ref)
+    loads[0].wait()
+
+    owner_ids = lax.broadcasted_iota(jnp.int32, (devices, marks), 0)
+    rank_ids = lax.broadcasted_iota(jnp.int32, (slots, marks), 0)
+    square = (marks, marks)
+    before = lax.broadcasted_iota(jnp.int32, square, 0) < lax.broadcasted_iota(jnp.int32, square, 1)
+    before = jnp.where(before, 1.0, 0.0).astype(BF16)
+    seen = jnp.zeros((devices, 1), F32)
+    owned, ranks = [], []
+    own_y = lax.axis_index("gy")
+    for k in range(blocks // marks):
+        dest = dest_ref[k : k + 1, :]
+        mine = owner_ids == dest
+        hot = jnp.where(mine, 1.0, 0.0)
+        earlier = jnp.dot(hot.astype(BF16), before, preferred_element_type=F32) + seen
+        rank = jnp.sum(jnp.where(mine, earlier, 0.0), axis=0, keepdims=True).astype(jnp.int32)
+        seen = seen + jnp.sum(hot, axis=1, keepdims=True)
+        line_ref[k : k + 1, :] = dest * chunk + rank
+        across = (dest & (size_y - 1)) ^ own_y
+        along = dest >> (size_y.bit_length() - 1)
+        spot_ref[k : k + 1, :] = (across * size_x + along) * slots + rank
+        owned.append(mine)
+        ranks.append(rank)
+    places = pltpu.make_async_copy(spot_ref, place_ref, place_sem)
+    places.start()
+    for load in loads[1:]:
+        load.wait()
+    ids = jnp.zeros((devices, slots), F32)
+    for k, (mine, rank) in enumerate(zip(owned, ranks)):
+        column = cell_ref[k * marks : (k + 1) * marks, :] >> depth.shift
+        column = column.astype(F32).T[0:1] + 1.0
+        spot = jnp.where(rank_ids == rank, 1.0, 0.0).astype(BF16)
+        for piece in split(column):
+            weighted = jnp.where(mine, piece, 0.0).astype(BF16)
+            ids = ids + lax.dot_general(weighted, spot, BY_LANES, preferred_element_type=F32)
+    ids_ref[...] = jnp.zeros_like(ids_ref)
+    ids_ref[:, 0:slots] = ids - 1.0
+
+    def compute(rows):
+        weight = live_ref[rows, :].astype(F32)
+        return depth.sums([(weight,)], cell_ref[rows, :])
+
+    placed(blocks, 1, compute, places, place_ref, sums_ref, rows_ref, slots)
+    for k, ref in enumerate(plane_refs):
+        ref[...] = rows_ref[pl.ds(k * size_x * slots, size_x * slots), :]
+
+
+def pack_kernel(
+    slots,
+    chunk,
+    comp_hbm,
+    strain_hbm,
+    live_hbm,
+    cell_hbm,
+    line_ref,
+    ids_ref,
+    out_ref,
+    place_ref,
+    sums_ref,
+    place_sem,
+    comp_ref,
+    strain_ref,
+    live_ref,
+    cell_ref,
+    load_sem,
+):
+    blocks, marks = comp_ref.shape
+    devices = out_ref.shape[0] // chunk
+    depth = Depth(marks)
+    pairs = (
+        (comp_hbm, comp_ref),
+        (strain_hbm, strain_ref),
+        (live_hbm, live_ref),
+        (cell_hbm, cell_ref),
+    )
+    loads = [pltpu.make_async_copy(*pair, load_sem.at[k]) for k, pair in enumerate(pairs)]
+    for load in loads:
+        load.start()
+    places = pltpu.make_async_copy(line_ref, place_ref, place_sem)
+    places.start()
+    out_ref[...] = jnp.zeros_like(out_ref)
+    for owner in range(devices):
+        at = owner * chunk + 2 * slots
+        out_ref[at : at + 1, :] = ids_ref[owner : owner + 1, :]
+    for load in loads:
+        load.wait()
+
+    def compute(rows):
+        comp = comp_ref[rows, :]
+        strain = strain_ref[rows, :]
+        weight = live_ref[rows, :].astype(F32)
+        soften = strain / (1.0 + strain)
+        logv = weight * (LOG_HIGH * comp + LOG_LOW * (1.0 - comp) - WEAKENING * soften)
+        rho = weight * (1.0 + DENSITY_JUMP * comp - SOFTENING * soften)
+        return depth.sums([split(logv), split(rho)], cell_ref[rows, :])
+
+    placed(blocks, 2, compute, places, place_ref, sums_ref, out_ref, slots)
+
+
+def regroup_kernel(slots, counts, *refs):
+    size_x, size_y = counts
+    own_x = lax.axis_index("gx")
+    for k, out_ref in enumerate(refs[size_y:]):
+        at = pl.multiple_of((own_x ^ k) * slots, 8)
+        for j, ref in enumerate(refs[:size_y]):
+            out_ref[j * slots : (j + 1) * slots, :] = ref[pl.ds(at, slots), :]
+
+
+def gather_kernel(slots, counts, *refs):
+    size_x, size_y = counts
+    own_x, own_y = lax.axis_index("gx"), lax.axis_index("gy")
+    out_ref = refs[size_x]
+    for k, ref in enumerate(refs[:size_x]):
+        for j in range(size_y):
+            at = pl.multiple_of(((own_x ^ k) * size_y + (own_y ^ j)) * slots, 8)
+            out_ref[pl.ds(at, slots), :] = ref[j * slots : (j + 1) * slots, :]
 
 
 def parities():
@@ -196,14 +273,7 @@
 
 
 def boundary_columns(size_x, size_y):
-    return (
-        (0, 2 * size_y, 1),
-        ((size_x - 2) * size_y, 2 * size_y, 1),
-        (0, size_x, size_y),
-        (1, size_x, size_y),
-        (size_y - 1, size_x, size_y),
-        (size_y - 2, size_x, size_y),
-    )
+    return tuple((first, size_x, size_y) for first in (0, 1, size_y - 1, size_y - 2))
 
 
 def averages(sums, depth, old):
@@ -218,17 +288,12 @@
     chunk,
     bricks,
     recv_ref,
+    count_ref,
     old_ref,
-    vy_low_ref,
-    vy_high_ref,
-    wide_in,
-    x_even_ref,
-    x_odd_ref,
     y_even_ref,
     y_odd_ref,
     value_ref,
     ids_ref,
-    wide_ref,
     hot_ref,
     visc_ref,
     force_ref,
@@ -239,11 +304,6 @@
     per = depth // slots
     lanes = lax.broadcasted_iota(jnp.int32, (1, depth), 1)
     runs = boundary_columns(size_x, size_y)
-    wide = Wide(bricks)
-    for c in range(3):
-        for ref, near, far in ((vy_low_ref, -1, -2), (vy_high_ref, size_y, size_y + 1)):
-            for k, row in enumerate((near, far)):
-                wide_ref[wide.line(c, row), :] = ref[pl.ds((2 * c + k) * size_x, size_x), :]
     names = []
     for first, count, stride in runs:
         names.append(lax.broadcasted_iota(jnp.int32, (count, depth), 0) * stride + first)
@@ -253,42 +313,32 @@
         ids = jnp.full((1, depth), -1.0, F32)
         for k in range(per):
             first = (part * per + k) * chunk
-            line = recv_ref[first + 3 * slots : first + 3 * slots + 1, :]
+            line = recv_ref[first + 2 * slots : first + 2 * slots + 1, :]
             if k:
                 line = pltpu.roll(line, k * slots, 1)
             ids = jnp.where((lanes >= k * slots) & (lanes < (k + 1) * slots), line, ids)
         ids_ref[part : part + 1, :] = ids
         hot_ref[:, span] = jnp.where(names == ids, 1.0, 0.0).astype(BF16)
-        for v in range(3):
+        for v in range(2):
             lines = []
             for k in range(per):
                 lines.append(recv_ref[pl.ds((part * per + k) * chunk + v * slots, slots), :])
             high, low = split(jnp.concatenate(lines, axis=0))
             value_ref[span, pl.ds(2 * v * depth, depth)] = high.astype(BF16)
-            if v < 2:
-                value_ref[span, pl.ds((2 * v + 1) * depth, depth)] = low.astype(BF16)
+            value_ref[span, pl.ds((2 * v + 1) * depth, depth)] = low.astype(BF16)
+        value_ref[span, pl.ds(4 * depth, depth)] = count_ref[span, :].astype(BF16)
     sums = jnp.dot(hot_ref[...], value_ref[...], preferred_element_type=F32)
     old = []
     for first, count, stride in runs:
-        old.append(old_ref[pl.ds(first, count, stride=stride) if stride > 1 else pl.ds(first, count), :])
+        old.append(old_ref[pl.ds(first, count, stride=stride), :])
     logvisc, density = averages(sums, depth, jnp.concatenate(old, axis=0))
     visc_ref[...] = jnp.exp(logvisc)
     force_ref[...] = GRAVITY * (1.0 - density)
-    odd_x, odd_y = parities()
+    odd_y = parities()[1]
     for ref, is_first in ((y_even_ref, odd_y == 1), (y_odd_ref, odd_y == 0)):
-        start = pl.multiple_of(jnp.where(is_first, 4 * size_y, 4 * size_y + 2 * size_x), 8)
+        start = pl.multiple_of(jnp.where(is_first, 0, 2 * size_x), 8)
         ref[0 : 2 * size_x, :] = visc_ref[pl.ds(start, 2 * size_x), :]
         ref[2 * size_x :, :] = force_ref[pl.ds(start, size_x), :]
-    for ref, is_first in ((x_even_ref, odd_x == 1), (x_odd_ref, odd_x == 0)):
-        start = pl.multiple_of(jnp.where(is_first, 0, 2 * size_y), 8)
-        ref[0 : 2 * size_y, :] = visc_ref[pl.ds(start, 2 * size_y), :]
-        start = pl.multiple_of(jnp.where(is_first, 0, 3 * size_y), 8)
-        ref[2 * size_y : 3 * size_y, :] = force_ref[pl.ds(start, size_y), :]
-        ref[3 * size_y :, :] = jnp.zeros((CORNERS, depth), F32)
-
-    @pl.when(at_end("gx"))
-    def _():
-        x_odd_ref[...] = jnp.zeros_like(x_odd_ref)
 
     @pl.when(at_end("gy"))
     def _():
@@ -409,9 +459,11 @@
     density_ref,
     force_ref,
     visc_ref,
+    x_even_ref,
+    x_odd_ref,
     hot_ref,
 ):
-    size_y = bricks[1]
+    size_x, size_y = bricks
     wide = Wide(bricks)
     columns, depth = old_ref.shape
     names = lax.broadcasted_iota(jnp.int32, (columns, depth), 0).astype(F32)
@@ -429,22 +481,41 @@
         for k in range(depth // size_y):
             plane = tile * (depth // size_y) + k
             visc_ref[wide.plane(0, plane), :] = visc[k * size_y : (k + 1) * size_y]
+    odd_x = parities()[0]
+    for ref, is_first in ((x_even_ref, odd_x == 1), (x_odd_ref, odd_x == 0)):
+        first = jnp.where(is_first, 0, size_x - 2)
+        for k in range(2):
+            ref[k * size_y : (k + 1) * size_y, :] = visc_ref[wide.plane(0, first + k), :]
+        start = pl.multiple_of(jnp.where(is_first, 0, columns - size_y), 8)
+        ref[2 * size_y : 3 * size_y, :] = force_ref[pl.ds(start, size_y), :]
+        ref[3 * size_y :, :] = jnp.zeros((CORNERS, depth), F32)
+
+    @pl.when(at_end("gx"))
+    def _():
+        x_odd_ref[...] = jnp.zeros_like(x_odd_ref)
 
 
 def sweep_kernel(
     bricks,
     visc_in,
+    wide_in,
     force_ref,
-    wide_ref,
+    vy_low_ref,
+    vy_high_ref,
     y_even_ref,
     y_odd_ref,
     visc_ref,
+    wide_ref,
     next_ref,
     coeff_ref,
     last_ref,
 ):
     size_x, size_y = bricks
     wide = Wide(bricks)
+    for c in range(3):
+        for ref, near, far in ((vy_low_ref, -1, -2), (vy_high_ref, size_y, size_y + 1)):
+            for k, row in enumerate((near, far)):
+                wide_ref[wide.line(c, row), :] = ref[pl.ds((2 * c + k) * size_x, size_x), :]
     odd_y = parities()[1]
     rows = ((odd_y == 1, y_even_ref), (odd_y == 0, y_odd_ref))
     for is_low, ref in rows:
@@ -532,19 +603,26 @@
 
 
 def corner_kernel(
-    bricks, even_in, odd_in, y_even_ref, y_odd_ref, wide_ref, x_even_ref, x_odd_ref
+    bricks,
+    even_in,
+    odd_in,
+    y_even_ref,
+    y_odd_ref,
+    vy_low_ref,
+    vy_high_ref,
+    x_even_ref,
+    x_odd_ref,
 ):
     size_x, size_y = bricks
-    wide = Wide(bricks)
     odd_x, odd_y = parities()
     for ref, is_first in ((x_even_ref, odd_x == 1), (x_odd_ref, odd_x == 0)):
         near = jnp.where(is_first, 0, size_x - 1)
         pair = (y_even_ref[pl.ds(near, 1), :], y_odd_ref[pl.ds(near, 1), :])
-        for k, row in enumerate((-1, size_y)):
+        for k, lines_ref in enumerate((vy_low_ref, vy_high_ref)):
             at = 3 * size_y + 4 * k
             ref[at : at + 1, :] = jnp.where(odd_y == 1 - k, *pair)
             for c in range(3):
-                ref[at + 1 + c : at + 2 + c, :] = wide_ref[wide.cell(c, near, row), :]
+                ref[at + 1 + c : at + 2 + c, :] = lines_ref[pl.ds(2 * c * size_x + near, 1), :]
 
     @pl.when(at_end("gx"))
     def _():
@@ -583,6 +661,11 @@
     return lax.ppermute(value, BOTH, pairs)
 
 
+def crossed(value, axis, bits):
+    pairs = [(i, i ^ bits) for i in range(lax.axis_size(axis))]
+    return lax.ppermute(value, axis, pairs)
+
+
 def per_device(
     marker_comp, marker_strain, marker_live, marker_cell, block_dest, old_logvisc, velocity
 ):
@@ -593,39 +676,81 @@
     size_x, size_y, depth = old_logvisc.shape
     columns = size_x * size_y
     slots = 2 * blocks // devices
-    chunk = 3 * slots + 1
+    chunk = 2 * slots + 1
     total = devices * slots
     lines = (blocks // marks, marks)
-
+    counts = (count_x, count_y)
+
+    def shape(rows, width=depth, kind=F32):
+        return jax.ShapeDtypeStruct((rows, width), kind)
+
+    def buffers(kinds):
+        return [pltpu.VMEM((blocks, marks), kind) for kind in kinds]
+
+    live, cell = in_hbm(marker_live), in_hbm(marker_cell)
+    *planes, places, ids = pl.pallas_call(
+        functools.partial(count_kernel, slots, chunk, counts),
+        out_shape=(
+            *(shape(count_x * slots),) * count_y,
+            shape(*lines, jnp.int32),
+            shape(devices),
+        ),
+        in_specs=[HBM] * 3,
+        out_specs=(VMEM,) * (count_y + 2),
+        scratch_shapes=[
+            pltpu.VMEM((total, marks), F32),
+            pltpu.SMEM(lines, jnp.int32),
+            pltpu.VMEM(lines, jnp.int32),
+            pltpu.VMEM((16 * BATCH, marks), F32),
+            pltpu.SemaphoreType.DMA,
+            pltpu.VMEM(lines, jnp.int32),
+            *buffers((jnp.int32, jnp.int32)),
+            pltpu.SemaphoreType.DMA((3,)),
+        ],
+        compiler_params=limit(12),
+        name="count",
+    )(in_hbm(block_dest.reshape(lines)), live, cell)
+    for k in range(1, count_y):
+        planes[k] = crossed(planes[k], "gy", k)
     payload = pl.pallas_call(
         functools.partial(pack_kernel, slots, chunk),
-        out_shape=jax.ShapeDtypeStruct((devices * chunk, marks), F32),
-        in_specs=[HBM] * 5,
+        out_shape=shape(devices * chunk),
+        in_specs=[HBM] * 4 + [VMEM] * 2,
         out_specs=VMEM,
         scratch_shapes=[
             pltpu.SMEM(lines, jnp.int32),
-            pltpu.VMEM(lines, jnp.int32),
-            pltpu.VMEM((48 * BATCH, marks), F32),
+            pltpu.VMEM((32 * BATCH, marks), F32),
             pltpu.SemaphoreType.DMA,
-            pltpu.VMEM(lines, jnp.int32),
-            pltpu.VMEM((blocks, marks), F32),
-            pltpu.VMEM((blocks, marks), F32),
-            pltpu.VMEM((blocks, marks), jnp.int32),
-            pltpu.VMEM((blocks, marks), jnp.int32),
-            pltpu.SemaphoreType.DMA((5,)),
+            *buffers((F32, F32, jnp.int32, jnp.int32)),
+            pltpu.SemaphoreType.DMA((4,)),
         ],
         compiler_params=limit(12),
+        cost_estimate=pl.CostEstimate(flops=10**11, bytes_accessed=1, transcendentals=0),
         name="pack",
-    )(
-        in_hbm(block_dest.reshape(lines)),
-        in_hbm(marker_comp),
-        in_hbm(marker_strain),
-        in_hbm(marker_live),
-        in_hbm(marker_cell),
-    )
+    )(in_hbm(marker_comp), in_hbm(marker_strain), live, cell, places, ids)
     payload = payload.reshape(devices * chunk, 1, marks)
     received = lax.all_to_all(payload, BOTH, split_axis=0, concat_axis=0, tiled=True)
     received = received.reshape(devices * chunk, marks)
+
+    messages = pl.pallas_call(
+        functools.partial(regroup_kernel, slots, counts),
+        out_shape=(shape(count_y * slots),) * count_x,
+        in_specs=[VMEM] * count_y,
+        out_specs=(VMEM,) * count_x,
+        compiler_params=limit(4),
+        cost_estimate=pl.CostEstimate(flops=10**11, bytes_accessed=1, transcendentals=0),
+        name="regroup",
+    )(*planes)
+    messages, velocity = lax.optimization_barrier((messages, velocity))
+    messages = [crossed(m, "gx", k) if k else m for k, m in enumerate(messages)]
+    gathered = pl.pallas_call(
+        functools.partial(gather_kernel, slots, counts),
+        out_shape=shape(total),
+        in_specs=[VMEM] * count_x,
+        out_specs=VMEM,
+        compiler_params=limit(4),
+        name="gather",
+    )(*messages)
 
     def y_lines(near, far):
         pair = jnp.concatenate([velocity[:, :, near], velocity[:, :, far]], axis=1)
@@ -641,9 +766,6 @@
 
     bricks = (size_x, size_y)
     wide = Wide(bricks)
-
-    def shape(rows, width=depth, kind=F32):
-        return jax.ShapeDtypeStruct((rows, width), kind)
 
     wide_vel = pl.pallas_call(
         functools.partial(widen_kernel, bricks),
@@ -653,65 +775,68 @@
         compiler_params=limit(8),
         name="widen",
     )(velocity.reshape(3 * columns, depth), vx_low, vx_high)
-    received, wide_vel = lax.optimization_barrier((received, wide_vel))
-
-    edge = 4 * (size_x + size_y)
+    received, wide_vel, gathered = lax.optimization_barrier((received, wide_vel, gathered))
+
+    edge = 4 * size_x
     x_side, y_side = shape(3 * size_y + CORNERS), shape(3 * size_x)
     old = old_logvisc.reshape(columns, depth)
-    x_even, x_odd, y_even, y_odd, values, ids, wide_vel = pl.pallas_call(
+    y_even, y_odd, values, ids = pl.pallas_call(
         functools.partial(edge_kernel, slots, chunk, bricks),
         out_shape=(
-            *(x_side, x_side, y_side, y_side),
+            *(y_side, y_side),
             shape(total, 5 * depth, BF16),
             shape(total // depth),
-            shape(3 * wide.field),
         ),
-        in_specs=[VMEM] * 5,
-        out_specs=(VMEM,) * 7,
-        input_output_aliases={4: 6},
+        in_specs=[VMEM] * 3,
+        out_specs=(VMEM,) * 4,
         scratch_shapes=[
             pltpu.VMEM((edge, total), BF16),
             pltpu.VMEM((edge, depth), F32),
             pltpu.VMEM((edge, depth), F32),
         ],
         compiler_params=limit(16),
+        cost_estimate=pl.CostEstimate(flops=1, bytes_accessed=1, transcendentals=0),
         name="edge",
-    )(received, old, vy_low, vy_high, wide_vel)
-    logvisc, density, force, visc = pl.pallas_call(
+    )(received, gathered, old)
+    logvisc, density, force, visc, x_even, x_odd = pl.pallas_call(
         functools.partial(interior_kernel, bricks),
-        out_shape=(*(shape(columns),) * 3, shape(wide.field)),
+        out_shape=(*(shape(columns),) * 3, shape(wide.field), x_side, x_side),
         in_specs=[VMEM] * 3,
-        out_specs=(VMEM,) * 4,
+        out_specs=(VMEM,) * 6,
         scratch_shapes=[pltpu.VMEM((columns, total), BF16)],
         compiler_params=limit(16),
+        cost_estimate=pl.CostEstimate(flops=1, bytes_accessed=1, transcendentals=0),
         name="interior",
     )(values, ids, old)
     y_even = swapped(y_even, "gy", 0)
     y_odd = swapped(y_odd, "gy", 1)
-    y_even, y_odd, visc, force = lax.optimization_barrier((y_even, y_odd, visc, force))
+    y_even, y_odd, visc, force, x_even, x_odd = lax.optimization_barrier(
+        (y_even, y_odd, visc, force, x_even, x_odd)
+    )
     x_even, x_odd = pl.pallas_call(
         functools.partial(corner_kernel, bricks),
         out_shape=(x_side, x_side),
-        in_specs=[VMEM] * 5,
+        in_specs=[VMEM] * 6,
         out_specs=(VMEM, VMEM),
         input_output_aliases={0: 0, 1: 1},
         compiler_params=limit(4),
         name="corners",
-    )(x_even, x_odd, y_even, y_odd, wide_vel)
-    visc, wide_next, coeff, last = pl.pallas_call(
+    )(x_even, x_odd, y_even, y_odd, vy_low, vy_high)
+    visc, wide_vel, wide_next, coeff, last = pl.pallas_call(
         functools.partial(sweep_kernel, bricks),
         out_shape=(
             shape(wide.field),
             shape(3 * wide.field),
+            shape(3 * wide.field),
             shape(7 * columns),
             shape(3 * columns),
         ),
-        in_specs=[VMEM] * 5,
-        out_specs=(VMEM,) * 4,
-        input_output_aliases={0: 0},
+        in_specs=[VMEM] * 7,
+        out_specs=(VMEM,) * 5,
+        input_output_aliases={0: 0, 1: 1},
         compiler_params=limit(12),
         name="sweep",
-    )(visc, force, wide_vel, y_even, y_odd)
+    )(visc, wide_vel, force, vy_low, vy_high, y_even, y_odd)
     x_even = swapped(x_even, "gx", 0)
     x_odd = swapped(x_odd, "gx", 1)
     smoothed = pl.pallas_call(

time: 61.2 us -> 57.5 us (0.940)
  waiting for transfers between devices: 24.9 us -> 10.7 us
  starting transfers between devices: 21.4 us -> 32.9 us
  local copies, waits for them, and re-layouts: 3.41 us -> 0.54 us
  Pallas kernels: 9.45 us -> 11.7 us
    all_to_all x1, waiting for transfers between devices: 21 us -> 1.57 us  [per_device(): lax.all_to_all(payload, BOTH, split_axis=0, concat_axis=0, tiled=True)]
    ppermute x0 -> x10, starting transfers between devices: none -> 8.69 us  [crossed(): return lax.ppermute(value, axis, pairs)]
    ppermute x0 -> x10, waiting for transfers between devices: none -> 5.9 us  [crossed(): return lax.ppermute(value, axis, pairs)]
    pallas_call x1 -> x4, Pallas kernels: 4.62 us -> 6.94 us  [the longest x1 3.86 us: per_device(): pl.pallas_call(functools.partial(pack_kernel, slots, chunk), out_shape=sh...]
    ppermute x4, starting transfers between devices: 2.95 us -> 5.03 us  [swapped(): return lax.ppermute(value, BOTH, pairs)]
    slice x1, local copies, waits for them, and re-layouts: 1.31 us -> 0.05 us  [y_lines(): pair = jnp.concatenate([velocity[:, :, near], velocity[:, :, far]], axis=1)]
    unnamed x4, local copies, waits for them, and re-layouts: 1.13 us -> 0.01 us
    slice x1, local copies, waits for them, and re-layouts: 0.96 us -> 0.02 us  [x_planes(): return velocity[:, first:first + 2].reshape(6 * size_y, depth)]
  transfers between devices with their start and end apart: 9 -> 19, of which waited for: 5 -> 5; matrix products, arithmetic and copies ran while one was open for 4% -> 1% of each run, Pallas kernels for 5% -> 13%
where the time goes in v5:
time: 57.5 us; the launch traced here: 56.8 us
  starting transfers between devices  32.9 us (57%)
  Pallas kernels  11.7 us (20%)
  waiting for transfers between devices  10.7 us (19%)
  between operations  0.91 us (2%)
    ppermute x4, starting transfers between devices, shifted(): return lax.ppermute(value, axis, pairs)  12.3 us
    ppermute x10, starting transfers between devices, crossed(): return lax.ppermute(value, axis, pairs)  8.69 us
    all_to_all x1, starting transfers between devices, per_device(): lax.all_to_all(payload, BOTH, split_axis=0, concat_axis=0, tiled=True)  6.9 us
    ppermute x10, waiting for transfers between devices, crossed(): return lax.ppermute(value, axis, pairs)  5.9 us
    ppermute x4, starting transfers between devices, swapped(): return lax.ppermute(value, BOTH, pairs)  5.03 us
    pallas_call x1, Pallas kernels, per_device(): pl.pallas_call(functools.partial(pack_kernel, slots, chunk), out_shape=sh...  3.86 us
    ppermute x4, waiting for transfers between devices, swapped(): return lax.ppermute(value, BOTH, pairs)  3.27 us
    pallas_call x1, Pallas kernels, per_device(): pl.pallas_call(functools.partial(count_kernel, slots, chunk, counts), out...  2.97 us
  transfers between devices with their start and end apart: 19, of which 5 were waited for; matrix products, arithmetic and copies ran while one was open for 1% of the time, Pallas kernels for 13%

profile of v5, /device:TPU:12, one launch (start us, length us, event | category | flops | bytes accessed | tf_op | source)
XLA Modules:
  0.0 56.8 jit_solution(2021009453193697524)
XLA Ops:
  0.6 3.0 %count.1 = (f32[256,128]{1,0:T(8,128)S(1)}, f32[256,128]{1,0:T(8,128)S(1)}, f32[256,128]{1,0:T(8,128)S(1)}, f32[256,128]{1,0:T(8,128)S(1)}, s32[4,128]{1,0:T(4,128)S(1)}, /*index=5*/f32[32,128]{1,0:T(8,128)S(1)}) custom-call(s32[4,128]{1,0:T(4,128)} %bitcast.29, s32[512,128]{1,0:T(8,128)} %live_hbm.3, s32[512,128]{1,0:T(8,128)} %cell_hbm.3), custom_call_target="tpu_custom_call" | custom-call | tf_op jit(solution)/shard_map/count/pallas_call | solution.py:691
  3.6 0.5 collective-permute-start
  4.1 2.6 %collective-permute-start.1 = (f32[256,128]{1,0:T(8,128)S(1)}, f32[256,128]{1,0:T(8,128)S(1)}, u32[]{:S(2)}, u32[]{:S(2)}) collective-permute-start(f32[256,128]{1,0:T(8,128)S(1)} %get-tuple-element.57), channel_id=1, source_target_pairs={{0,2},{1,3},{2,0},{3,1},{4,6},{5,7},{6,4},{7,5},{8,10},{9,11},{10,... | collective-permute-start | bytes 393224 | tf_op jit(solution)/shard_map/ppermute | solution.py:666
  6.7 0.4 collective-permute-start.2
  7.2 3.9 %pack.1 = f32[2080,128]{1,0:T(8,128)} custom-call(f32[512,128]{1,0:T(8,128)} %comp_hbm.1, f32[512,128]{1,0:T(8,128)} %strain_hbm.1, s32[512,128]{1,0:T(8,128)} %live_hbm.3, s32[512,128]{1,0:T(8,128)} %cell_hbm.3, s32[4,128]{1,0:T(4,128)S(1)} %get-tuple-element.53.line_ref, f32[32,128]{1,0:T(8,128)S(1)} %get-tuple-element.54.ids_ref), custom_call_target="tpu_custom_call" | custom-call | flops 99999997952 | bytes 1 | tf_op jit(solution)/shard_map/pack/pallas_call | solution.py:715
  11.0 6.9 %all-to-all-start = ((f32[2080,1,128]{2,1,0:T(1,128)}), f32[2080,1,128]{2,1,0:T(1,128)S(1)}, u32[]{:S(2)}, u32[]{:S(2)}) async-start(f32[2080,1,128]{2,1,0:T(1,128)} %bitcast.2), calls=%async_computation | async-start | bytes 2129920 | tf_op jit(solution)/shard_map/all_to_all | solution.py:732
  17.9 0.0 collective-permute-done.refs_1_
  17.9 0.0 collective-permute-done.1.refs_2_
  18.0 0.6 %collective-permute-done.2.refs_3_ = f32[256,128]{1,0:T(8,128)S(1)} collective-permute-done((f32[256,128]{1,0:T(8,128)S(1)}, f32[256,128]{1,0:T(8,128)S(1)}, u32[]{:S(2)}, u32[]{:S(2)}) %collective-permute-start.2) | collective-permute-done | bytes 131104 | tf_op jit(solution)/shard_map/ppermute | solution.py:666
  18.6 0.0 copy-start
  18.6 0.1 collective-permute-start.5
  18.7 1.6 %collective-permute-start.6 = (f32[128,128]{1,0:T(8,128)S(1)}, f32[128,128]{1,0:T(8,128)S(1)}, u32[]{:S(2)}, u32[]{:S(2)}) collective-permute-start(f32[128,128]{1,0:T(8,128)S(1)} %get-tuple-element.70), channel_id=1, source_target_pairs={{0,8},{4,12},{8,0},{12,4},{16,24},{20,28},{24,16},{28,20},{1,9},{5... | collective-permute-start | bytes 196616 | tf_op jit(solution)/shard_map/ppermute | solution.py:666
  20.2 0.3 collective-permute-start.7
  20.5 0.5 collective-permute-start.8
  21.1 1.2 %collective-permute-start.9 = (f32[128,128]{1,0:T(8,128)S(1)}, f32[128,128]{1,0:T(8,128)S(1)}, u32[]{:S(2)}, u32[]{:S(2)}) collective-permute-start(f32[128,128]{1,0:T(8,128)S(1)} %get-tuple-element.73), channel_id=1, source_target_pairs={{0,20},{4,16},{8,28},{12,24},{16,4},{20,0},{24,12},{28,8},{1,21},{... | collective-permute-start | bytes 196616 | tf_op jit(solution)/shard_map/ppermute | solution.py:666
  22.2 0.0 copy-done
  22.2 0.5 copy.22
  22.8 0.0 collective-permute-done.5.refs_1_
  22.8 1.5 %collective-permute-start.10 = (f32[128,128]{1,0:T(8,128)S(1)}, f32[128,128]{1,0:T(8,128)S(1)}, u32[]{:S(2)}, u32[]{:S(2)}) collective-permute-start(f32[128,128]{1,0:T(8,128)S(1)} %get-tuple-element.74), channel_id=1, source_target_pairs={{0,24},{4,28},{8,16},{12,20},{16,8},{20,12},{24,0},{28,4},{1,25},{... | collective-permute-start | bytes 196616 | tf_op jit(solution)/shard_map/ppermute | solution.py:666
  24.3 3.5 %collective-permute-done.6.refs_2_ = f32[128,128]{1,0:T(8,128)S(1)} collective-permute-done((f32[128,128]{1,0:T(8,128)S(1)}, f32[128,128]{1,0:T(8,128)S(1)}, u32[]{:S(2)}, u32[]{:S(2)}) %collective-permute-start.6) | collective-permute-done | bytes 65568 | tf_op jit(solution)/shard_map/ppermute | solution.py:666
  27.8 0.0 collective-permute-start.11
  27.8 1.8 %collective-permute-done.7.refs_3_ = f32[128,128]{1,0:T(8,128)S(1)} collective-permute-done((f32[128,128]{1,0:T(8,128)S(1)}, f32[128,128]{1,0:T(8,128)S(1)}, u32[]{:S(2)}, u32[]{:S(2)}) %collective-permute-start.7) | collective-permute-done | bytes 65568 | tf_op jit(solution)/shard_map/ppermute | solution.py:666
  29.6 3.0 %collective-permute-start.3 = (f32[192,128]{1,0:T(8,128)S(1)}, f32[192,128]{1,0:T(8,128)S(1)}, u32[]{:S(2)}, u32[]{:S(2)}) collective-permute-start(f32[192,128]{1,0:T(8,128)S(1)} %bitcast.24), channel_id=1, source_target_pairs={{0,4},{4,8},{8,12},{12,16},{16,20},{20,24},{24,28},{1,5},{5,9},{9,... | collective-permute-start | bytes 294920 | tf_op jit(solution)/shard_map/ppermute | solution.py:643
  32.6 0.0 collective-permute-done.8.refs_4_
  32.6 3.5 %collective-permute-start.4 = (f32[192,128]{1,0:T(8,128)S(1)}, f32[192,128]{1,0:T(8,128)S(1)}, u32[]{:S(2)}, u32[]{:S(2)}) collective-permute-start(f32[192,128]{1,0:T(8,128)S(1)} %bitcast.23), channel_id=1, source_target_pairs={{4,0},{8,4},{12,8},{16,12},{20,16},{24,20},{28,24},{5,1},{9,5},{13... | collective-permute-start | bytes 294920 | tf_op jit(solution)/shard_map/ppermute | solution.py:643
  36.1 0.0 collective-permute-done.9.refs_5_
  36.1 2.7 %collective-permute-start.14 = (f32[96,128]{1,0:T(8,128)S(1)}, f32[96,128]{1,0:T(8,128)S(1)}, u32[]{:S(2)}, u32[]{:S(2)}) collective-permute-start(f32[96,128]{1,0:T(8,128)S(1)} %bitcast.28), channel_id=1, source_target_pairs={{0,1},{1,2},{2,3},{4,5},{5,6},{6,7},{8,9},{9,10},{10,11},{12,13},{... | collective-permute-start | bytes 147464 | tf_op jit(solution)/shard_map/ppermute | solution.py:643
  38.8 0.0 collective-permute-done.10.refs_6_
  38.8 3.1 %collective-permute-start.15 = (f32[96,128]{1,0:T(8,128)S(1)}, f32[96,128]{1,0:T(8,128)S(1)}, u32[]{:S(2)}, u32[]{:S(2)}) collective-permute-start(f32[96,128]{1,0:T(8,128)S(1)} %bitcast.27), channel_id=1, source_target_pairs={{1,0},{2,1},{3,2},{5,4},{6,5},{7,6},{9,8},{10,9},{11,10},{13,12},{... | collective-permute-start | bytes 147464 | tf_op jit(solution)/shard_map/ppermute | solution.py:643
  42.0 0.0 collective-permute-done.11.refs_7_
  42.0 0.1 gather.1.count_ref
  42.1 0.0 copy-start.1
  42.1 0.0 collective-permute-done.3.vx_low_ref
  42.1 0.0 collective-permute-done.4.vx_high_ref
  42.1 0.1 widen.1.wide_in
  42.2 1.6 %all-to-all-done = f32[2080,1,128]{2,1,0:T(1,128)S(1)} async-done(((f32[2080,1,128]{2,1,0:T(1,128)}), f32[2080,1,128]{2,1,0:T(1,128)S(1)}, u32[]{:S(2)}, u32[]{:S(2)}) %all-to-all-start) | async-done | bytes 1064992 | tf_op jit(solution)/shard_map/all_to_all | solution.py:732
  43.7 0.0 copy-done.1
  43.7 0.5 edge.1
  44.3 0.1 collective-permute-start.12
  44.4 4.8 %collective-permute-start.13 = (f32[48,128]{1,0:T(8,128)S(1)}, f32[48,128]{1,0:T(8,128)S(1)}, u32[]{:S(2)}, u32[]{:S(2)}) collective-permute-start(f32[48,128]{1,0:T(8,128)S(1)} %get-tuple-element.83), channel_id=1, source_target_pairs={{0,4},{4,0},{8,12},{12,8},{16,20},{20,16},{24,28},{28,24},{1,2},{5... | collective-permute-start | bytes 73736 | tf_op jit(solution)/shard_map/ppermute | solution.py:661
  49.2 1.8 %interior.1 = (f32[512,128]{1,0:T(8,128)}, f32[512,128]{1,0:T(8,128)}, f32[512,128]{1,0:T(8,128)S(1)}, f32[960,128]{1,0:T(8,128)S(1)}, f32[104,128]{1,0:T(8,128)S(1)}, /*index=5*/f32[104,128]{1,0:T(8,128)S(1)}) custom-call(bf16[1024,640]{1,0:T(8,128)(2,1)S(1)} %get-tuple-element.78.value_ref, f32[8,128]{1,0:T(8,128)S(1)} %get-tuple-element.79.ids_ref, ...), custom_call_target="tpu_custom_call" | custom-call | flops 1 | bytes 1 | tf_op jit(solution)/shard_map/interior/pallas_call | solution.py:801
  51.0 0.0 collective-permute-done.12.y_even_ref
  51.0 0.0 collective-permute-done.13.y_odd_ref
  51.0 0.0 collective-permute-done.14.vy_low_ref
  51.0 0.0 collective-permute-done.15.vy_high_ref
  51.1 0.1 collective-permute-start.16
  51.1 0.1 collective-permute-start.17
  51.2 1.2 %sweep.1 = (f32[960,128]{1,0:T(8,128)S(1)}, f32[2880,128]{1,0:T(8,128)S(1)}, f32[2880,128]{1,0:T(8,128)S(1)}, f32[3584,128]{1,0:T(8,128)S(1)}, f32[1536,128]{1,0:T(8,128)S(1)}) custom-call(f32[960,128]{1,0:T(8,128)S(1)} %get-tuple-element.88.visc_in, f32[2880,128]{1,0:T(8,128)S(1)} %widen.1.wide_in, ...), custom_call_target="tpu_custom_call", output_to_operand_aliasing={{0}: (0, {}), {1}: (1, {})} | custom-call | tf_op jit(solution)/shard_map/sweep/pallas_call | solution.py:825
  52.4 0.0 collective-permute-done.16.x_even_ref
  52.4 3.3 %collective-permute-done.17.x_odd_ref = f32[104,128]{1,0:T(8,128)S(1)} collective-permute-done((f32[104,128]{1,0:T(8,128)S(1)}, f32[104,128]{1,0:T(8,128)S(1)}, u32[]{:S(2)}, u32[]{:S(2)}) %collective-permute-start.17) | collective-permute-done | bytes 53280 | tf_op jit(solution)/shard_map/ppermute | solution.py:661
  55.7 1.1 %finish.1 = (f32[3,16,32,128]{3,2,1,0:T(8,128)}, f32[960,128]{1,0:T(8,128)S(1)}, f32[2880,128]{1,0:T(8,128)S(1)}, f32[3584,128]{1,0:T(8,128)S(1)}, f32[1536,128]{1,0:T(8,128)S(1)}, /*index=5*/f32[2880,128]{1,0:T(8,128)S(1)}) custom-call(f32[960,128]{1,0:T(8,128)S(1)} %get-tuple-element.93.vis, ...), custom_call_target="tpu_custom_call", output_to_operand_aliasing={{1}: (0, {}), {2}: (1, {}), {3}: (2, {}), {4}: (3, {}), {5}... | custom-call | tf_op jit(solution)/shard_map/finish/pallas_call | solution.py:842
  (7 shorter events, 0.1 us)
Async XLA Ops:
  3.6 14.3 %collective-permute-start = (f32[256,128]{1,0:T(8,128)S(1)}, f32[256,128]{1,0:T(8,128)S(1)}, u32[]{:S(2)}, u32[]{:S(2)}) collective-permute-start(f32[256,128]{1,0:T(8,128)S(1)} %get-tuple-element.56), channel_id=1, source_target_pairs={{0,1},{1,0},{2,3},{3,2},{4,5},{5,4},{6,7},{7,6},{8,9},{9,8},{10,11... | collective-permute-start | bytes 393224 | tf_op jit(solution)/shard_map/ppermute | solution.py:666
  4.1 13.8 %collective-permute-start.1 = (f32[256,128]{1,0:T(8,128)S(1)}, f32[256,128]{1,0:T(8,128)S(1)}, u32[]{:S(2)}, u32[]{:S(2)}) collective-permute-start(f32[256,128]{1,0:T(8,128)S(1)} %get-tuple-element.57), channel_id=1, source_target_pairs={{0,2},{1,3},{2,0},{3,1},{4,6},{5,7},{6,4},{7,5},{8,10},{9,11},{10,... | collective-permute-start | bytes 393224 | tf_op jit(solution)/shard_map/ppermute | solution.py:666
  6.7 11.8 %collective-permute-start.2 = (f32[256,128]{1,0:T(8,128)S(1)}, f32[256,128]{1,0:T(8,128)S(1)}, u32[]{:S(2)}, u32[]{:S(2)}) collective-permute-start(f32[256,128]{1,0:T(8,128)S(1)} %get-tuple-element.58), channel_id=1, source_target_pairs={{0,3},{1,2},{2,1},{3,0},{4,7},{5,6},{6,5},{7,4},{8,11},{9,10},{10,... | collective-permute-start | bytes 393224 | tf_op jit(solution)/shard_map/ppermute | solution.py:666
  11.0 32.7 %all-to-all-start = ((f32[2080,1,128]{2,1,0:T(1,128)}), f32[2080,1,128]{2,1,0:T(1,128)S(1)}, u32[]{:S(2)}, u32[]{:S(2)}) async-start(f32[2080,1,128]{2,1,0:T(1,128)} %bitcast.2), calls=%async_computation | async-start | bytes 2129920 | tf_op jit(solution)/shard_map/all_to_all | solution.py:732
  18.6 3.7 %copy-start = (f32[3,16,32,128]{3,2,1,0:T(8,128)S(1)}, f32[3,16,32,128]{3,2,1,0:T(8,128)}, u32[]{:S(2)}) copy-start(f32[3,16,32,128]{3,2,1,0:T(8,128)} %param.13) | copy-start | bytes 2359300
  18.6 4.2 %collective-permute-start.5 = (f32[128,128]{1,0:T(8,128)S(1)}, f32[128,128]{1,0:T(8,128)S(1)}, u32[]{:S(2)}, u32[]{:S(2)}) collective-permute-start(f32[128,128]{1,0:T(8,128)S(1)} %get-tuple-element.69), channel_id=1, source_target_pairs={{0,4},{4,0},{8,12},{12,8},{16,20},{20,16},{24,28},{28,24},{1,5},{5... | collective-permute-start | bytes 196616 | tf_op jit(solution)/shard_map/ppermute | solution.py:666
  18.7 9.1 %collective-permute-start.6 = (f32[128,128]{1,0:T(8,128)S(1)}, f32[128,128]{1,0:T(8,128)S(1)}, u32[]{:S(2)}, u32[]{:S(2)}) collective-permute-start(f32[128,128]{1,0:T(8,128)S(1)} %get-tuple-element.70), channel_id=1, source_target_pairs={{0,8},{4,12},{8,0},{12,4},{16,24},{20,28},{24,16},{28,20},{1,9},{5... | collective-permute-start | bytes 196616 | tf_op jit(solution)/shard_map/ppermute | solution.py:666
  20.2 9.4 %collective-permute-start.7 = (f32[128,128]{1,0:T(8,128)S(1)}, f32[128,128]{1,0:T(8,128)S(1)}, u32[]{:S(2)}, u32[]{:S(2)}) collective-permute-start(f32[128,128]{1,0:T(8,128)S(1)} %get-tuple-element.71), channel_id=1, source_target_pairs={{0,12},{4,8},{8,4},{12,0},{16,28},{20,24},{24,20},{28,16},{1,13},{... | collective-permute-start | bytes 196616 | tf_op jit(solution)/shard_map/ppermute | solution.py:666
  20.5 12.0 %collective-permute-start.8 = (f32[128,128]{1,0:T(8,128)S(1)}, f32[128,128]{1,0:T(8,128)S(1)}, u32[]{:S(2)}, u32[]{:S(2)}) collective-permute-start(f32[128,128]{1,0:T(8,128)S(1)} %get-tuple-element.72), channel_id=1, source_target_pairs={{0,16},{4,20},{8,24},{12,28},{16,0},{20,4},{24,8},{28,12},{1,17},{... | collective-permute-start | bytes 196616 | tf_op jit(solution)/shard_map/ppermute | solution.py:666
  21.1 15.0 %collective-permute-start.9 = (f32[128,128]{1,0:T(8,128)S(1)}, f32[128,128]{1,0:T(8,128)S(1)}, u32[]{:S(2)}, u32[]{:S(2)}) collective-permute-start(f32[128,128]{1,0:T(8,128)S(1)} %get-tuple-element.73), channel_id=1, source_target_pairs={{0,20},{4,16},{8,28},{12,24},{16,4},{20,0},{24,12},{28,8},{1,21},{... | collective-permute-start | bytes 196616 | tf_op jit(solution)/shard_map/ppermute | solution.py:666
  22.8 16.0 %collective-permute-start.10 = (f32[128,128]{1,0:T(8,128)S(1)}, f32[128,128]{1,0:T(8,128)S(1)}, u32[]{:S(2)}, u32[]{:S(2)}) collective-permute-start(f32[128,128]{1,0:T(8,128)S(1)} %get-tuple-element.74), channel_id=1, source_target_pairs={{0,24},{4,28},{8,16},{12,20},{16,8},{20,12},{24,0},{28,4},{1,25},{... | collective-permute-start | bytes 196616 | tf_op jit(solution)/shard_map/ppermute | solution.py:666
  27.8 14.2 %collective-permute-start.11 = (f32[128,128]{1,0:T(8,128)S(1)}, f32[128,128]{1,0:T(8,128)S(1)}, u32[]{:S(2)}, u32[]{:S(2)}) collective-permute-start(f32[128,128]{1,0:T(8,128)S(1)} %get-tuple-element.75), channel_id=1, source_target_pairs={{0,28},{4,24},{8,20},{12,16},{16,12},{20,8},{24,4},{28,0},{1,29},{... | collective-permute-start | bytes 196616 | tf_op jit(solution)/shard_map/ppermute | solution.py:666
  29.6 12.5 %collective-permute-start.3 = (f32[192,128]{1,0:T(8,128)S(1)}, f32[192,128]{1,0:T(8,128)S(1)}, u32[]{:S(2)}, u32[]{:S(2)}) collective-permute-start(f32[192,128]{1,0:T(8,128)S(1)} %bitcast.24), channel_id=1, source_target_pairs={{0,4},{4,8},{8,12},{12,16},{16,20},{20,24},{24,28},{1,5},{5,9},{9,... | collective-permute-start | bytes 294920 | tf_op jit(solution)/shard_map/ppermute | solution.py:643
  32.6 9.5 %collective-permute-start.4 = (f32[192,128]{1,0:T(8,128)S(1)}, f32[192,128]{1,0:T(8,128)S(1)}, u32[]{:S(2)}, u32[]{:S(2)}) collective-permute-start(f32[192,128]{1,0:T(8,128)S(1)} %bitcast.23), channel_id=1, source_target_pairs={{4,0},{8,4},{12,8},{16,12},{20,16},{24,20},{28,24},{5,1},{9,5},{13... | collective-permute-start | bytes 294920 | tf_op jit(solution)/shard_map/ppermute | solution.py:643
  36.1 14.9 %collective-permute-start.14 = (f32[96,128]{1,0:T(8,128)S(1)}, f32[96,128]{1,0:T(8,128)S(1)}, u32[]{:S(2)}, u32[]{:S(2)}) collective-permute-start(f32[96,128]{1,0:T(8,128)S(1)} %bitcast.28), channel_id=1, source_target_pairs={{0,1},{1,2},{2,3},{4,5},{5,6},{6,7},{8,9},{9,10},{10,11},{12,13},{... | collective-permute-start | bytes 147464 | tf_op jit(solution)/shard_map/ppermute | solution.py:643
  38.8 12.2 %collective-permute-start.15 = (f32[96,128]{1,0:T(8,128)S(1)}, f32[96,128]{1,0:T(8,128)S(1)}, u32[]{:S(2)}, u32[]{:S(2)}) collective-permute-start(f32[96,128]{1,0:T(8,128)S(1)} %bitcast.27), channel_id=1, source_target_pairs={{1,0},{2,1},{3,2},{5,4},{6,5},{7,6},{9,8},{10,9},{11,10},{13,12},{... | collective-permute-start | bytes 147464 | tf_op jit(solution)/shard_map/ppermute | solution.py:643
  42.1 1.7 %copy-start.1 = (f32[16,32,128]{2,1,0:T(8,128)S(1)}, f32[16,32,128]{2,1,0:T(8,128)}, u32[]{:S(2)}) copy-start(f32[16,32,128]{2,1,0:T(8,128)} %param.12) | copy-start | bytes 786436
  44.3 6.7 %collective-permute-start.12 = (f32[48,128]{1,0:T(8,128)S(1)}, f32[48,128]{1,0:T(8,128)S(1)}, u32[]{:S(2)}, u32[]{:S(2)}) collective-permute-start(f32[48,128]{1,0:T(8,128)S(1)} %get-tuple-element.82), channel_id=1, source_target_pairs={{0,1},{4,5},{8,9},{12,13},{16,17},{20,21},{24,25},{28,29},{1,0},{5... | collective-permute-start | bytes 73736 | tf_op jit(solution)/shard_map/ppermute | solution.py:661
  44.4 6.7 %collective-permute-start.13 = (f32[48,128]{1,0:T(8,128)S(1)}, f32[48,128]{1,0:T(8,128)S(1)}, u32[]{:S(2)}, u32[]{:S(2)}) collective-permute-start(f32[48,128]{1,0:T(8,128)S(1)} %get-tuple-element.83), channel_id=1, source_target_pairs={{0,4},{4,0},{8,12},{12,8},{16,20},{20,16},{24,28},{28,24},{1,2},{5... | collective-permute-start | bytes 73736 | tf_op jit(solution)/shard_map/ppermute | solution.py:661
  51.1 1.3 %collective-permute-start.16 = (f32[104,128]{1,0:T(8,128)S(1)}, f32[104,128]{1,0:T(8,128)S(1)}, u32[]{:S(2)}, u32[]{:S(2)}) collective-permute-start(f32[104,128]{1,0:T(8,128)S(1)} %get-tuple-element.100), channel_id=1, source_target_pairs={{0,4},{1,5},{2,6},{3,7},{4,0},{5,1},{6,2},{7,3},{8,12},{9,13},{10,... | collective-permute-start | bytes 159752 | tf_op jit(solution)/shard_map/ppermute | solution.py:661
  51.1 4.5 %collective-permute-start.17 = (f32[104,128]{1,0:T(8,128)S(1)}, f32[104,128]{1,0:T(8,128)S(1)}, u32[]{:S(2)}, u32[]{:S(2)}) collective-permute-start(f32[104,128]{1,0:T(8,128)S(1)} %get-tuple-element.101), channel_id=1, source_target_pairs={{0,1},{1,0},{2,3},{3,2},{4,8},{5,9},{6,10},{7,11},{8,4},{9,5},{10,... | collective-permute-start | bytes 159752 | tf_op jit(solution)/shard_map/ppermute | solution.py:661

commit v6 on v5

--- a/solution.py
+++ b/solution.py
@@ -126,8 +126,8 @@
     plane_refs = refs[:size_y]
     (
         line_ref,
+        rows_ref,
         ids_ref,
-        rows_ref,
         place_ref,
         spot_ref,
         sums_ref,
@@ -180,8 +180,11 @@
         for piece in split(column):
             weighted = jnp.where(mine, piece, 0.0).astype(BF16)
             ids = ids + lax.dot_general(weighted, spot, BY_LANES, preferred_element_type=F32)
-    ids_ref[...] = jnp.zeros_like(ids_ref)
-    ids_ref[:, 0:slots] = ids - 1.0
+    ids = ids - 1.0
+    for owner in range(devices):
+        across, along = owner % size_y, owner // size_y
+        at = pl.ds((across ^ own_y) * size_x + along, 1)
+        ids_ref[at, 0:slots] = ids[owner : owner + 1, :]
 
     def compute(rows):
         weight = live_ref[rows, :].astype(F32)
@@ -189,7 +192,8 @@
 
     placed(blocks, 1, compute, places, place_ref, sums_ref, rows_ref, slots)
     for k, ref in enumerate(plane_refs):
-        ref[...] = rows_ref[pl.ds(k * size_x * slots, size_x * slots), :]
+        ref[0 : size_x * slots, :] = rows_ref[pl.ds(k * size_x * slots, size_x * slots), :]
+        ref[size_x * slots :, :] = ids_ref[pl.ds(k * size_x, size_x), :]
 
 
 def pack_kernel(
@@ -200,11 +204,12 @@
     live_hbm,
     cell_hbm,
     line_ref,
-    ids_ref,
+    out_hbm,
     out_ref,
     place_ref,
     sums_ref,
     place_sem,
+    out_sem,
     comp_ref,
     strain_ref,
     live_ref,
@@ -212,7 +217,6 @@
     load_sem,
 ):
     blocks, marks = comp_ref.shape
-    devices = out_ref.shape[0] // chunk
     depth = Depth(marks)
     pairs = (
         (comp_hbm, comp_ref),
@@ -226,9 +230,6 @@
     places = pltpu.make_async_copy(line_ref, place_ref, place_sem)
     places.start()
     out_ref[...] = jnp.zeros_like(out_ref)
-    for owner in range(devices):
-        at = owner * chunk + 2 * slots
-        out_ref[at : at + 1, :] = ids_ref[owner : owner + 1, :]
     for load in loads:
         load.wait()
 
@@ -242,6 +243,9 @@
         return depth.sums([split(logv), split(rho)], cell_ref[rows, :])
 
     placed(blocks, 2, compute, places, place_ref, sums_ref, out_ref, slots)
+    copy = pltpu.make_async_copy(out_ref.at[pl.ds(0, out_hbm.shape[0])], out_hbm, out_sem)
+    copy.start()
+    copy.wait()
 
 
 def regroup_kernel(slots, counts, *refs):
@@ -251,6 +255,8 @@
         at = pl.multiple_of((own_x ^ k) * slots, 8)
         for j, ref in enumerate(refs[:size_y]):
             out_ref[j * slots : (j + 1) * slots, :] = ref[pl.ds(at, slots), :]
+            line = ref[pl.ds(size_x * slots + (own_x ^ k), 1), :]
+            out_ref[size_y * slots + j : size_y * slots + j + 1, :] = line
 
 
 def gather_kernel(slots, counts, *refs):
@@ -259,8 +265,11 @@
     out_ref = refs[size_x]
     for k, ref in enumerate(refs[:size_x]):
         for j in range(size_y):
-            at = pl.multiple_of(((own_x ^ k) * size_y + (own_y ^ j)) * slots, 8)
+            source = (own_x ^ k) * size_y + (own_y ^ j)
+            at = pl.multiple_of(source * slots, 8)
             out_ref[pl.ds(at, slots), :] = ref[j * slots : (j + 1) * slots, :]
+            line = ref[size_y * slots + j : size_y * slots + j + 1, :]
+            out_ref[pl.ds(size_x * size_y * slots + source, 1), :] = line
 
 
 def parities():
@@ -290,6 +299,7 @@
     recv_ref,
     count_ref,
     old_ref,
+    vel_ref,
     y_even_ref,
     y_odd_ref,
     value_ref,
@@ -312,8 +322,8 @@
         span = slice(part * depth, (part + 1) * depth)
         ids = jnp.full((1, depth), -1.0, F32)
         for k in range(per):
-            first = (part * per + k) * chunk
-            line = recv_ref[first + 2 * slots : first + 2 * slots + 1, :]
+            at = total + part * per + k
+            line = count_ref[at : at + 1, :]
             if k:
                 line = pltpu.roll(line, k * slots, 1)
             ids = jnp.where((lanes >= k * slots) & (lanes < (k + 1) * slots), line, ids)
@@ -338,7 +348,13 @@
     for ref, is_first in ((y_even_ref, odd_y == 1), (y_odd_ref, odd_y == 0)):
         start = pl.multiple_of(jnp.where(is_first, 0, 2 * size_x), 8)
         ref[0 : 2 * size_x, :] = visc_ref[pl.ds(start, 2 * size_x), :]
-        ref[2 * size_x :, :] = force_ref[pl.ds(start, size_x), :]
+        ref[2 * size_x : 3 * size_x, :] = force_ref[pl.ds(start, size_x), :]
+        wide = Wide(bricks)
+        for c in range(3):
+            for k in range(2):
+                row = jnp.where(is_first, k, size_y - 1 - k)
+                at = (3 + 2 * c + k) * size_x
+                ref[at : at + size_x, :] = vel_ref[wide.line(c, row), :]
 
     @pl.when(at_end("gy"))
     def _():
@@ -500,8 +516,6 @@
     visc_in,
     wide_in,
     force_ref,
-    vy_low_ref,
-    vy_high_ref,
     y_even_ref,
     y_odd_ref,
     visc_ref,
@@ -512,10 +526,6 @@
 ):
     size_x, size_y = bricks
     wide = Wide(bricks)
-    for c in range(3):
-        for ref, near, far in ((vy_low_ref, -1, -2), (vy_high_ref, size_y, size_y + 1)):
-            for k, row in enumerate((near, far)):
-                wide_ref[wide.line(c, row), :] = ref[pl.ds((2 * c + k) * size_x, size_x), :]
     odd_y = parities()[1]
     rows = ((odd_y == 1, y_even_ref), (odd_y == 0, y_odd_ref))
     for is_low, ref in rows:
@@ -523,6 +533,10 @@
         visc_ref[wide.line(0, row), :] = ref[pl.ds(0, size_x), :]
         outer = jnp.where(is_low, -2, size_y + 1)
         visc_ref[wide.line(0, outer), :] = ref[pl.ds(size_x, size_x), :]
+        for c in range(3):
+            at = (3 + 2 * c) * size_x
+            wide_ref[wide.line(c, row), :] = ref[pl.ds(at, size_x), :]
+            wide_ref[wide.line(c, outer), :] = ref[pl.ds(at + size_x, size_x), :]
     for is_low, ref in rows:
         row = jnp.where(is_low, -1, size_y)
         visc = ref[pl.ds(0, size_x), :]
@@ -608,8 +622,6 @@
     odd_in,
     y_even_ref,
     y_odd_ref,
-    vy_low_ref,
-    vy_high_ref,
     x_even_ref,
     x_odd_ref,
 ):
@@ -617,12 +629,12 @@
     odd_x, odd_y = parities()
     for ref, is_first in ((x_even_ref, odd_x == 1), (x_odd_ref, odd_x == 0)):
         near = jnp.where(is_first, 0, size_x - 1)
-        pair = (y_even_ref[pl.ds(near, 1), :], y_odd_ref[pl.ds(near, 1), :])
-        for k, lines_ref in enumerate((vy_low_ref, vy_high_ref)):
-            at = 3 * size_y + 4 * k
-            ref[at : at + 1, :] = jnp.where(odd_y == 1 - k, *pair)
-            for c in range(3):
-                ref[at + 1 + c : at + 2 + c, :] = lines_ref[pl.ds(2 * c * size_x + near, 1), :]
+        for c, line in enumerate((0, 3, 5, 7)):
+            row = pl.ds(line * size_x + near, 1)
+            pair = (y_even_ref[row, :], y_odd_ref[row, :])
+            for k in range(2):
+                at = 3 * size_y + 4 * k + c
+                ref[at : at + 1, :] = jnp.where(odd_y == 1 - k, *pair)
 
     @pl.when(at_end("gx"))
     def _():
@@ -676,7 +688,7 @@
     size_x, size_y, depth = old_logvisc.shape
     columns = size_x * size_y
     slots = 2 * blocks // devices
-    chunk = 2 * slots + 1
+    chunk = 2 * slots
     total = devices * slots
     lines = (blocks // marks, marks)
     counts = (count_x, count_y)
@@ -688,17 +700,18 @@
         return [pltpu.VMEM((blocks, marks), kind) for kind in kinds]
 
     live, cell = in_hbm(marker_live), in_hbm(marker_cell)
-    *planes, places, ids = pl.pallas_call(
+    spare = -(-count_y // 8) * 8
+    *planes, places = pl.pallas_call(
         functools.partial(count_kernel, slots, chunk, counts),
         out_shape=(
-            *(shape(count_x * slots),) * count_y,
+            *(shape(count_x * (slots + 1)),) * count_y,
             shape(*lines, jnp.int32),
-            shape(devices),
         ),
         in_specs=[HBM] * 3,
-        out_specs=(VMEM,) * (count_y + 2),
+        out_specs=(VMEM,) * (count_y + 1),
         scratch_shapes=[
-            pltpu.VMEM((total, marks), F32),
+            pltpu.VMEM((total + 8, marks), F32),
+            pltpu.VMEM((devices + 8, marks), F32),
             pltpu.SMEM(lines, jnp.int32),
             pltpu.VMEM(lines, jnp.int32),
             pltpu.VMEM((16 * BATCH, marks), F32),
@@ -714,12 +727,14 @@
         planes[k] = crossed(planes[k], "gy", k)
     payload = pl.pallas_call(
         functools.partial(pack_kernel, slots, chunk),
-        out_shape=shape(devices * chunk),
-        in_specs=[HBM] * 4 + [VMEM] * 2,
-        out_specs=VMEM,
+        out_shape=pltpu.HBM((devices * chunk, marks), F32),
+        in_specs=[HBM] * 4 + [VMEM],
+        out_specs=HBM,
         scratch_shapes=[
+            pltpu.VMEM((devices * chunk + 8, marks), F32),
             pltpu.SMEM(lines, jnp.int32),
             pltpu.VMEM((32 * BATCH, marks), F32),
+            pltpu.SemaphoreType.DMA,
             pltpu.SemaphoreType.DMA,
             *buffers((F32, F32, jnp.int32, jnp.int32)),
             pltpu.SemaphoreType.DMA((4,)),
@@ -727,14 +742,14 @@
         compiler_params=limit(12),
         cost_estimate=pl.CostEstimate(flops=10**11, bytes_accessed=1, transcendentals=0),
         name="pack",
-    )(in_hbm(marker_comp), in_hbm(marker_strain), live, cell, places, ids)
+    )(in_hbm(marker_comp), in_hbm(marker_strain), live, cell, places)
     payload = payload.reshape(devices * chunk, 1, marks)
     received = lax.all_to_all(payload, BOTH, split_axis=0, concat_axis=0, tiled=True)
     received = received.reshape(devices * chunk, marks)
 
     messages = pl.pallas_call(
         functools.partial(regroup_kernel, slots, counts),
-        out_shape=(shape(count_y * slots),) * count_x,
+        out_shape=(shape(count_y * slots + spare),) * count_x,
         in_specs=[VMEM] * count_y,
         out_specs=(VMEM,) * count_x,
         compiler_params=limit(4),
@@ -745,22 +760,16 @@
     messages = [crossed(m, "gx", k) if k else m for k, m in enumerate(messages)]
     gathered = pl.pallas_call(
         functools.partial(gather_kernel, slots, counts),
-        out_shape=shape(total),
+        out_shape=shape(total + devices + 8),
         in_specs=[VMEM] * count_x,
         out_specs=VMEM,
         compiler_params=limit(4),
         name="gather",
     )(*messages)
 
-    def y_lines(near, far):
-        pair = jnp.concatenate([velocity[:, :, near], velocity[:, :, far]], axis=1)
-        return pair.reshape(6 * size_x, depth)
-
     def x_planes(first):
         return velocity[:, first : first + 2].reshape(6 * size_y, depth)
 
-    vy_low = shifted(y_lines(size_y - 1, size_y - 2), "gy", 1)
-    vy_high = shifted(y_lines(0, 1), "gy", -1)
     vx_low = shifted(x_planes(size_x - 2), "gx", 1)
     vx_high = shifted(x_planes(0), "gx", -1)
 
@@ -778,7 +787,7 @@
     received, wide_vel, gathered = lax.optimization_barrier((received, wide_vel, gathered))
 
     edge = 4 * size_x
-    x_side, y_side = shape(3 * size_y + CORNERS), shape(3 * size_x)
+    x_side, y_side = shape(3 * size_y + CORNERS), shape(9 * size_x)
     old = old_logvisc.reshape(columns, depth)
     y_even, y_odd, values, ids = pl.pallas_call(
         functools.partial(edge_kernel, slots, chunk, bricks),
@@ -787,7 +796,7 @@
             shape(total, 5 * depth, BF16),
             shape(total // depth),
         ),
-        in_specs=[VMEM] * 3,
+        in_specs=[VMEM] * 4,
         out_specs=(VMEM,) * 4,
         scratch_shapes=[
             pltpu.VMEM((edge, total), BF16),
@@ -797,7 +806,7 @@
         compiler_params=limit(16),
         cost_estimate=pl.CostEstimate(flops=1, bytes_accessed=1, transcendentals=0),
         name="edge",
-    )(received, gathered, old)
+    )(received, gathered, old, wide_vel)
     logvisc, density, force, visc, x_even, x_odd = pl.pallas_call(
         functools.partial(interior_kernel, bricks),
         out_shape=(*(shape(columns),) * 3, shape(wide.field), x_side, x_side),
@@ -816,12 +825,12 @@
     x_even, x_odd = pl.pallas_call(
         functools.partial(corner_kernel, bricks),
         out_shape=(x_side, x_side),
-        in_specs=[VMEM] * 6,
+        in_specs=[VMEM] * 4,
         out_specs=(VMEM, VMEM),
         input_output_aliases={0: 0, 1: 1},
         compiler_params=limit(4),
         name="corners",
-    )(x_even, x_odd, y_even, y_odd, vy_low, vy_high)
+    )(x_even, x_odd, y_even, y_odd)
     visc, wide_vel, wide_next, coeff, last = pl.pallas_call(
         functools.partial(sweep_kernel, bricks),
         out_shape=(
@@ -831,12 +840,12 @@
             shape(7 * columns),
             shape(3 * columns),
         ),
-        in_specs=[VMEM] * 7,
+        in_specs=[VMEM] * 5,
         out_specs=(VMEM,) * 5,
         input_output_aliases={0: 0, 1: 1},
         compiler_params=limit(12),
         name="sweep",
-    )(visc, wide_vel, force, vy_low, vy_high, y_even, y_odd)
+    )(visc, wide_vel, force, y_even, y_odd)
     x_even = swapped(x_even, "gx", 0)
     x_odd = swapped(x_odd, "gx", 1)
     smoothed = pl.pallas_call(

time: 57.5 us -> 56.4 us (0.981)
  starting transfers between devices: 32.9 us -> 26.2 us
  waiting for transfers between devices: 10.7 us -> 16.6 us
    ppermute x4 -> x2, starting transfers between devices: 12.3 us -> 6.46 us  [shifted(): return lax.ppermute(value, axis, pairs)]
    ppermute x10, waiting for transfers between devices: 5.9 us -> 9.66 us  [crossed(): return lax.ppermute(value, axis, pairs)]
    all_to_all x1, waiting for transfers between devices: 1.57 us -> 3.57 us  [per_device(): lax.all_to_all(payload, BOTH, split_axis=0, concat_axis=0, tiled=True)]
    ppermute x4, starting transfers between devices: 5.03 us -> 3.87 us  [swapped(): return lax.ppermute(value, BOTH, pairs)]
  transfers between devices with their start and end apart: 19 -> 17, of which waited for: 5 -> 7; matrix products, arithmetic and copies ran while one was open for 1% -> 0% of each run, Pallas kernels for 13% -> 13%
where the time goes in v6:
time: 56.4 us; the launch traced here: 55.4 us
  starting transfers between devices  26.2 us (46%)
  waiting for transfers between devices  16.6 us (29%)
  Pallas kernels  11.7 us (21%)
  between operations  0.8 us (1%)
    ppermute x10, waiting for transfers between devices, crossed(): return lax.ppermute(value, axis, pairs)  9.66 us
    ppermute x10, starting transfers between devices, crossed(): return lax.ppermute(value, axis, pairs)  9 us
    all_to_all x1, starting transfers between devices, per_device(): lax.all_to_all(payload, BOTH, split_axis=0, concat_axis=0, tiled=True)  6.91 us
    ppermute x2, starting transfers between devices, shifted(): return lax.ppermute(value, axis, pairs)  6.46 us
    pallas_call x1, Pallas kernels, per_device(): pl.pallas_call(functools.partial(pack_kernel, slots, chunk), out_shape=pl...  3.9 us
    ppermute x4, starting transfers between devices, swapped(): return lax.ppermute(value, BOTH, pairs)  3.87 us
    all_to_all x1, waiting for transfers between devices, per_device(): lax.all_to_all(payload, BOTH, split_axis=0, concat_axis=0, tiled=True)  3.57 us
    ppermute x4, waiting for transfers between devices, swapped(): return lax.ppermute(value, BOTH, pairs)  3.4 us
  transfers between devices with their start and end apart: 17, of which 7 were waited for; matrix products, arithmetic and copies ran while one was open for 0% of the time, Pallas kernels for 13%

profile of v6, /device:TPU:12, one launch (start us, length us, event | category | flops | bytes accessed | tf_op | source)
XLA Modules:
  0.0 55.4 jit_solution(4142805460808498935)
XLA Ops:
  0.6 3.0 %count.1 = (f32[264,128]{1,0:T(8,128)S(1)}, f32[264,128]{1,0:T(8,128)S(1)}, f32[264,128]{1,0:T(8,128)S(1)}, f32[264,128]{1,0:T(8,128)S(1)}, s32[4,128]{1,0:T(4,128)S(1)}) custom-call(s32[4,128]{1,0:T(4,128)} %bitcast.18, s32[512,128]{1,0:T(8,128)} %live_hbm.3, s32[512,128]{1,0:T(8,128)} %cell_hbm.3), custom_call_target="tpu_custom_call" | custom-call | tf_op jit(solution)/shard_map/count/pallas_call | solution.py:704
  3.6 0.5 collective-permute-start
  4.1 2.6 %collective-permute-start.1 = (f32[264,128]{1,0:T(8,128)S(1)}, f32[264,128]{1,0:T(8,128)S(1)}, u32[]{:S(2)}, u32[]{:S(2)}) collective-permute-start(f32[264,128]{1,0:T(8,128)S(1)} %get-tuple-element.55), channel_id=1, source_target_pairs={{0,2},{1,3},{2,0},{3,1},{4,6},{5,7},{6,4},{7,5},{8,10},{9,11},{10,... | collective-permute-start | bytes 405512 | tf_op jit(solution)/shard_map/ppermute | solution.py:678
  6.7 0.5 collective-permute-start.2
  7.2 3.9 %pack.1 = f32[2048,128]{1,0:T(8,128)} custom-call(f32[512,128]{1,0:T(8,128)} %comp_hbm.1, f32[512,128]{1,0:T(8,128)} %strain_hbm.1, s32[512,128]{1,0:T(8,128)} %live_hbm.3, s32[512,128]{1,0:T(8,128)} %cell_hbm.3, s32[4,128]{1,0:T(4,128)S(1)} %get-tuple-element.52.line_ref), custom_call_target="tpu_custom_call" | custom-call | flops 99999997952 | bytes 1 | tf_op jit(solution)/shard_map/pack/pallas_call | solution.py:728
  11.1 6.9 %all-to-all-start = ((f32[2048,1,128]{2,1,0:T(1,128)}), f32[2048,1,128]{2,1,0:T(1,128)S(1)}, u32[]{:S(2)}, u32[]{:S(2)}) async-start(f32[2048,1,128]{2,1,0:T(1,128)} %bitcast.15), calls=%async_computation | async-start | bytes 2097152 | tf_op jit(solution)/shard_map/all_to_all | solution.py:747
  18.0 0.0 collective-permute-done.refs_1_
  18.0 0.0 collective-permute-done.1.refs_2_
  18.0 0.9 %collective-permute-done.2.refs_3_ = f32[264,128]{1,0:T(8,128)S(1)} collective-permute-done((f32[264,128]{1,0:T(8,128)S(1)}, f32[264,128]{1,0:T(8,128)S(1)}, u32[]{:S(2)}, u32[]{:S(2)}) %collective-permute-start.2) | collective-permute-done | bytes 135200 | tf_op jit(solution)/shard_map/ppermute | solution.py:678
  18.9 0.0 copy-start
  19.0 0.1 collective-permute-start.5
  19.0 1.6 %collective-permute-start.6 = (f32[136,128]{1,0:T(8,128)S(1)}, f32[136,128]{1,0:T(8,128)S(1)}, u32[]{:S(2)}, u32[]{:S(2)}) collective-permute-start(f32[136,128]{1,0:T(8,128)S(1)} %get-tuple-element.68), channel_id=1, source_target_pairs={{0,8},{4,12},{8,0},{12,4},{16,24},{20,28},{24,16},{28,20},{1,9},{5... | collective-permute-start | bytes 208904 | tf_op jit(solution)/shard_map/ppermute | solution.py:678
  20.6 0.3 collective-permute-start.7
  20.9 0.5 collective-permute-start.8
  21.4 0.0 copy-done
  21.4 2.0 %collective-permute-start.3 = (f32[192,128]{1,0:T(8,128)S(1)}, f32[192,128]{1,0:T(8,128)S(1)}, u32[]{:S(2)}, u32[]{:S(2)}) collective-permute-start(f32[192,128]{1,0:T(8,128)S(1)} %bitcast.17), channel_id=1, source_target_pairs={{0,4},{4,8},{8,12},{12,16},{16,20},{20,24},{24,28},{1,5},{5,9},{9,... | collective-permute-start | bytes 294920 | tf_op jit(solution)/shard_map/ppermute | solution.py:655
  23.4 0.0 collective-permute-done.5.refs_1_
  23.4 4.5 %collective-permute-start.4 = (f32[192,128]{1,0:T(8,128)S(1)}, f32[192,128]{1,0:T(8,128)S(1)}, u32[]{:S(2)}, u32[]{:S(2)}) collective-permute-start(f32[192,128]{1,0:T(8,128)S(1)} %bitcast.16), channel_id=1, source_target_pairs={{4,0},{8,4},{12,8},{16,12},{20,16},{24,20},{28,24},{5,1},{9,5},{13... | collective-permute-start | bytes 294920 | tf_op jit(solution)/shard_map/ppermute | solution.py:655
  27.9 0.0 collective-permute-done.6.refs_2_
  27.9 0.2 collective-permute-start.9
  28.1 1.6 %collective-permute-done.7.refs_3_ = f32[136,128]{1,0:T(8,128)S(1)} collective-permute-done((f32[136,128]{1,0:T(8,128)S(1)}, f32[136,128]{1,0:T(8,128)S(1)}, u32[]{:S(2)}, u32[]{:S(2)}) %collective-permute-start.7) | collective-permute-done | bytes 69664 | tf_op jit(solution)/shard_map/ppermute | solution.py:678
  29.7 0.7 %collective-permute-start.10 = (f32[136,128]{1,0:T(8,128)S(1)}, f32[136,128]{1,0:T(8,128)S(1)}, u32[]{:S(2)}, u32[]{:S(2)}) collective-permute-start(f32[136,128]{1,0:T(8,128)S(1)} %get-tuple-element.72), channel_id=1, source_target_pairs={{0,24},{4,28},{8,16},{12,20},{16,8},{20,12},{24,0},{28,4},{1,25},{... | collective-permute-start | bytes 208904 | tf_op jit(solution)/shard_map/ppermute | solution.py:678
  30.4 0.0 collective-permute-done.8.refs_4_
  30.4 2.1 %collective-permute-start.11 = (f32[136,128]{1,0:T(8,128)S(1)}, f32[136,128]{1,0:T(8,128)S(1)}, u32[]{:S(2)}, u32[]{:S(2)}) collective-permute-start(f32[136,128]{1,0:T(8,128)S(1)} %get-tuple-element.73), channel_id=1, source_target_pairs={{0,28},{4,24},{8,20},{12,16},{16,12},{20,8},{24,4},{28,0},{1,29},{... | collective-permute-start | bytes 208904 | tf_op jit(solution)/shard_map/ppermute | solution.py:678
  32.6 7.1 %collective-permute-done.9.refs_5_ = f32[136,128]{1,0:T(8,128)S(1)} collective-permute-done((f32[136,128]{1,0:T(8,128)S(1)}, f32[136,128]{1,0:T(8,128)S(1)}, u32[]{:S(2)}, u32[]{:S(2)}) %collective-permute-start.9) | collective-permute-done | bytes 69664 | tf_op jit(solution)/shard_map/ppermute | solution.py:678
  39.7 0.0 collective-permute-done.10.refs_6_
  39.7 0.0 collective-permute-done.11.refs_7_
  39.7 0.1 gather.1.count_ref
  39.8 0.0 copy-start.1
  39.8 0.0 collective-permute-done.3.vx_low_ref
  39.8 0.0 collective-permute-done.4.vx_high_ref
  39.8 0.1 widen.1.vel_ref.wide_in
  39.9 3.6 %all-to-all-done = f32[2048,1,128]{2,1,0:T(1,128)S(1)} async-done(((f32[2048,1,128]{2,1,0:T(1,128)}), f32[2048,1,128]{2,1,0:T(1,128)S(1)}, u32[]{:S(2)}, u32[]{:S(2)}) %all-to-all-start) | async-done | bytes 1048608 | tf_op jit(solution)/shard_map/all_to_all | solution.py:747
  43.4 0.0 copy-done.1
  43.4 0.5 edge.1
  44.0 0.1 collective-permute-start.12
  44.1 2.1 %collective-permute-start.13 = (f32[144,128]{1,0:T(8,128)S(1)}, f32[144,128]{1,0:T(8,128)S(1)}, u32[]{:S(2)}, u32[]{:S(2)}) collective-permute-start(f32[144,128]{1,0:T(8,128)S(1)} %get-tuple-element.82), channel_id=1, source_target_pairs={{0,4},{4,0},{8,12},{12,8},{16,20},{20,16},{24,28},{28,24},{1,2},{5... | collective-permute-start | bytes 221192 | tf_op jit(solution)/shard_map/ppermute | solution.py:673
  46.2 1.8 %interior.1 = (f32[512,128]{1,0:T(8,128)}, f32[512,128]{1,0:T(8,128)}, f32[512,128]{1,0:T(8,128)S(1)}, f32[960,128]{1,0:T(8,128)S(1)}, f32[104,128]{1,0:T(8,128)S(1)}, /*index=5*/f32[104,128]{1,0:T(8,128)S(1)}) custom-call(bf16[1024,640]{1,0:T(8,128)(2,1)S(1)} %get-tuple-element.77.value_ref, f32[8,128]{1,0:T(8,128)S(1)} %get-tuple-element.78.ids_ref, ...), custom_call_target="tpu_custom_call" | custom-call | flops 1 | bytes 1 | tf_op jit(solution)/shard_map/interior/pallas_call | solution.py:810
  48.0 0.4 collective-permute-done.12.y_even_ref
  48.4 0.9 %collective-permute-done.13.y_odd_ref = f32[144,128]{1,0:T(8,128)S(1)} collective-permute-done((f32[144,128]{1,0:T(8,128)S(1)}, f32[144,128]{1,0:T(8,128)S(1)}, u32[]{:S(2)}, u32[]{:S(2)}) %collective-permute-start.13) | collective-permute-done | bytes 73760 | tf_op jit(solution)/shard_map/ppermute | solution.py:673
  49.3 0.2 collective-permute-start.14
  49.4 1.5 %collective-permute-start.15 = (f32[104,128]{1,0:T(8,128)S(1)}, f32[104,128]{1,0:T(8,128)S(1)}, u32[]{:S(2)}, u32[]{:S(2)}) collective-permute-start(f32[104,128]{1,0:T(8,128)S(1)} %get-tuple-element.99), channel_id=1, source_target_pairs={{0,1},{1,0},{2,3},{3,2},{4,8},{5,9},{6,10},{7,11},{8,4},{9,5},{10,... | collective-permute-start | bytes 159752 | tf_op jit(solution)/shard_map/ppermute | solution.py:673
  50.9 1.2 %sweep.1 = (f32[960,128]{1,0:T(8,128)S(1)}, f32[2880,128]{1,0:T(8,128)S(1)}, f32[2880,128]{1,0:T(8,128)S(1)}, f32[3584,128]{1,0:T(8,128)S(1)}, f32[1536,128]{1,0:T(8,128)S(1)}) custom-call(f32[960,128]{1,0:T(8,128)S(1)} %get-tuple-element.87.visc_in, f32[2880,128]{1,0:T(8,128)S(1)} %widen.1.vel_ref.wide_in, ...), custom_call_target="tpu_custom_call", output_to_operand_aliasing={{0}: (0, {}), {1}: (1, {})} | custom-call | tf_op jit(solution)/shard_map/sweep/pallas_call | solution.py:834
  52.1 0.0 collective-permute-done.14.x_even_ref
  52.1 2.2 %collective-permute-done.15.x_odd_ref = f32[104,128]{1,0:T(8,128)S(1)} collective-permute-done((f32[104,128]{1,0:T(8,128)S(1)}, f32[104,128]{1,0:T(8,128)S(1)}, u32[]{:S(2)}, u32[]{:S(2)}) %collective-permute-start.15) | collective-permute-done | bytes 53280 | tf_op jit(solution)/shard_map/ppermute | solution.py:673
  54.3 1.1 %finish.1 = (f32[3,16,32,128]{3,2,1,0:T(8,128)}, f32[960,128]{1,0:T(8,128)S(1)}, f32[2880,128]{1,0:T(8,128)S(1)}, f32[3584,128]{1,0:T(8,128)S(1)}, f32[1536,128]{1,0:T(8,128)S(1)}, /*index=5*/f32[2880,128]{1,0:T(8,128)S(1)}) custom-call(f32[960,128]{1,0:T(8,128)S(1)} %get-tuple-element.91.vis, ...), custom_call_target="tpu_custom_call", output_to_operand_aliasing={{1}: (0, {}), {2}: (1, {}), {3}: (2, {}), {4}: (3, {}), {5}... | custom-call | tf_op jit(solution)/shard_map/finish/pallas_call | solution.py:851
  (3 shorter events, 0.1 us)
Async XLA Ops:
  3.6 14.4 %collective-permute-start = (f32[264,128]{1,0:T(8,128)S(1)}, f32[264,128]{1,0:T(8,128)S(1)}, u32[]{:S(2)}, u32[]{:S(2)}) collective-permute-start(f32[264,128]{1,0:T(8,128)S(1)} %get-tuple-element.54), channel_id=1, source_target_pairs={{0,1},{1,0},{2,3},{3,2},{4,5},{5,4},{6,7},{7,6},{8,9},{9,8},{10,11... | collective-permute-start | bytes 405512 | tf_op jit(solution)/shard_map/ppermute | solution.py:678
  4.1 13.9 %collective-permute-start.1 = (f32[264,128]{1,0:T(8,128)S(1)}, f32[264,128]{1,0:T(8,128)S(1)}, u32[]{:S(2)}, u32[]{:S(2)}) collective-permute-start(f32[264,128]{1,0:T(8,128)S(1)} %get-tuple-element.55), channel_id=1, source_target_pairs={{0,2},{1,3},{2,0},{3,1},{4,6},{5,7},{6,4},{7,5},{8,10},{9,11},{10,... | collective-permute-start | bytes 405512 | tf_op jit(solution)/shard_map/ppermute | solution.py:678
  6.7 12.2 %collective-permute-start.2 = (f32[264,128]{1,0:T(8,128)S(1)}, f32[264,128]{1,0:T(8,128)S(1)}, u32[]{:S(2)}, u32[]{:S(2)}) collective-permute-start(f32[264,128]{1,0:T(8,128)S(1)} %get-tuple-element.56), channel_id=1, source_target_pairs={{0,3},{1,2},{2,1},{3,0},{4,7},{5,6},{6,5},{7,4},{8,11},{9,10},{10,... | collective-permute-start | bytes 405512 | tf_op jit(solution)/shard_map/ppermute | solution.py:678
  11.1 32.4 %all-to-all-start = ((f32[2048,1,128]{2,1,0:T(1,128)}), f32[2048,1,128]{2,1,0:T(1,128)S(1)}, u32[]{:S(2)}, u32[]{:S(2)}) async-start(f32[2048,1,128]{2,1,0:T(1,128)} %bitcast.15), calls=%async_computation | async-start | bytes 2097152 | tf_op jit(solution)/shard_map/all_to_all | solution.py:747
  18.9 2.5 %copy-start = (f32[3,16,32,128]{3,2,1,0:T(8,128)S(1)}, f32[3,16,32,128]{3,2,1,0:T(8,128)}, u32[]{:S(2)}) copy-start(f32[3,16,32,128]{3,2,1,0:T(8,128)} %param.13) | copy-start | bytes 2359300
  19.0 4.5 %collective-permute-start.5 = (f32[136,128]{1,0:T(8,128)S(1)}, f32[136,128]{1,0:T(8,128)S(1)}, u32[]{:S(2)}, u32[]{:S(2)}) collective-permute-start(f32[136,128]{1,0:T(8,128)S(1)} %get-tuple-element.67), channel_id=1, source_target_pairs={{0,4},{4,0},{8,12},{12,8},{16,20},{20,16},{24,28},{28,24},{1,5},{5... | collective-permute-start | bytes 208904 | tf_op jit(solution)/shard_map/ppermute | solution.py:678
  19.0 8.9 %collective-permute-start.6 = (f32[136,128]{1,0:T(8,128)S(1)}, f32[136,128]{1,0:T(8,128)S(1)}, u32[]{:S(2)}, u32[]{:S(2)}) collective-permute-start(f32[136,128]{1,0:T(8,128)S(1)} %get-tuple-element.68), channel_id=1, source_target_pairs={{0,8},{4,12},{8,0},{12,4},{16,24},{20,28},{24,16},{28,20},{1,9},{5... | collective-permute-start | bytes 208904 | tf_op jit(solution)/shard_map/ppermute | solution.py:678
  20.6 9.1 %collective-permute-start.7 = (f32[136,128]{1,0:T(8,128)S(1)}, f32[136,128]{1,0:T(8,128)S(1)}, u32[]{:S(2)}, u32[]{:S(2)}) collective-permute-start(f32[136,128]{1,0:T(8,128)S(1)} %get-tuple-element.69), channel_id=1, source_target_pairs={{0,12},{4,8},{8,4},{12,0},{16,28},{20,24},{24,20},{28,16},{1,13},{... | collective-permute-start | bytes 208904 | tf_op jit(solution)/shard_map/ppermute | solution.py:678
  20.9 9.5 %collective-permute-start.8 = (f32[136,128]{1,0:T(8,128)S(1)}, f32[136,128]{1,0:T(8,128)S(1)}, u32[]{:S(2)}, u32[]{:S(2)}) collective-permute-start(f32[136,128]{1,0:T(8,128)S(1)} %get-tuple-element.70), channel_id=1, source_target_pairs={{0,16},{4,20},{8,24},{12,28},{16,0},{20,4},{24,8},{28,12},{1,17},{... | collective-permute-start | bytes 208904 | tf_op jit(solution)/shard_map/ppermute | solution.py:678
  21.4 18.3 %collective-permute-start.3 = (f32[192,128]{1,0:T(8,128)S(1)}, f32[192,128]{1,0:T(8,128)S(1)}, u32[]{:S(2)}, u32[]{:S(2)}) collective-permute-start(f32[192,128]{1,0:T(8,128)S(1)} %bitcast.17), channel_id=1, source_target_pairs={{0,4},{4,8},{8,12},{12,16},{16,20},{20,24},{24,28},{1,5},{5,9},{9,... | collective-permute-start | bytes 294920 | tf_op jit(solution)/shard_map/ppermute | solution.py:655
  23.4 16.4 %collective-permute-start.4 = (f32[192,128]{1,0:T(8,128)S(1)}, f32[192,128]{1,0:T(8,128)S(1)}, u32[]{:S(2)}, u32[]{:S(2)}) collective-permute-start(f32[192,128]{1,0:T(8,128)S(1)} %bitcast.16), channel_id=1, source_target_pairs={{4,0},{8,4},{12,8},{16,12},{20,16},{24,20},{28,24},{5,1},{9,5},{13... | collective-permute-start | bytes 294920 | tf_op jit(solution)/shard_map/ppermute | solution.py:655
  27.9 11.7 %collective-permute-start.9 = (f32[136,128]{1,0:T(8,128)S(1)}, f32[136,128]{1,0:T(8,128)S(1)}, u32[]{:S(2)}, u32[]{:S(2)}) collective-permute-start(f32[136,128]{1,0:T(8,128)S(1)} %get-tuple-element.71), channel_id=1, source_target_pairs={{0,20},{4,16},{8,28},{12,24},{16,4},{20,0},{24,12},{28,8},{1,21},{... | collective-permute-start | bytes 208904 | tf_op jit(solution)/shard_map/ppermute | solution.py:678
  29.7 10.0 %collective-permute-start.10 = (f32[136,128]{1,0:T(8,128)S(1)}, f32[136,128]{1,0:T(8,128)S(1)}, u32[]{:S(2)}, u32[]{:S(2)}) collective-permute-start(f32[136,128]{1,0:T(8,128)S(1)} %get-tuple-element.72), channel_id=1, source_target_pairs={{0,24},{4,28},{8,16},{12,20},{16,8},{20,12},{24,0},{28,4},{1,25},{... | collective-permute-start | bytes 208904 | tf_op jit(solution)/shard_map/ppermute | solution.py:678
  30.4 9.2 %collective-permute-start.11 = (f32[136,128]{1,0:T(8,128)S(1)}, f32[136,128]{1,0:T(8,128)S(1)}, u32[]{:S(2)}, u32[]{:S(2)}) collective-permute-start(f32[136,128]{1,0:T(8,128)S(1)} %get-tuple-element.73), channel_id=1, source_target_pairs={{0,28},{4,24},{8,20},{12,16},{16,12},{20,8},{24,4},{28,0},{1,29},{... | collective-permute-start | bytes 208904 | tf_op jit(solution)/shard_map/ppermute | solution.py:678
  39.8 3.7 %copy-start.1 = (f32[16,32,128]{2,1,0:T(8,128)S(1)}, f32[16,32,128]{2,1,0:T(8,128)}, u32[]{:S(2)}) copy-start(f32[16,32,128]{2,1,0:T(8,128)} %param.12) | copy-start | bytes 786436
  44.0 4.4 %collective-permute-start.12 = (f32[144,128]{1,0:T(8,128)S(1)}, f32[144,128]{1,0:T(8,128)S(1)}, u32[]{:S(2)}, u32[]{:S(2)}) collective-permute-start(f32[144,128]{1,0:T(8,128)S(1)} %get-tuple-element.81), channel_id=1, source_target_pairs={{0,1},{4,5},{8,9},{12,13},{16,17},{20,21},{24,25},{28,29},{1,0},{5... | collective-permute-start | bytes 221192 | tf_op jit(solution)/shard_map/ppermute | solution.py:673
  44.1 5.2 %collective-permute-start.13 = (f32[144,128]{1,0:T(8,128)S(1)}, f32[144,128]{1,0:T(8,128)S(1)}, u32[]{:S(2)}, u32[]{:S(2)}) collective-permute-start(f32[144,128]{1,0:T(8,128)S(1)} %get-tuple-element.82), channel_id=1, source_target_pairs={{0,4},{4,0},{8,12},{12,8},{16,20},{20,16},{24,28},{28,24},{1,2},{5... | collective-permute-start | bytes 221192 | tf_op jit(solution)/shard_map/ppermute | solution.py:673
  49.3 2.8 %collective-permute-start.14 = (f32[104,128]{1,0:T(8,128)S(1)}, f32[104,128]{1,0:T(8,128)S(1)}, u32[]{:S(2)}, u32[]{:S(2)}) collective-permute-start(f32[104,128]{1,0:T(8,128)S(1)} %get-tuple-element.98), channel_id=1, source_target_pairs={{0,4},{1,5},{2,6},{3,7},{4,0},{5,1},{6,2},{7,3},{8,12},{9,13},{10,... | collective-permute-start | bytes 159752 | tf_op jit(solution)/shard_map/ppermute | solution.py:673
  49.4 4.9 %collective-permute-start.15 = (f32[104,128]{1,0:T(8,128)S(1)}, f32[104,128]{1,0:T(8,128)S(1)}, u32[]{:S(2)}, u32[]{:S(2)}) collective-permute-start(f32[104,128]{1,0:T(8,128)S(1)} %get-tuple-element.99), channel_id=1, source_target_pairs={{0,1},{1,0},{2,3},{3,2},{4,8},{5,9},{6,10},{7,11},{8,4},{9,5},{10,... | collective-permute-start | bytes 159752 | tf_op jit(solution)/shard_map/ppermute | solution.py:673

commit v7 on v6

--- a/solution.py
+++ b/solution.py
@@ -121,11 +121,17 @@
     place(steps - 1)
 
 
-def count_kernel(slots, chunk, counts, dest_hbm, live_hbm, cell_hbm, *refs):
+def count_kernel(
+    slots, chunk, counts, dest_hbm, live_hbm, cell_hbm, comp_hbm, strain_hbm, *refs
+):
     size_x, size_y = counts
     plane_refs = refs[:size_y]
     (
         line_ref,
+        live_ref,
+        cell_ref,
+        comp_ref,
+        strain_ref,
         rows_ref,
         ids_ref,
         place_ref,
@@ -133,14 +139,18 @@
         sums_ref,
         place_sem,
         dest_ref,
-        live_ref,
-        cell_ref,
         load_sem,
     ) = refs[size_y:]
     blocks, marks = live_ref.shape
     devices = size_x * size_y
     depth = Depth(marks)
-    pairs = ((dest_hbm, dest_ref), (cell_hbm, cell_ref), (live_hbm, live_ref))
+    pairs = (
+        (dest_hbm, dest_ref),
+        (cell_hbm, cell_ref),
+        (live_hbm, live_ref),
+        (comp_hbm, comp_ref),
+        (strain_hbm, strain_ref),
+    )
     loads = [pltpu.make_async_copy(*pair, load_sem.at[k]) for k, pair in enumerate(pairs)]
     for load in loads:
         load.start()
@@ -170,7 +180,7 @@
         ranks.append(rank)
     places = pltpu.make_async_copy(spot_ref, place_ref, place_sem)
     places.start()
-    for load in loads[1:]:
+    for load in loads[1:3]:
         load.wait()
     ids = jnp.zeros((devices, slots), F32)
     for k, (mine, rank) in enumerate(zip(owned, ranks)):
@@ -194,15 +204,16 @@
     for k, ref in enumerate(plane_refs):
         ref[0 : size_x * slots, :] = rows_ref[pl.ds(k * size_x * slots, size_x * slots), :]
         ref[size_x * slots :, :] = ids_ref[pl.ds(k * size_x, size_x), :]
+    for load in loads[3:]:
+        load.wait()
 
 
 def pack_kernel(
     slots,
-    chunk,
-    comp_hbm,
-    strain_hbm,
-    live_hbm,
-    cell_hbm,
+    comp_ref,
+    strain_ref,
+    live_ref,
+    cell_ref,
     line_ref,
     out_hbm,
     out_ref,
@@ -210,28 +221,12 @@
     sums_ref,
     place_sem,
     out_sem,
-    comp_ref,
-    strain_ref,
-    live_ref,
-    cell_ref,
-    load_sem,
 ):
     blocks, marks = comp_ref.shape
     depth = Depth(marks)
-    pairs = (
-        (comp_hbm, comp_ref),
-        (strain_hbm, strain_ref),
-        (live_hbm, live_ref),
-        (cell_hbm, cell_ref),
-    )
-    loads = [pltpu.make_async_copy(*pair, load_sem.at[k]) for k, pair in enumerate(pairs)]
-    for load in loads:
-        load.start()
     places = pltpu.make_async_copy(line_ref, place_ref, place_sem)
     places.start()
     out_ref[...] = jnp.zeros_like(out_ref)
-    for load in loads:
-        load.wait()
 
     def compute(rows):
         comp = comp_ref[rows, :]
@@ -696,19 +691,17 @@
     def shape(rows, width=depth, kind=F32):
         return jax.ShapeDtypeStruct((rows, width), kind)
 
-    def buffers(kinds):
-        return [pltpu.VMEM((blocks, marks), kind) for kind in kinds]
-
-    live, cell = in_hbm(marker_live), in_hbm(marker_cell)
     spare = -(-count_y // 8) * 8
-    *planes, places = pl.pallas_call(
+    *planes, places, live, cell, comp, strain = pl.pallas_call(
         functools.partial(count_kernel, slots, chunk, counts),
         out_shape=(
             *(shape(count_x * (slots + 1)),) * count_y,
             shape(*lines, jnp.int32),
+            *(shape(blocks, marks, jnp.int32),) * 2,
+            *(shape(blocks, marks),) * 2,
         ),
-        in_specs=[HBM] * 3,
-        out_specs=(VMEM,) * (count_y + 1),
+        in_specs=[HBM] * 5,
+        out_specs=(VMEM,) * (count_y + 5),
         scratch_shapes=[
             pltpu.VMEM((total + 8, marks), F32),
             pltpu.VMEM((devices + 8, marks), F32),
@@ -717,18 +710,23 @@
             pltpu.VMEM((16 * BATCH, marks), F32),
             pltpu.SemaphoreType.DMA,
             pltpu.VMEM(lines, jnp.int32),
-            *buffers((jnp.int32, jnp.int32)),
-            pltpu.SemaphoreType.DMA((3,)),
+            pltpu.SemaphoreType.DMA((5,)),
         ],
         compiler_params=limit(12),
         name="count",
-    )(in_hbm(block_dest.reshape(lines)), live, cell)
+    )(
+        in_hbm(block_dest.reshape(lines)),
+        in_hbm(marker_live),
+        in_hbm(marker_cell),
+        in_hbm(marker_comp),
+        in_hbm(marker_strain),
+    )
     for k in range(1, count_y):
         planes[k] = crossed(planes[k], "gy", k)
     payload = pl.pallas_call(
-        functools.partial(pack_kernel, slots, chunk),
+        functools.partial(pack_kernel, slots),
         out_shape=pltpu.HBM((devices * chunk, marks), F32),
-        in_specs=[HBM] * 4 + [VMEM],
+        in_specs=[VMEM] * 5,
         out_specs=HBM,
         scratch_shapes=[
             pltpu.VMEM((devices * chunk + 8, marks), F32),
@@ -736,13 +734,11 @@
             pltpu.VMEM((32 * BATCH, marks), F32),
             pltpu.SemaphoreType.DMA,
             pltpu.SemaphoreType.DMA,
-            *buffers((F32, F32, jnp.int32, jnp.int32)),
-            pltpu.SemaphoreType.DMA((4,)),
         ],
         compiler_params=limit(12),
         cost_estimate=pl.CostEstimate(flops=10**11, bytes_accessed=1, transcendentals=0),
         name="pack",
-    )(in_hbm(marker_comp), in_hbm(marker_strain), live, cell, places)
+    )(comp, strain, live, cell, places)
     payload = payload.reshape(devices * chunk, 1, marks)
     received = lax.all_to_all(payload, BOTH, split_axis=0, concat_axis=0, tiled=True)
     received = received.reshape(devices * chunk, marks)

time: 56.4 us -> 55.2 us (0.979)
  Pallas kernels: 11.7 us -> 10.6 us
  waiting for transfers between devices: 16.6 us -> 15.9 us
  starting transfers between devices: 26.2 us -> 26.9 us
    pallas_call x1, Pallas kernels: 3.9 us -> 2.72 us  [per_device(): pl.pallas_call(functools.partial(pack_kernel, slots), out_shape=pltpu.HBM...]
    ppermute x4, waiting for transfers between devices: 3.4 us -> 2.8 us  [swapped(): return lax.ppermute(value, BOTH, pairs)]
    ppermute x4, starting transfers between devices: 3.87 us -> 4.44 us  [swapped(): return lax.ppermute(value, BOTH, pairs)]
  transfers between devices with their start and end apart: 17 -> 17, of which waited for: 7 -> 6; matrix products, arithmetic and copies ran while one was open for 0% -> 0% of each run, Pallas kernels for 13% -> 11%
where the time goes in v7:
time: 55.2 us; the launch traced here: 54.3 us
  starting transfers between devices  26.9 us (49%)
  waiting for transfers between devices  15.9 us (29%)
  Pallas kernels  10.6 us (19%)
  between operations  0.81 us (1%)
    ppermute x10, waiting for transfers between devices, crossed(): return lax.ppermute(value, axis, pairs)  9.17 us
    ppermute x10, starting transfers between devices, crossed(): return lax.ppermute(value, axis, pairs)  9.15 us
    all_to_all x1, starting transfers between devices, per_device(): lax.all_to_all(payload, BOTH, split_axis=0, concat_axis=0, tiled=True)  6.9 us
    ppermute x2, starting transfers between devices, shifted(): return lax.ppermute(value, axis, pairs)  6.46 us
    ppermute x4, starting transfers between devices, swapped(): return lax.ppermute(value, BOTH, pairs)  4.44 us
    all_to_all x1, waiting for transfers between devices, per_device(): lax.all_to_all(payload, BOTH, split_axis=0, concat_axis=0, tiled=True)  3.92 us
    pallas_call x1, Pallas kernels, per_device(): pl.pallas_call(functools.partial(count_kernel, slots, chunk, counts), out...  2.99 us
    ppermute x4, waiting for transfers between devices, swapped(): return lax.ppermute(value, BOTH, pairs)  2.8 us
  transfers between devices with their start and end apart: 17, of which 6 were waited for; matrix products, arithmetic and copies ran while one was open for 0% of the time, Pallas kernels for 11%

profile of v7, /device:TPU:12, one launch (start us, length us, event | category | flops | bytes accessed | tf_op | source)
XLA Modules:
  0.0 54.3 jit_solution(14314681003756643697)
XLA Ops:
  0.6 3.0 %count.1 = (f32[264,128]{1,0:T(8,128)S(1)}, f32[264,128]{1,0:T(8,128)S(1)}, f32[264,128]{1,0:T(8,128)S(1)}, f32[264,128]{1,0:T(8,128)S(1)}, s32[4,128]{1,0:T(4,1...) custom-call(s32[4,128]{1,0:T(4,128)} %bitcast.18, ...), custom_call_target="tpu_custom_call" | custom-call | tf_op jit(solution)/shard_map/count/pallas_call | solution.py:695
  3.6 0.5 collective-permute-start
  4.1 2.6 %collective-permute-start.1 = (f32[264,128]{1,0:T(8,128)S(1)}, f32[264,128]{1,0:T(8,128)S(1)}, u32[]{:S(2)}, u32[]{:S(2)}) collective-permute-start(f32[264,128]{1,0:T(8,128)S(1)} %get-tuple-element.63), channel_id=1, source_target_pairs={{0,2},{1,3},{2,0},{3,1},{4,6},{5,7},{6,4},{7,5},{8,10},{9,11},{10,... | collective-permute-start | bytes 405512 | tf_op jit(solution)/shard_map/ppermute | solution.py:673
  6.7 0.5 collective-permute-start.2
  7.2 2.7 %pack.1 = f32[2048,128]{1,0:T(8,128)} custom-call(f32[512,128]{1,0:T(8,128)S(1)} %get-tuple-element.56.comp_ref, f32[512,128]{1,0:T(8,128)S(1)} %get-tuple-element.57.strain_ref, s32[512,128]{1,0:T(8,128)S(1)} %get-tuple-element.58.live_ref, s32[512,128]{1,0:T(8,128)S(1)} %get-tuple-element.59.cell_ref, s32[4,128]{1,0:T(4,128)S(1)} %get-tuple-element.60.line_ref), custom_call_target="tpu_custom_call" | custom-call | flops 99999997952 | bytes 1 | tf_op jit(solution)/shard_map/pack/pallas_call | solution.py:726
  9.9 6.9 %all-to-all-start = ((f32[2048,1,128]{2,1,0:T(1,128)}), f32[2048,1,128]{2,1,0:T(1,128)S(1)}, u32[]{:S(2)}, u32[]{:S(2)}) async-start(f32[2048,1,128]{2,1,0:T(1,128)} %bitcast.15), calls=%async_computation | async-start | bytes 2097152 | tf_op jit(solution)/shard_map/all_to_all | solution.py:743
  16.8 0.0 collective-permute-done.refs_1_
  16.8 0.0 collective-permute-done.1.refs_2_
  16.8 2.4 %collective-permute-done.2.refs_3_ = f32[264,128]{1,0:T(8,128)S(1)} collective-permute-done((f32[264,128]{1,0:T(8,128)S(1)}, f32[264,128]{1,0:T(8,128)S(1)}, u32[]{:S(2)}, u32[]{:S(2)}) %collective-permute-start.2) | collective-permute-done | bytes 135200 | tf_op jit(solution)/shard_map/ppermute | solution.py:673
  19.2 0.0 copy-start
  19.3 0.1 collective-permute-start.5
  19.3 2.5 %collective-permute-start.6 = (f32[136,128]{1,0:T(8,128)S(1)}, f32[136,128]{1,0:T(8,128)S(1)}, u32[]{:S(2)}, u32[]{:S(2)}) collective-permute-start(f32[136,128]{1,0:T(8,128)S(1)} %get-tuple-element.76), channel_id=1, source_target_pairs={{0,8},{4,12},{8,0},{12,4},{16,24},{20,28},{24,16},{28,20},{1,9},{5... | collective-permute-start | bytes 208904 | tf_op jit(solution)/shard_map/ppermute | solution.py:673
  21.9 0.1 collective-permute-start.7
  21.9 0.8 %collective-permute-start.8 = (f32[136,128]{1,0:T(8,128)S(1)}, f32[136,128]{1,0:T(8,128)S(1)}, u32[]{:S(2)}, u32[]{:S(2)}) collective-permute-start(f32[136,128]{1,0:T(8,128)S(1)} %get-tuple-element.78), channel_id=1, source_target_pairs={{0,16},{4,20},{8,24},{12,28},{16,0},{20,4},{24,8},{28,12},{1,17},{... | collective-permute-start | bytes 208904 | tf_op jit(solution)/shard_map/ppermute | solution.py:673
  22.7 0.0 copy-done
  22.8 2.0 %collective-permute-start.3 = (f32[192,128]{1,0:T(8,128)S(1)}, f32[192,128]{1,0:T(8,128)S(1)}, u32[]{:S(2)}, u32[]{:S(2)}) collective-permute-start(f32[192,128]{1,0:T(8,128)S(1)} %bitcast.17), channel_id=1, source_target_pairs={{0,4},{4,8},{8,12},{12,16},{16,20},{20,24},{24,28},{1,5},{5,9},{9,... | collective-permute-start | bytes 294920 | tf_op jit(solution)/shard_map/ppermute | solution.py:650
  24.7 0.0 collective-permute-done.5.refs_1_
  24.8 4.5 %collective-permute-start.4 = (f32[192,128]{1,0:T(8,128)S(1)}, f32[192,128]{1,0:T(8,128)S(1)}, u32[]{:S(2)}, u32[]{:S(2)}) collective-permute-start(f32[192,128]{1,0:T(8,128)S(1)} %bitcast.16), channel_id=1, source_target_pairs={{4,0},{8,4},{12,8},{16,12},{20,16},{24,20},{28,24},{5,1},{9,5},{13... | collective-permute-start | bytes 294920 | tf_op jit(solution)/shard_map/ppermute | solution.py:650
  29.3 0.0 collective-permute-done.6.refs_2_
  29.3 0.1 collective-permute-start.9
  29.3 0.0 collective-permute-done.7.refs_3_
  29.4 1.5 %collective-permute-start.10 = (f32[136,128]{1,0:T(8,128)S(1)}, f32[136,128]{1,0:T(8,128)S(1)}, u32[]{:S(2)}, u32[]{:S(2)}) collective-permute-start(f32[136,128]{1,0:T(8,128)S(1)} %get-tuple-element.80), channel_id=1, source_target_pairs={{0,24},{4,28},{8,16},{12,20},{16,8},{20,12},{24,0},{28,4},{1,25},{... | collective-permute-start | bytes 208904 | tf_op jit(solution)/shard_map/ppermute | solution.py:673
  30.9 0.0 collective-permute-done.8.refs_4_
  30.9 0.5 collective-permute-start.11
  31.4 5.3 %collective-permute-done.9.refs_5_ = f32[136,128]{1,0:T(8,128)S(1)} collective-permute-done((f32[136,128]{1,0:T(8,128)S(1)}, f32[136,128]{1,0:T(8,128)S(1)}, u32[]{:S(2)}, u32[]{:S(2)}) %collective-permute-start.9) | collective-permute-done | bytes 69664 | tf_op jit(solution)/shard_map/ppermute | solution.py:673
  36.7 1.4 %collective-permute-done.10.refs_6_ = f32[136,128]{1,0:T(8,128)S(1)} collective-permute-done((f32[136,128]{1,0:T(8,128)S(1)}, f32[136,128]{1,0:T(8,128)S(1)}, u32[]{:S(2)}, u32[]{:S(2)}) %collective-permute-start.10) | collective-permute-done | bytes 69664 | tf_op jit(solution)/shard_map/ppermute | solution.py:673
  38.2 0.0 collective-permute-done.11.refs_7_
  38.2 0.1 gather.1.count_ref
  38.2 0.0 copy-start.1
  38.2 0.0 collective-permute-done.3.vx_low_ref
  38.3 0.0 collective-permute-done.4.vx_high_ref
  38.3 0.1 widen.1.vel_ref.wide_in
  38.3 3.9 %all-to-all-done = f32[2048,1,128]{2,1,0:T(1,128)S(1)} async-done(((f32[2048,1,128]{2,1,0:T(1,128)}), f32[2048,1,128]{2,1,0:T(1,128)S(1)}, u32[]{:S(2)}, u32[]{:S(2)}) %all-to-all-start) | async-done | bytes 1048608 | tf_op jit(solution)/shard_map/all_to_all | solution.py:743
  42.3 0.0 copy-done.1
  42.3 0.5 %edge.1 = (f32[144,128]{1,0:T(8,128)S(1)}, f32[144,128]{1,0:T(8,128)S(1)}, bf16[1024,640]{1,0:T(8,128)(2,1)S(1)}, f32[8,128]{1,0:T(8,128)S(1)}) custom-call(f32[2048,128]{1,0:T(8,128)S(1)} %bitcast.11, f32[1064,128]{1,0:T(8,128)S(1)} %gather.1.count_ref, f32[512,128]{1,0:T(8,128)S(1)} %bitcast.13, f32[2880,128]{1,0:T(8,128)S(1)} %widen.1.vel_ref.wide_in), custom_call_target="tpu_custom_call" | custom-call | flops 1 | bytes 1 | tf_op jit(solution)/shard_map/edge/pallas_call | solution.py:788
  42.8 0.1 collective-permute-start.12
  42.9 2.7 %collective-permute-start.13 = (f32[144,128]{1,0:T(8,128)S(1)}, f32[144,128]{1,0:T(8,128)S(1)}, u32[]{:S(2)}, u32[]{:S(2)}) collective-permute-start(f32[144,128]{1,0:T(8,128)S(1)} %get-tuple-element.90), channel_id=1, source_target_pairs={{0,4},{4,0},{8,12},{12,8},{16,20},{20,16},{24,28},{28,24},{1,2},{5... | collective-permute-start | bytes 221192 | tf_op jit(solution)/shard_map/ppermute | solution.py:668
  45.6 1.9 %interior.1 = (f32[512,128]{1,0:T(8,128)}, f32[512,128]{1,0:T(8,128)}, f32[512,128]{1,0:T(8,128)S(1)}, f32[960,128]{1,0:T(8,128)S(1)}, f32[104,128]{1,0:T(8,128)S(1)}, /*index=5*/f32[104,128]{1,0:T(8,128)S(1)}) custom-call(bf16[1024,640]{1,0:T(8,128)(2,1)S(1)} %get-tuple-element.85.value_ref, f32[8,128]{1,0:T(8,128)S(1)} %get-tuple-element.86.ids_ref, ...), custom_call_target="tpu_custom_call" | custom-call | flops 1 | bytes 1 | tf_op jit(solution)/shard_map/interior/pallas_call | solution.py:806
  47.5 0.0 collective-permute-done.12.y_even_ref
  47.5 0.7 %collective-permute-done.13.y_odd_ref = f32[144,128]{1,0:T(8,128)S(1)} collective-permute-done((f32[144,128]{1,0:T(8,128)S(1)}, f32[144,128]{1,0:T(8,128)S(1)}, u32[]{:S(2)}, u32[]{:S(2)}) %collective-permute-start.13) | collective-permute-done | bytes 73760 | tf_op jit(solution)/shard_map/ppermute | solution.py:668
  48.2 0.1 collective-permute-start.14
  48.3 1.5 %collective-permute-start.15 = (f32[104,128]{1,0:T(8,128)S(1)}, f32[104,128]{1,0:T(8,128)S(1)}, u32[]{:S(2)}, u32[]{:S(2)}) collective-permute-start(f32[104,128]{1,0:T(8,128)S(1)} %get-tuple-element.107), channel_id=1, source_target_pairs={{0,1},{1,0},{2,3},{3,2},{4,8},{5,9},{6,10},{7,11},{8,4},{9,5},{10,... | collective-permute-start | bytes 159752 | tf_op jit(solution)/shard_map/ppermute | solution.py:668
  49.9 1.2 %sweep.1 = (f32[960,128]{1,0:T(8,128)S(1)}, f32[2880,128]{1,0:T(8,128)S(1)}, f32[2880,128]{1,0:T(8,128)S(1)}, f32[3584,128]{1,0:T(8,128)S(1)}, f32[1536,128]{1,0:T(8,128)S(1)}) custom-call(f32[960,128]{1,0:T(8,128)S(1)} %get-tuple-element.95.visc_in, f32[2880,128]{1,0:T(8,128)S(1)} %widen.1.vel_ref.wide_in, ...), custom_call_target="tpu_custom_call", output_to_operand_aliasing={{0}: (0, {}), {1}: (1, {})} | custom-call | tf_op jit(solution)/shard_map/sweep/pallas_call | solution.py:830
  51.0 0.0 collective-permute-done.14.x_even_ref
  51.1 2.1 %collective-permute-done.15.x_odd_ref = f32[104,128]{1,0:T(8,128)S(1)} collective-permute-done((f32[104,128]{1,0:T(8,128)S(1)}, f32[104,128]{1,0:T(8,128)S(1)}, u32[]{:S(2)}, u32[]{:S(2)}) %collective-permute-start.15) | collective-permute-done | bytes 53280 | tf_op jit(solution)/shard_map/ppermute | solution.py:668
  53.1 1.1 %finish.1 = (f32[3,16,32,128]{3,2,1,0:T(8,128)}, f32[960,128]{1,0:T(8,128)S(1)}, f32[2880,128]{1,0:T(8,128)S(1)}, f32[3584,128]{1,0:T(8,128)S(1)}, f32[1536,128]{1,0:T(8,128)S(1)}, /*index=5*/f32[2880,128]{1,0:T(8,128)S(1)}) custom-call(f32[960,128]{1,0:T(8,128)S(1)} %get-tuple-element.99.vis, ...), custom_call_target="tpu_custom_call", output_to_operand_aliasing={{1}: (0, {}), {2}: (1, {}), {3}: (2, {}), {4}: (3, {}), {5}... | custom-call | tf_op jit(solution)/shard_map/finish/pallas_call | solution.py:847
  (3 shorter events, 0.1 us)
Async XLA Ops:
  3.6 13.2 %collective-permute-start = (f32[264,128]{1,0:T(8,128)S(1)}, f32[264,128]{1,0:T(8,128)S(1)}, u32[]{:S(2)}, u32[]{:S(2)}) collective-permute-start(f32[264,128]{1,0:T(8,128)S(1)} %get-tuple-element.62), channel_id=1, source_target_pairs={{0,1},{1,0},{2,3},{3,2},{4,5},{5,4},{6,7},{7,6},{8,9},{9,8},{10,11... | collective-permute-start | bytes 405512 | tf_op jit(solution)/shard_map/ppermute | solution.py:673
  4.1 12.7 %collective-permute-start.1 = (f32[264,128]{1,0:T(8,128)S(1)}, f32[264,128]{1,0:T(8,128)S(1)}, u32[]{:S(2)}, u32[]{:S(2)}) collective-permute-start(f32[264,128]{1,0:T(8,128)S(1)} %get-tuple-element.63), channel_id=1, source_target_pairs={{0,2},{1,3},{2,0},{3,1},{4,6},{5,7},{6,4},{7,5},{8,10},{9,11},{10,... | collective-permute-start | bytes 405512 | tf_op jit(solution)/shard_map/ppermute | solution.py:673
  6.7 12.5 %collective-permute-start.2 = (f32[264,128]{1,0:T(8,128)S(1)}, f32[264,128]{1,0:T(8,128)S(1)}, u32[]{:S(2)}, u32[]{:S(2)}) collective-permute-start(f32[264,128]{1,0:T(8,128)S(1)} %get-tuple-element.64), channel_id=1, source_target_pairs={{0,3},{1,2},{2,1},{3,0},{4,7},{5,6},{6,5},{7,4},{8,11},{9,10},{10,... | collective-permute-start | bytes 405512 | tf_op jit(solution)/shard_map/ppermute | solution.py:673
  9.9 32.4 %all-to-all-start = ((f32[2048,1,128]{2,1,0:T(1,128)}), f32[2048,1,128]{2,1,0:T(1,128)S(1)}, u32[]{:S(2)}, u32[]{:S(2)}) async-start(f32[2048,1,128]{2,1,0:T(1,128)} %bitcast.15), calls=%async_computation | async-start | bytes 2097152 | tf_op jit(solution)/shard_map/all_to_all | solution.py:743
  19.2 3.5 %copy-start = (f32[3,16,32,128]{3,2,1,0:T(8,128)S(1)}, f32[3,16,32,128]{3,2,1,0:T(8,128)}, u32[]{:S(2)}) copy-start(f32[3,16,32,128]{3,2,1,0:T(8,128)} %param.13) | copy-start | bytes 2359300
  19.3 5.5 %collective-permute-start.5 = (f32[136,128]{1,0:T(8,128)S(1)}, f32[136,128]{1,0:T(8,128)S(1)}, u32[]{:S(2)}, u32[]{:S(2)}) collective-permute-start(f32[136,128]{1,0:T(8,128)S(1)} %get-tuple-element.75), channel_id=1, source_target_pairs={{0,4},{4,0},{8,12},{12,8},{16,20},{20,16},{24,28},{28,24},{1,5},{5... | collective-permute-start | bytes 208904 | tf_op jit(solution)/shard_map/ppermute | solution.py:673
  19.3 9.9 %collective-permute-start.6 = (f32[136,128]{1,0:T(8,128)S(1)}, f32[136,128]{1,0:T(8,128)S(1)}, u32[]{:S(2)}, u32[]{:S(2)}) collective-permute-start(f32[136,128]{1,0:T(8,128)S(1)} %get-tuple-element.76), channel_id=1, source_target_pairs={{0,8},{4,12},{8,0},{12,4},{16,24},{20,28},{24,16},{28,20},{1,9},{5... | collective-permute-start | bytes 208904 | tf_op jit(solution)/shard_map/ppermute | solution.py:673
  21.9 7.5 %collective-permute-start.7 = (f32[136,128]{1,0:T(8,128)S(1)}, f32[136,128]{1,0:T(8,128)S(1)}, u32[]{:S(2)}, u32[]{:S(2)}) collective-permute-start(f32[136,128]{1,0:T(8,128)S(1)} %get-tuple-element.77), channel_id=1, source_target_pairs={{0,12},{4,8},{8,4},{12,0},{16,28},{20,24},{24,20},{28,16},{1,13},{... | collective-permute-start | bytes 208904 | tf_op jit(solution)/shard_map/ppermute | solution.py:673
  21.9 9.0 %collective-permute-start.8 = (f32[136,128]{1,0:T(8,128)S(1)}, f32[136,128]{1,0:T(8,128)S(1)}, u32[]{:S(2)}, u32[]{:S(2)}) collective-permute-start(f32[136,128]{1,0:T(8,128)S(1)} %get-tuple-element.78), channel_id=1, source_target_pairs={{0,16},{4,20},{8,24},{12,28},{16,0},{20,4},{24,8},{28,12},{1,17},{... | collective-permute-start | bytes 208904 | tf_op jit(solution)/shard_map/ppermute | solution.py:673
  22.8 15.5 %collective-permute-start.3 = (f32[192,128]{1,0:T(8,128)S(1)}, f32[192,128]{1,0:T(8,128)S(1)}, u32[]{:S(2)}, u32[]{:S(2)}) collective-permute-start(f32[192,128]{1,0:T(8,128)S(1)} %bitcast.17), channel_id=1, source_target_pairs={{0,4},{4,8},{8,12},{12,16},{16,20},{20,24},{24,28},{1,5},{5,9},{9,... | collective-permute-start | bytes 294920 | tf_op jit(solution)/shard_map/ppermute | solution.py:650
  24.8 13.5 %collective-permute-start.4 = (f32[192,128]{1,0:T(8,128)S(1)}, f32[192,128]{1,0:T(8,128)S(1)}, u32[]{:S(2)}, u32[]{:S(2)}) collective-permute-start(f32[192,128]{1,0:T(8,128)S(1)} %bitcast.16), channel_id=1, source_target_pairs={{4,0},{8,4},{12,8},{16,12},{20,16},{24,20},{28,24},{5,1},{9,5},{13... | collective-permute-start | bytes 294920 | tf_op jit(solution)/shard_map/ppermute | solution.py:650
  29.3 7.5 %collective-permute-start.9 = (f32[136,128]{1,0:T(8,128)S(1)}, f32[136,128]{1,0:T(8,128)S(1)}, u32[]{:S(2)}, u32[]{:S(2)}) collective-permute-start(f32[136,128]{1,0:T(8,128)S(1)} %get-tuple-element.79), channel_id=1, source_target_pairs={{0,20},{4,16},{8,28},{12,24},{16,4},{20,0},{24,12},{28,8},{1,21},{... | collective-permute-start | bytes 208904 | tf_op jit(solution)/shard_map/ppermute | solution.py:673
  29.4 8.8 %collective-permute-start.10 = (f32[136,128]{1,0:T(8,128)S(1)}, f32[136,128]{1,0:T(8,128)S(1)}, u32[]{:S(2)}, u32[]{:S(2)}) collective-permute-start(f32[136,128]{1,0:T(8,128)S(1)} %get-tuple-element.80), channel_id=1, source_target_pairs={{0,24},{4,28},{8,16},{12,20},{16,8},{20,12},{24,0},{28,4},{1,25},{... | collective-permute-start | bytes 208904 | tf_op jit(solution)/shard_map/ppermute | solution.py:673
  30.9 7.3 %collective-permute-start.11 = (f32[136,128]{1,0:T(8,128)S(1)}, f32[136,128]{1,0:T(8,128)S(1)}, u32[]{:S(2)}, u32[]{:S(2)}) collective-permute-start(f32[136,128]{1,0:T(8,128)S(1)} %get-tuple-element.81), channel_id=1, source_target_pairs={{0,28},{4,24},{8,20},{12,16},{16,12},{20,8},{24,4},{28,0},{1,29},{... | collective-permute-start | bytes 208904 | tf_op jit(solution)/shard_map/ppermute | solution.py:673
  38.2 4.0 %copy-start.1 = (f32[16,32,128]{2,1,0:T(8,128)S(1)}, f32[16,32,128]{2,1,0:T(8,128)}, u32[]{:S(2)}) copy-start(f32[16,32,128]{2,1,0:T(8,128)} %param.12) | copy-start | bytes 786436
  42.8 4.7 %collective-permute-start.12 = (f32[144,128]{1,0:T(8,128)S(1)}, f32[144,128]{1,0:T(8,128)S(1)}, u32[]{:S(2)}, u32[]{:S(2)}) collective-permute-start(f32[144,128]{1,0:T(8,128)S(1)} %get-tuple-element.89), channel_id=1, source_target_pairs={{0,1},{4,5},{8,9},{12,13},{16,17},{20,21},{24,25},{28,29},{1,0},{5... | collective-permute-start | bytes 221192 | tf_op jit(solution)/shard_map/ppermute | solution.py:668
  42.9 5.3 %collective-permute-start.13 = (f32[144,128]{1,0:T(8,128)S(1)}, f32[144,128]{1,0:T(8,128)S(1)}, u32[]{:S(2)}, u32[]{:S(2)}) collective-permute-start(f32[144,128]{1,0:T(8,128)S(1)} %get-tuple-element.90), channel_id=1, source_target_pairs={{0,4},{4,0},{8,12},{12,8},{16,20},{20,16},{24,28},{28,24},{1,2},{5... | collective-permute-start | bytes 221192 | tf_op jit(solution)/shard_map/ppermute | solution.py:668
  48.2 2.8 %collective-permute-start.14 = (f32[104,128]{1,0:T(8,128)S(1)}, f32[104,128]{1,0:T(8,128)S(1)}, u32[]{:S(2)}, u32[]{:S(2)}) collective-permute-start(f32[104,128]{1,0:T(8,128)S(1)} %get-tuple-element.106), channel_id=1, source_target_pairs={{0,4},{1,5},{2,6},{3,7},{4,0},{5,1},{6,2},{7,3},{8,12},{9,13},{10,... | collective-permute-start | bytes 159752 | tf_op jit(solution)/shard_map/ppermute | solution.py:668
  48.3 4.8 %collective-permute-start.15 = (f32[104,128]{1,0:T(8,128)S(1)}, f32[104,128]{1,0:T(8,128)S(1)}, u32[]{:S(2)}, u32[]{:S(2)}) collective-permute-start(f32[104,128]{1,0:T(8,128)S(1)} %get-tuple-element.107), channel_id=1, source_target_pairs={{0,1},{1,0},{2,3},{3,2},{4,8},{5,9},{6,10},{7,11},{8,4},{9,5},{10,... | collective-permute-start | bytes 159752 | tf_op jit(solution)/shard_map/ppermute | solution.py:668
